TPU v7x, 128 devices: a whole 4x4x4 slice. The times are simulated.
128 devices in a mesh: ctx: 8 (over z_lo, x), head: 16 (over z_hi, y, core).
Axes of the slice: x: 4, y: 4, z: 4 (z_hi: 2, z_lo: 2; z = z_hi * 2 + z_lo), core: 2. Of those that a mesh axis runs over, the one named last changes fastest.
Arguments:
- query_rows: bfloat16 [24576, 5120], P('ctx', 'head'), may hold values from -20 to 20
- key_rows: bfloat16 [24576, 5120], P('ctx', 'head'), may hold values from -20 to 20
- value_rows: bfloat16 [24576, 5120], P('ctx', 'head'), may hold values from -6 to 6
- gate_rows: bfloat16 [24576, 5120], P('ctx', 'head'), may hold values from -6 to 6
- token_rates: float32 [16, 24576], P('head', 'ctx'), may hold values from 0.05 to 1
- step_sizes: float32 [16], P('head'), may hold values from 0.2 to 2
- fast_first: bfloat16 [16, 320, 640], P('head'), may hold values from -0.3125 to 0.3125
- fast_third: bfloat16 [16, 320, 640], P('head'), may hold values from -0.3125 to 0.3125
- fast_second: bfloat16 [16, 640, 320], P('head'), may hold values from -0.25 to 0.25
- norm_gain: float32 [5120], replicated, may hold values from 0.5 to 1.5
Outputs:
- gated_output: bfloat16 [24576, 5120], P(('ctx', 'head'))
All inputs are finite; a program needn't handle non-finite values.
Results may differ from a plain program's by a relative error of at most 0.019.
Values may be sent and summed in bfloat16 or wider, within the bound.
No kernel may reach another device: no remote copies, remote signals or barrier semaphores. Data moves between devices by JAX's collectives and lax.ppermute only.
A program may use at most 128 MiB of HBM per device.

v0:
```python
import math

import jax
import jax.numpy as jnp
from jax import lax
from jax.sharding import PartitionSpec as P

ATT_DIM = 160
WINDOW = 1024
NS_ITERS = 5


coef_first = 3.4445
coef_second = -4.775
coef_third = 2.0315
epsilon = 1e-06


def from_behind(array, axis, by):
    devices = lax.axis_size(axis)
    pairs = [(i, i + by) for i in range(devices) if 0 <= i + by < devices]
    return lax.ppermute(array, axis, pairs)


def silu_slope(pre):
    sig = jax.nn.sigmoid(pre)
    return sig * (1.0 + pre * (1.0 - sig))


def fast_apply(inputs, first, third, second):
    pre_gate = jnp.dot(inputs, first, preferred_element_type=jnp.float32)
    pre_up = jnp.dot(inputs, third, preferred_element_type=jnp.float32)
    hidden = (jax.nn.silu(pre_gate) * pre_up).astype(jnp.bfloat16)
    return jnp.dot(hidden, second, preferred_element_type=jnp.float32)


def fast_grads(key_block, scaled, first, third, second):
    pre_gate = jnp.dot(key_block, first, preferred_element_type=jnp.float32)
    pre_up = jnp.dot(key_block, third, preferred_element_type=jnp.float32)
    gated = jax.nn.silu(pre_gate)
    hidden = (gated * pre_up).astype(jnp.bfloat16)
    back = jnp.dot(scaled, second.T, preferred_element_type=jnp.float32)
    d_gate = (back * pre_up * silu_slope(pre_gate)).astype(jnp.bfloat16)
    d_up = (back * gated).astype(jnp.bfloat16)
    return (
        jnp.dot(key_block.T, d_gate, preferred_element_type=jnp.float32),
        jnp.dot(key_block.T, d_up, preferred_element_type=jnp.float32),
        jnp.dot(hidden.T, scaled, preferred_element_type=jnp.float32),
    )


def orthogonal(grad):
    high = lax.Precision.HIGHEST
    current = grad * lax.rsqrt(jnp.sum(grad * grad) + epsilon)
    for sweep in range(NS_ITERS):
        gram = jnp.dot(current, current.T, precision=high, preferred_element_type=jnp.float32)
        square = jnp.dot(gram, gram, precision=high, preferred_element_type=jnp.float32)
        mix = coef_second * gram + coef_third * square
        current = coef_first * current + jnp.dot(
            mix, current, precision=high, preferred_element_type=jnp.float32
        )
    return current


def attend(queries, keys_ext, values_ext, start):
    count = queries.shape[0]
    block = min(512, count)
    heads = queries.shape[1] // ATT_DIM
    scale = 1.0 / math.sqrt(ATT_DIM)

    def one_block(index):
        begin = index * block
        q_block = lax.dynamic_slice_in_dim(queries, begin, block, 0).reshape(block, heads, ATT_DIM)
        k_block = lax.dynamic_slice_in_dim(keys_ext, begin, block + WINDOW, 0).reshape(
            block + WINDOW, heads, ATT_DIM
        )
        v_block = lax.dynamic_slice_in_dim(values_ext, begin, block + WINDOW, 0).reshape(
            block + WINDOW, heads, ATT_DIM
        )
        scores = (
            jnp.einsum("qhd,khd->hqk", q_block, k_block, preferred_element_type=jnp.float32) * scale
        )
        q_pos = start + begin + jnp.arange(block)
        k_pos = start + begin - WINDOW + jnp.arange(block + WINDOW)
        valid = (
            (k_pos[None, :] <= q_pos[:, None])
            & (k_pos[None, :] > q_pos[:, None] - WINDOW)
            & (k_pos[None, :] >= 0)
        )
        scores = jnp.where(valid[None], scores, -jnp.inf)
        top = jnp.max(scores, -1, keepdims=True)
        expo = jnp.exp(scores - top)
        weights = (expo / jnp.sum(expo, -1, keepdims=True)).astype(jnp.bfloat16)
        result = jnp.einsum("hqk,khd->qhd", weights, v_block, preferred_element_type=jnp.float32)
        return result.reshape(block, heads * ATT_DIM)

    return lax.map(one_block, jnp.arange(count // block)).reshape(count, heads * ATT_DIM)


def shards(
    query_rows,
    key_rows,
    value_rows,
    gate_rows,
    token_rates,
    step_sizes,
    fast_first,
    fast_third,
    fast_second,
    norm_gain,
):
    count, width = query_rows.shape
    ctx_count = lax.axis_size("ctx")
    ctx_index = lax.axis_index("ctx")
    own_part = ctx_index // (ctx_count // 2)
    scaled = (token_rates[0][:, None] * value_rows).astype(jnp.bfloat16)
    step = step_sizes[0]
    weights = (fast_first[0], fast_third[0], fast_second[0])
    after = []
    for part in range(2):
        held = weights

        def compute(unused):
            return fast_grads(key_rows, scaled, *held)

        def nothing(unused):
            return tuple((jnp.zeros(matrix.shape, jnp.float32) for matrix in held))

        pieces = lax.cond(own_part == part, compute, nothing, 0)
        totals = lax.psum(pieces, "ctx")
        updates = (orthogonal(totals[0]), orthogonal(totals[1]), orthogonal(totals[2].T).T)
        weights = tuple(
            (
                (old.astype(jnp.float32) + step * upd).astype(jnp.bfloat16)
                for old, upd in zip(weights, updates)
            )
        )
        after.append(weights)
    chosen = tuple(
        (jnp.where(own_part == 0, early, late) for early, late in zip(after[0], after[1]))
    )
    fast_out = fast_apply(query_rows, *chosen)
    rim_keys, rim_values = from_behind(
        (key_rows[count - WINDOW :], value_rows[count - WINDOW :]), "ctx", 1
    )
    attn_out = attend(
        query_rows,
        jnp.concatenate([rim_keys, key_rows], 0),
        jnp.concatenate([rim_values, value_rows], 0),
        ctx_index * count,
    )
    mixed = (fast_out + attn_out).astype(jnp.bfloat16)
    mixed_tokens, gate_tokens = (
        lax.all_to_all(mixed, "head", split_axis=0, concat_axis=1, tiled=True),
        lax.all_to_all(gate_rows, "head", split_axis=0, concat_axis=1, tiled=True),
    )
    values_full = mixed_tokens.astype(jnp.float32)
    square_mean = jnp.mean(values_full * values_full, -1, keepdims=True)
    gated = (
        values_full
        * lax.rsqrt(square_mean + epsilon)
        * norm_gain
        * jax.nn.silu(gate_tokens.astype(jnp.float32))
    )
    return gated.astype(jnp.bfloat16)


def solution(mesh):
    placed = (
        P("ctx", "head"),
        P("ctx", "head"),
        P("ctx", "head"),
        P("ctx", "head"),
        P("head", "ctx"),
        P("head"),
        P("head", None, None),
        P("head", None, None),
        P("head", None, None),
        P(),
    )
    return jax.shard_map(
        shards, mesh=mesh, in_specs=placed, out_specs=P(("ctx", "head"), None), check_vma=False
    )
```

profile of v0, /device:TPU:32, one launch (start us, length us, event | category | flops | bytes accessed | tf_op | source)
XLA Modules:
  0.0 528.8 jit_solution(3988631881732399780)
XLA Ops:
  6.5 4.2 copy.28
  10.8 3.7 multiply_convert_fusion.20
  14.5 11.2 %conditional.2 = (f32[320,640]{1,0:T(8,128)S(1)}, f32[320,640]{1,0:T(8,128)}, f32[640,320]{0,1:T(8,128)}) conditional(s32[]{:T(128)} %convert_element_type.105, () %tuple.36, (bf16[3072,320]{1,0:T(8,128)(2,1)}, bf16[640,320]{0,1:T(8,128)(2,1)S(1)}, bf16[3072,320]{0,1:T(8,128)(2,1)S(1)}, bf16[320,640]{1,0:T(8,128)(2,1)S(1)}, ...), branch_computations={%region_0.1_spmd, %region_1.2_spmd} | conditional | flops 7593000960 | bytes 94126104 | solution.py:129
  26.6 2.0 slice.6
  28.7 3.4 collective-permute-start
  32.9 3.4 collective-permute-start.1
  36.3 4.1 copy.37
  40.4 7.0 %all-to-all-start.1 = ((bf16[16,192,320]{2,1,0:T(8,128)(2,1)}), bf16[16,192,320]{2,1,0:T(8,128)(2,1)}, u32[]{:S(2)}, u32[]{:S(2)}) async-start(bf16[16,192,320]{2,1,0:T(8,128)(2,1)} %bitcast.312), calls=%async_computation.1 | async-start | bytes 4718592 | tf_op jit(solution)/shard_map/all_to_all | solution.py:155
  48.2 32.9 %collective-permute-done = bf16[1024,320]{0,1:T(8,128)(2,1)S(1)} collective-permute-done((bf16[1024,320]{0,1:T(8,128)(2,1)}, bf16[1024,320]{0,1:T(8,128)(2,1)S(1)}, u32[]{:S(2)}, u32[]{:S(2)}) %collective-permute-start) | collective-permute-done | bytes 655392 | tf_op jit(solution)/shard_map/ppermute | solution.py:22
  81.1 3.4 pad_maximum_fusion
  84.4 37.2 %collective-permute-done.1 = bf16[1024,320]{0,1:T(8,128)(2,1)S(1)} collective-permute-done((bf16[1024,320]{0,1:T(8,128)(2,1)}, bf16[1024,320]{0,1:T(8,128)(2,1)S(1)}, u32[]{:S(2)}, u32[]{:S(2)}) %collective-permute-start.1) | collective-permute-done | bytes 655392 | tf_op jit(solution)/shard_map/ppermute | solution.py:22
  123.3 41.2 %all-reduce.7.cloned.1.call-done = (f32[640,320]{0,1:T(8,128)}, f32[320,640]{1,0:T(8,128)}, f32[320,640]{1,0:T(8,128)}) async-done(((f32[640,320]{0,1:T(8,128)}, f32[320,640]{1,0:T(8,128)}, f32[320,640]{1,0:T(8,128)}), (f32[640,320]{0,1:T(8,128)}, f32[320,640]{1,0:T(8,128)}, f32[320,640]{1,0:T(8,128)})) %all-reduce.7.cloned.1.call-update) | async-done | bytes 2457616 | tf_op jit(solution)/shard_map/psum | solution.py:130
  164.6 2.3 multiply_reduce_fusion.3
  167.5 3.0 fusion.110
  179.2 9.8 %fusion.87 = f32[320,320]{1,0:T(8,128)S(1)} fusion(f32[320,320]{1,0:T(8,128)S(1)} %fusion.156), kind=kOutput, calls=%fused_computation.161 | convolution fusion | flops 393523200 | bytes 819200 | tf_op jit(solution)/shard_map/dot_general | solution.py:57
  197.5 1.9 fusion.85
  202.8 1.8 convolution_add_fusion.16
  220.6 1.9 fusion.75
  231.0 1.8 multiply_add_fusion.5
  243.4 3.2 fusion.80
  248.4 2.5 fusion.56
  250.9 2.9 fusion.55
  253.8 30.3 %conditional.3 = (f32[320,640]{1,0:T(8,128)S(1)}, f32[320,640]{1,0:T(8,128)}, f32[640,320]{0,1:T(8,128)}) conditional(s32[]{:T(128)} %convert_element_type.110, () %tuple.38, (bf16[3072,320]{1,0:T(8,128)(2,1)}, bf16[640,320]{0,1:T(8,128)(2,1)}, bf16[3072,320]{0,1:T(8,128)(2,1)S(1)}, bf16[320,640]{1,0:T(8,128)(2,1)}, ...), branch_computations={%region_8.9_spmd, %region_9.10_spmd} | conditional | flops 7593000960 | bytes 94126104 | solution.py:129
  253.8 2.5 fusion.154
  256.3 5.6 %fusion.153 = f32[3072,640]{1,0:T(8,128)} fusion(bf16[3072,320]{0,1:T(8,128)(2,1)S(1)} %get-tuple-element.184, bf16[320,640]{1,0:T(8,128)(2,1)} %get-tuple-element.133), kind=kOutput, calls=%fused_computation.252 | convolution fusion | flops 1258291200 | bytes 10240000 | tf_op jit(solution)/shard_map/cond/branch_1_fun/dot_general | solution.py:39
  261.9 4.1 fusion.152
  266.0 6.8 %fusion.18 = f32[320,640]{1,0:T(8,128)S(1)} fusion(bf16[3072,320]{0,1:T(8,128)(2,1)S(1)} %get-tuple-element.184, f32[3072,640]{1,0:T(8,128)S(1)} %fusion.154, f32[3072,640]{1,0:T(8,128)S(1)} %fusion.152, f32[3072,640]{1,0:T(8,128)} %fusion.153), kind=kOutput, calls=%fused_computation.22 | convolution fusion | flops 1277952000 | bytes 26378240 | tf_op jit(solution)/shard_map/cond/branch_1_fun/dot_general | solution.py:46
  272.8 7.6 %fusion.13 = f32[640,320]{0,1:T(8,128)} fusion(bf16[3072,320]{1,0:T(8,128)(2,1)} %get-tuple-element.130, f32[3072,640]{1,0:T(8,128)} %fusion.153, f32[3072,640]{1,0:T(8,128)S(1)} %fusion.154), kind=kOutput, calls=%fused_computation.19 | convolution fusion | flops 1270087680 | bytes 18513920 | tf_op jit(solution)/shard_map/cond/branch_1_fun/dot_general | solution.py:48
  280.4 3.6 fusion.17
  285.1 72.0 %while.13 = (s32[]{:T(128)}, f32[6,512,320]{1,2,0:T(8,128)}, s32[6]{0:T(128)S(1)}, bf16[4096,320]{0,1:T(8,128)(2,1)}, s32[]{:T(128)}, /*index=5*/bf16[3072,320]{...) while((s32[]{:T(128)}, f32[6,512,320]{1,2,0:T(8,128)}, ...), condition=%wide.region_19.20_spmd, body=%wide.region_16.19_spmd.sunk | while | flops 1527260672 | bytes 13860632 | solution.py:97
  289.9 2.4 fusion.368
  292.3 3.8 fusion.369
  302.0 2.4 fusion.368
  304.4 3.8 fusion.369
  314.0 2.4 fusion.368
  316.4 3.8 fusion.369
  326.0 2.4 fusion.368
  328.4 3.8 fusion.369
  338.0 2.4 fusion.368
  340.4 3.8 fusion.369
  350.0 2.4 fusion.368
  352.4 3.8 fusion.369
  357.1 5.7 %copy.33 = f32[6,512,320]{2,1,0:T(8,128)} copy(f32[6,512,320]{1,2,0:T(8,128)} %get-tuple-element.156) | data formatting | bytes 7864320 | tf_op jit(solution)/shard_map/while | solution.py:97
  362.8 6.0 %copy.34 = f32[3072,320]{0,1:T(8,128)} copy(f32[3072,320]{1,0:T(8,128)} %bitcast.310) | data formatting | bytes 7864320 | tf_op jit(solution)/shard_map/reshape | solution.py:97
  369.9 2.0 multiply_reduce_fusion.1
  372.6 3.0 fusion.101
  376.7 3.0 convolution_add_fusion.6
  386.8 2.0 convolution_add_fusion.4
  400.1 1.8 convolution_add_fusion.11
  419.5 5.3 %fusion.170 = f32[640,3072]{1,0:T(8,128)} fusion(bf16[320,640]{1,0:T(8,128)(2,1)S(1)} %fusion.92, bf16[3072,320]{0,1:T(8,128)(2,1)S(1)} %copy-done.11), kind=kOutput, calls=%fused_computation.269 | convolution fusion | flops 1258291200 | bytes 10240000 | tf_op jit(solution)/shard_map/dot_general | solution.py:31
  429.0 2.0 bitcast_add_fusion.3
  442.5 1.8 fusion.146
  447.2 3.3 fusion.90
  450.5 2.9 fusion.91
  453.4 9.9 %fusion.41 = bf16[3072,320]{0,1:T(8,128)(2,1)S(1)} fusion(f32[3072,320]{0,1:T(8,128)} %copy.34, bf16[640,320]{0,1:T(8,128)(2,1)S(1)} %fusion.90, f32[640,3072]{1,0:T(8,128)} %fusion.170, bf16[320,640]{1,0:T(8,128)(2,1)S(1)} %fusion.91, bf16[3072,320]{0,1:T(8,128)(2,1)} %get-tuple-element.348), kind=kOutput, calls=%fused_computation.62 | convolution fusion | flops 2530344960 | bytes 16547840 | tf_op jit(solution)/shard_map/dot_general | solution.py:34
  463.3 2.5 copy.35
  465.8 6.8 %all-to-all-start = ((bf16[16,192,320]{2,1,0:T(8,128)(2,1)}), bf16[16,192,320]{2,1,0:T(8,128)(2,1)S(1)}, u32[]{:S(2)}, u32[]{:S(2)}) async-start(bf16[16,192,320]{2,1,0:T(8,128)(2,1)} %bitcast.313), calls=%async_computation | async-start | bytes 4718592 | tf_op jit(solution)/shard_map/all_to_all | solution.py:154
  472.6 2.1 convert_bitcast_fusion.1
  474.7 4.9 copy.38
  479.6 5.5 %reshape.143 = f32[192,5120]{1,0:T(8,128)} reshape(f32[192,16,320]{2,1,0:T(8,128)} %copy.38) | data formatting | bytes 7864320 | tf_op jit(solution)/shard_map/convert_element_type | solution.py:163
  485.0 19.6 %all-to-all-done = bf16[16,192,320]{2,1,0:T(8,128)(2,1)S(1)} async-done(((bf16[16,192,320]{2,1,0:T(8,128)(2,1)}), bf16[16,192,320]{2,1,0:T(8,128)(2,1)S(1)}, u32[]{:S(2)}, u32[]{:S(2)}) %all-to-all-start) | async-done | bytes 1966112 | tf_op jit(solution)/shard_map/all_to_all | solution.py:154
  505.1 4.9 copy.36
  510.0 5.4 %reshape.142 = f32[192,5120]{1,0:T(8,128)} reshape(f32[192,16,320]{2,1,0:T(8,128)} %copy.36) | data formatting | bytes 7864320 | tf_op jit(solution)/shard_map/convert_element_type | solution.py:157
  516.0 5.8 %multiply_convert_fusion.21 = bf16[192,5120]{1,0:T(8,128)(2,1)} fusion(f32[192,5120]{1,0:T(8,128)} %reshape.143, f32[192,5120]{1,0:T(8,128)} %reshape.142, f32[5120]{0:T(1024)S(1)} %copy-done.24, f32[192]{0:T(256)S(1)} %add_rsqrt_fusion), kind=kLoop, calls=%fused_computation.63 | loop fusion | flops 7864320 | bytes 9851648 | tf_op jit(solution)/shard_map/convert_element_type | solution.py:165
  (200 shorter events, 148.2 us)
Async XLA Ops:
  6.5 7.9 %copy-start.18 = (bf16[1,640,320]{1,2,0:T(8,128)(2,1)S(1)}, bf16[1,640,320]{1,2,0:T(8,128)(2,1)}, u32[]{:S(2)}) copy-start(bf16[1,640,320]{1,2,0:T(8,128)(2,1)} %param.24) | copy-start | bytes 1228804
  6.5 7.9 %copy-start = (bf16[3072,320]{0,1:T(8,128)(2,1)S(1)}, bf16[3072,320]{0,1:T(8,128)(2,1)}, u32[]{:S(2)}) copy-start(bf16[3072,320]{0,1:T(8,128)(2,1)} %param.17) | copy-start | bytes 5898244
  6.5 158.0 %all-reduce.7.cloned.1.call-start = ((), (), s32[]{:S(2)}) async-start(), calls=%async_computation.3 | async-start | bytes 4915200 | tf_op jit(solution)/shard_map/psum | solution.py:130
  10.8 3.7 copy-start.20
  10.8 3.7 copy-start.22
  25.7 0.9 copy-start.14
  28.7 52.4 %collective-permute-start = (bf16[1024,320]{0,1:T(8,128)(2,1)}, bf16[1024,320]{0,1:T(8,128)(2,1)S(1)}, u32[]{:S(2)}, u32[]{:S(2)}) collective-permute-start(bf16[1024,320]{0,1:T(8,128)(2,1)} %slice.6), channel_id=1, source_target_pairs={{0,16},{16,32},{32,48},{48,64},{64,80},{80,96},{96,112},{1,17},{17... | collective-permute-start | bytes 1966088 | tf_op jit(solution)/shard_map/ppermute | solution.py:22
  32.9 88.7 %collective-permute-start.1 = (bf16[1024,320]{0,1:T(8,128)(2,1)}, bf16[1024,320]{0,1:T(8,128)(2,1)S(1)}, u32[]{:S(2)}, u32[]{:S(2)}) collective-permute-start(bf16[1024,320]{0,1:T(8,128)(2,1)} %slice.7), channel_id=1, source_target_pairs={{0,16},{16,32},{32,48},{48,64},{64,80},{80,96},{96,112},{1,17},{17... | collective-permute-start | bytes 1966088 | tf_op jit(solution)/shard_map/ppermute | solution.py:22
  40.4 425.3 %all-to-all-start.1 = ((bf16[16,192,320]{2,1,0:T(8,128)(2,1)}), bf16[16,192,320]{2,1,0:T(8,128)(2,1)}, u32[]{:S(2)}, u32[]{:S(2)}) async-start(bf16[16,192,320]{2,1,0:T(8,128)(2,1)} %bitcast.312), calls=%async_computation.1 | async-start | bytes 4718592 | tf_op jit(solution)/shard_map/all_to_all | solution.py:155
  47.5 322.5 %all-reduce.5.cloned.1.call-start = ((), (), s32[]{:S(2)}) async-start(), calls=%async_computation.2 | async-start | bytes 4915200 | tf_op jit(solution)/shard_map/psum | solution.py:130
  164.6 7.1 %copy-start.10 = (f32[320,640]{1,0:T(8,128)S(1)}, f32[320,640]{1,0:T(8,128)}, u32[]{:S(2)}) copy-start(f32[320,640]{1,0:T(8,128)} %get-tuple-element.206) | copy-start | bytes 2457604
  190.7 9.4 %copy-start.9 = (f32[320,640]{1,0:T(8,128)S(1)}, f32[320,640]{1,0:T(8,128)}, u32[]{:S(2)}) copy-start(f32[320,640]{1,0:T(8,128)} %get-tuple-element.205) | copy-start | bytes 2457604
  195.0 0.9 copy-start.3
  213.3 9.2 %copy-start.1 = (f32[640,320]{0,1:T(8,128)S(1)}, f32[640,320]{0,1:T(8,128)}, u32[]{:S(2)}) copy-start(f32[640,320]{0,1:T(8,128)} %get-tuple-element.204) | copy-start | bytes 2457604
  218.1 0.9 copy-start.5
  238.8 7.8 %copy-start.4 = (f32[320,640]{1,0:T(8,128)S(1)}, f32[320,640]{1,0:T(8,128)}, u32[]{:S(2)}) copy-start(f32[320,640]{1,0:T(8,128)} %copy-done.3) | copy-start | bytes 2457604
  238.8 7.8 %copy-start.16 = (f32[320,320]{1,0:T(8,128)S(1)}, f32[320,320]{1,0:T(8,128)}, u32[]{:S(2)}) copy-start(f32[320,320]{1,0:T(8,128)} %fusion.85) | copy-start | bytes 1228804
  238.8 7.8 %copy-start.21 = (bf16[1,320,640]{2,1,0:T(8,128)(2,1)S(1)}, bf16[1,320,640]{2,1,0:T(8,128)(2,1)}, u32[]{:S(2)}) copy-start(bf16[1,320,640]{2,1,0:T(8,128)(2,1)} %param.22) | copy-start | bytes 1228804
  239.9 8.4 %copy-start.6 = (f32[320,640]{1,0:T(8,128)S(1)}, f32[320,640]{1,0:T(8,128)}, u32[]{:S(2)}) copy-start(f32[320,640]{1,0:T(8,128)} %copy-done.5) | copy-start | bytes 2457604
  239.9 8.4 %copy-start.17 = (f32[320,320]{1,0:T(8,128)S(1)}, f32[320,320]{1,0:T(8,128)}, u32[]{:S(2)}) copy-start(f32[320,320]{1,0:T(8,128)} %fusion.75) | copy-start | bytes 1228804
  240.0 8.4 %copy-start.23 = (bf16[1,320,640]{2,1,0:T(8,128)(2,1)S(1)}, bf16[1,320,640]{2,1,0:T(8,128)(2,1)}, u32[]{:S(2)}) copy-start(bf16[1,320,640]{2,1,0:T(8,128)(2,1)} %param.23) | copy-start | bytes 1228804
  241.6 9.3 %copy-start.19 = (bf16[1,640,320]{1,2,0:T(8,128)(2,1)S(1)}, bf16[1,640,320]{1,2,0:T(8,128)(2,1)}, u32[]{:S(2)}) copy-start(bf16[1,640,320]{1,2,0:T(8,128)(2,1)} %param.24) | copy-start | bytes 1228804
  248.4 5.4 %copy-start.12 = (bf16[320,640]{1,0:T(8,128)(2,1)}, bf16[320,640]{1,0:T(8,128)(2,1)S(1)}, u32[]{:S(2)}) copy-start(bf16[320,640]{1,0:T(8,128)(2,1)S(1)} %fusion.54) | copy-start | bytes 1228804
  284.1 0.9 copy-start.15
  289.9 2.4 copy-start.7
  302.0 2.4 copy-start.7
  314.0 2.4 copy-start.7
  326.0 2.4 copy-start.7
  338.0 2.4 copy-start.7
  350.0 2.4 copy-start.7
  388.8 7.0 %copy-start.8 = (f32[320,640]{1,0:T(8,128)S(1)}, f32[320,640]{1,0:T(8,128)}, u32[]{:S(2)}) copy-start(f32[320,640]{1,0:T(8,128)} %get-tuple-element.202) | copy-start | bytes 2457604
  410.5 7.3 %copy-start.13 = (bf16[320,640]{1,0:T(8,128)(2,1)S(1)}, bf16[320,640]{1,0:T(8,128)(2,1)}, u32[]{:S(2)}) copy-start(bf16[320,640]{1,0:T(8,128)(2,1)} %copy-done.12) | copy-start | bytes 1228804
  412.1 7.4 %copy-start.11 = (bf16[3072,320]{0,1:T(8,128)(2,1)S(1)}, bf16[3072,320]{0,1:T(8,128)(2,1)}, u32[]{:S(2)}) copy-start(bf16[3072,320]{0,1:T(8,128)(2,1)} %get-tuple-element.348) | copy-start | bytes 5898244
  419.5 5.3 %copy-start.2 = (f32[640,320]{0,1:T(8,128)S(1)}, f32[640,320]{0,1:T(8,128)}, u32[]{:S(2)}) copy-start(f32[640,320]{0,1:T(8,128)} %get-tuple-element.201) | copy-start | bytes 2457604
  465.8 38.8 %all-to-all-start = ((bf16[16,192,320]{2,1,0:T(8,128)(2,1)}), bf16[16,192,320]{2,1,0:T(8,128)(2,1)S(1)}, u32[]{:S(2)}, u32[]{:S(2)}) async-start(bf16[16,192,320]{2,1,0:T(8,128)(2,1)} %bitcast.313), calls=%async_computation | async-start | bytes 4718592 | tf_op jit(solution)/shard_map/all_to_all | solution.py:154
  510.0 6.0 %copy-start.24 = (f32[5120]{0:T(1024)S(1)}, f32[5120]{0:T(1024)}, u32[]{:S(2)}) copy-start(f32[5120]{0:T(1024)} %param.25) | copy-start | bytes 61444
Sparse Core Ops, SparseCore 0:
  26.8 137.7 all-reduce.6
  285.2 84.7 all-reduce.4
where the time goes:
time: 536 us; the launch traced here: 529 us
  matrix products  237 us (44%)
  waiting for transfers between devices  132 us (25%)
  local copies, waits for them, and re-layouts  76.9 us (14%)
  other arithmetic  29.2 us (5%)
  starting transfers between devices  20.6 us (4%)
  between operations  19.4 us (4%)
  loops' own time  14 us (3%)
    ppermute x2, waiting for transfers between devices, from_behind(): return lax.ppermute(array, axis, pairs)  70.1 us
    dot_general x30, matrix products, orthogonal(): jnp.dot(mix, current, precision=high, preferred_element_type=jnp.float32)  56.6 us
    dot_general x30, matrix products, orthogonal(): jnp.dot(current, current.T, precision=high, preferred_element_type=jnp.fl...  51.3 us
    dot_general x30, matrix products, orthogonal(): jnp.dot(gram, gram, precision=high, preferred_element_type=jnp.float32)  46 us
    psum x2, waiting for transfers between devices, shards(): totals = lax.psum(pieces, 'ctx')  42.4 us
    dot_general x6, matrix products, one_block(): jnp.einsum('hqk,khd->qhd', weights, v_block, preferred_element_type=jnp.f...  22.9 us
    all_to_all x1, waiting for transfers between devices, shards(): lax.all_to_all(mixed, 'head', split_axis=0, concat_axis=1, tiled=True)  19.6 us
    sub x6, matrix products, one_block(): expo = jnp.exp(scores - top)  14.4 us
  transfers between devices with their start and end apart: 6, of which 5 were waited for; matrix products, arithmetic and copies ran while one was open for 59% of the time, Pallas kernels for 0%

commit v1 on v0

v1 whole, which is shorter than its diff:
```python
import functools
import math

import jax
import jax.numpy as jnp
from jax import lax
from jax.experimental import pallas as pl
from jax.experimental.pallas import tpu as pltpu
from jax.sharding import PartitionSpec as P

ATT_DIM = 160
WINDOW = 1024
RING = 4
QB = 256
TB = 512

coef_first = 3.4445
coef_second = -4.775
coef_third = 2.0315
epsilon = 1e-06
LOG2E = 1.4426950408889634
CENTRES = (0.0, 0.0, 0.5, 0.8, 0.8)
F32 = jnp.float32
BF16 = jnp.bfloat16
VMEM_LIMIT = 56 * 1024 * 1024


def params():
    return pltpu.CompilerParams(vmem_limit_bytes=VMEM_LIMIT)


def dot(a, b, dims=((1,), (0,))):
    return lax.dot_general(a, b, (dims, ((), ())), preferred_element_type=F32)


def sigmoid(x):
    return 0.5 * jnp.tanh(0.5 * x) + 0.5


def pick_weights(place, sources, put):
    for j in range(3):
        for s in range(RING):

            @pl.when(lax.rem(place + RING - j, RING) == s)
            def _(j=j, s=s):
                put(j, sources[s][...])


def grads_kernel(static, place_ref, x_ref, v_ref, r_ref, *rest):
    n_src = 3 if static else RING
    sources, (own, s1, s2, s3), (acc, wt) = rest[:n_src], rest[n_src : n_src + 4], rest[n_src + 4 :]
    step = pl.program_id(0)
    place = place_ref[0]

    @pl.when(step == 0)
    def _():
        def put(j, w):
            wt[j] = w.T

        if static:
            for j in range(3):
                put(j, sources[j][...])
        else:
            pick_weights(place, sources, put)
        acc[...] = jnp.zeros_like(acc)

    x = x_ref[...]
    e = (r_ref[...] * v_ref[...].astype(F32)).astype(BF16)
    gate = dot(wt[0], x)
    up = dot(wt[1], x)
    back = dot(wt[2], e)
    sig = sigmoid(gate)
    gated = gate * sig
    hidden = (gated * up).astype(BF16)
    d_gate = (back * up * (sig + gated * (1.0 - sig))).astype(BF16)
    d_up = (back * gated).astype(BF16)
    nt = ((1,), (1,))
    acc[0] += dot(x, d_gate, nt)
    acc[1] += dot(x, d_up, nt)
    acc[2] += dot(e, hidden, nt)

    @pl.when(step == pl.num_programs(0) - 1)
    def _():
        for shift, out in enumerate((own, s1, s2, s3)):
            out[...] = acc[jnp.minimum(lax.rem(place + shift, RING), 2)].astype(BF16)


def grads(place, xt, vt, rates, sources, static):
    width, count = xt.shape
    matrix = sources[0].shape
    whole = pl.BlockSpec(matrix, lambda i, p: (0, 0))
    tokens = pl.BlockSpec((width, TB), lambda i, p: (0, i))
    hidden = matrix[1]
    return pl.pallas_call(
        functools.partial(grads_kernel, static),
        grid_spec=pltpu.PrefetchScalarGridSpec(
            num_scalar_prefetch=1,
            grid=(count // TB,),
            in_specs=[tokens, tokens, pl.BlockSpec((1, TB), lambda i, p: (0, i))]
            + [whole] * len(sources),
            out_specs=[whole] * 4,
            scratch_shapes=[
                pltpu.VMEM((3,) + matrix, F32),
                pltpu.VMEM((3, hidden, width), BF16),
            ],
        ),
        out_shape=[jax.ShapeDtypeStruct(matrix, BF16)] * 4,
        compiler_params=params(),
        cost_estimate=pl.CostEstimate(
            flops=12 * width * hidden * count,
            bytes_accessed=4 * width * count,
            transcendentals=hidden * count,
        ),
    )(place, xt, vt, rates, *sources)


def update_kernel(place_ref, step_ref, own, r1, r2, r3, *rest):
    olds, out = rest[:-1], rest[-1]
    place = place_ref[0]
    if len(olds) == 3:
        old = jnp.where(
            place == 0, olds[0][...], jnp.where(place == 1, olds[1][...], olds[2][...])
        )
    else:
        old = olds[0][...]
    g = own[...].astype(F32) + r1[...].astype(F32) + r2[...].astype(F32) + r3[...].astype(F32)
    x = g * lax.rsqrt(jnp.sum(g * g) + epsilon)
    rows = g.shape[0]
    diagonal = lax.broadcasted_iota(jnp.int32, (rows, rows), 0) == lax.broadcasted_iota(
        jnp.int32, (rows, rows), 1
    )
    for c in CENTRES:
        xb = x.astype(BF16)
        e = dot(xb, xb, ((1,), (1,)))
        if c:
            e = e - jnp.where(diagonal, c, 0.0)
        eb = e.astype(BF16)
        mix = (coef_second + 2.0 * c * coef_third) * e + coef_third * dot(eb, eb)
        k = coef_first + coef_second * c + coef_third * c * c
        x = k * x + dot(mix.astype(BF16), xb)
    out[...] = (old.astype(F32) + step_ref[0] * x).astype(BF16)


def update(place, step, pieces, olds):
    matrix = pieces[0].shape
    smem = pl.BlockSpec(memory_space=pltpu.SMEM)
    vmem = pl.BlockSpec(memory_space=pltpu.VMEM)
    return pl.pallas_call(
        update_kernel,
        in_specs=[smem, smem] + [vmem] * (4 + len(olds)),
        out_specs=vmem,
        out_shape=jax.ShapeDtypeStruct(matrix, BF16),
        compiler_params=params(),
        cost_estimate=pl.CostEstimate(
            flops=5 * 2 * 5 * matrix[0] * matrix[0] * matrix[0],
            bytes_accessed=16 * matrix[0] * matrix[1],
            transcendentals=0,
        ),
    )(place, step, *pieces, *olds)


def attend_kernel(blocks, kb_first, first_ref, q_ref, k_ref, v_ref, *rest):
    if kb_first is None:
        (out, k_nat) = rest
        rims = ()
    else:
        (rim_k, rim_v, _, out, k_nat) = rest
        rims = (rim_k, rim_v)
    step = pl.program_id(0)
    heads = q_ref.shape[0] // ATT_DIM
    chunks = WINDOW // QB + 1
    rim_blocks = WINDOW // QB if rims else 0

    @pl.when(step == 0)
    def _():
        if rims:
            for h in range(heads):
                k_nat[h, :WINDOW, :] = rims[0][pl.ds(h * ATT_DIM, ATT_DIM), :].T
        for h in range(heads):
            k_nat[h, rim_blocks * QB :, :] = k_ref[pl.ds(h * ATT_DIM, ATT_DIM), :].T

    later = lax.broadcasted_iota(jnp.int32, (QB, QB), 0) > lax.broadcasted_iota(
        jnp.int32, (QB, QB), 1
    )
    scale = LOG2E / math.sqrt(ATT_DIM)
    low = -1e30

    def values(h, block):
        return v_ref[pl.ds(h * ATT_DIM, ATT_DIM), pl.ds(pl.multiple_of(block * QB, QB), QB)]

    def body(i, fresh):
        for h in range(heads):
            q = q_ref[pl.ds(h * ATT_DIM, ATT_DIM), :]
            s = []
            for c in range(chunks):
                k = k_nat[h, pl.ds(pl.multiple_of((i + c) * QB, QB), QB), :]
                part = dot(k, q)
                if c == 0:
                    part = jnp.where(later, part, low)
                elif c == chunks - 1:
                    part = jnp.where(later, low, part)
                if c < fresh:
                    part = jnp.where(first_ref[0] == 1, low, part)
                s.append(part)
            top = functools.reduce(
                jnp.maximum, [jnp.max(part, axis=0, keepdims=True) for part in s]
            )
            total = jnp.zeros((1, QB), F32)
            result = jnp.zeros((ATT_DIM, QB), F32)
            for c in range(chunks):
                expo = jnp.exp2((s[c] - top) * scale)
                total += jnp.sum(expo, axis=0, keepdims=True)
                if c < fresh:
                    v = rims[1][pl.ds(h * ATT_DIM, ATT_DIM), pl.ds((i + c) * QB, QB)]
                else:
                    v = values(h, i + c - rim_blocks)
                result += dot(v, expo.astype(BF16))
            out[pl.ds(h * ATT_DIM, ATT_DIM), :] = result / total

    if rims:
        for i in range(blocks):

            @pl.when(step == i)
            def _(i=i):
                body(i, rim_blocks - i)
    else:
        body(step, 0)


def attend_main(qt, kt, vt, first):
    width, count = qt.shape
    skip = WINDOW // QB
    blocks = count // QB - skip
    heads = width // ATT_DIM
    whole = pl.BlockSpec((width, count), lambda i, f: (0, 0))
    return pl.pallas_call(
        functools.partial(attend_kernel, blocks, None),
        grid_spec=pltpu.PrefetchScalarGridSpec(
            num_scalar_prefetch=1,
            grid=(blocks,),
            in_specs=[pl.BlockSpec((width, QB), lambda i, f: (0, i + skip)), whole, whole],
            out_specs=pl.BlockSpec((width, QB), lambda i, f: (0, i + skip)),
            scratch_shapes=[pltpu.VMEM((heads, count, ATT_DIM), BF16)],
        ),
        out_shape=jax.ShapeDtypeStruct((width, count), F32),
        compiler_params=params(),
        cost_estimate=pl.CostEstimate(
            flops=4 * blocks * QB * (WINDOW + QB) * width,
            bytes_accessed=10 * width * count,
            transcendentals=blocks * QB * (WINDOW + QB) * heads,
        ),
    )(first, qt, kt, vt)


def attend_rim(qt, kt, vt, rim_k, rim_v, main, first):
    width = qt.shape[0]
    blocks = WINDOW // QB
    heads = width // ATT_DIM
    whole = pl.BlockSpec((width, WINDOW), lambda i, f: (0, 0))
    return pl.pallas_call(
        functools.partial(attend_kernel, blocks, 0),
        grid_spec=pltpu.PrefetchScalarGridSpec(
            num_scalar_prefetch=1,
            grid=(blocks,),
            in_specs=[pl.BlockSpec((width, QB), lambda i, f: (0, i))] + [whole] * 4
            + [pl.BlockSpec(memory_space=pl.ANY)],
            out_specs=pl.BlockSpec((width, QB), lambda i, f: (0, i)),
            scratch_shapes=[pltpu.VMEM((heads, 2 * WINDOW, ATT_DIM), BF16)],
        ),
        out_shape=jax.ShapeDtypeStruct(main.shape, F32),
        input_output_aliases={6: 0},
        compiler_params=params(),
        cost_estimate=pl.CostEstimate(
            flops=4 * blocks * QB * (WINDOW + QB) * width,
            bytes_accessed=16 * width * WINDOW,
            transcendentals=blocks * QB * (WINDOW + QB) * heads,
        ),
    )(first, qt, kt, vt, rim_k, rim_v, main)


def pack(rows, out, dests):
    n = rows.shape[0] // (2 * dests)
    width = rows.shape[1]
    for d in range(dests):
        begin = 2 * n * d
        out[d] = jnp.concatenate([rows[begin : begin + n], rows[begin + n : begin + 2 * n]], 1)


def apply_kernel(dests, place_ref, part_ref, q_ref, att_ref, *rest):
    sources, out, (wt, w2) = rest[: 2 * RING], rest[2 * RING], rest[2 * RING + 1 :]

    @pl.when(pl.program_id(0) == 0)
    def _():
        def put(j, w):
            if j < 2:
                wt[j] = w.T
            else:
                w2[...] = w

        for part in range(2):

            @pl.when(part_ref[0] == part)
            def _(part=part):
                pick_weights(place_ref[0], sources[part * RING : (part + 1) * RING], put)

    q = q_ref[...]
    gate = dot(wt[0], q)
    up = dot(wt[1], q)
    hidden = (gate * sigmoid(gate) * up).astype(BF16)
    fast = dot(w2[...], hidden)
    pack((fast + att_ref[...]).astype(BF16).T, out, dests)


def apply_mix(place, part, qt, att, early, late, parts_out):
    width, count = qt.shape
    matrix = early[0].shape
    rows = count // parts_out
    dests = 4
    tokens = pl.BlockSpec((width, dests * rows), lambda i, p, g: (0, i))
    return pl.pallas_call(
        functools.partial(apply_kernel, dests),
        grid_spec=pltpu.PrefetchScalarGridSpec(
            num_scalar_prefetch=2,
            grid=(parts_out // dests,),
            in_specs=[tokens, tokens] + [pl.BlockSpec(matrix, lambda i, p, g: (0, 0))] * 8,
            out_specs=pl.BlockSpec((dests, rows // 2, 2 * width), lambda i, p, g: (i, 0, 0)),
            scratch_shapes=[
                pltpu.VMEM((2, matrix[1], width), BF16),
                pltpu.VMEM(matrix, BF16),
            ],
        ),
        out_shape=jax.ShapeDtypeStruct((parts_out, rows // 2, 2 * width), BF16),
        compiler_params=params(),
        cost_estimate=pl.CostEstimate(
            flops=6 * width * matrix[1] * count,
            bytes_accessed=8 * width * count,
            transcendentals=matrix[1] * count,
        ),
    )(place, part, qt, att, *early, *late)


def gate_kernel(dests, g_ref, out):
    pack(g_ref[...].T, out, dests)


def pack_gate(gt, parts_out):
    width, count = gt.shape
    rows = count // parts_out
    dests = 4
    return pl.pallas_call(
        functools.partial(gate_kernel, dests),
        grid=(parts_out // dests,),
        in_specs=[pl.BlockSpec((width, dests * rows), lambda i: (0, i))],
        out_specs=pl.BlockSpec((dests, rows // 2, 2 * width), lambda i: (i, 0, 0)),
        out_shape=jax.ShapeDtypeStruct((parts_out, rows // 2, 2 * width), BF16),
        compiler_params=params(),
        cost_estimate=pl.CostEstimate(
            flops=0, bytes_accessed=8 * width * count, transcendentals=0
        ),
    )(gt)


def final_kernel(m_ref, g_ref, gain_ref, out):
    heads, _, double = m_ref.shape
    width = double // 2
    for half in range(2):
        lanes = slice(half * width, (half + 1) * width)
        total = 0.0
        for h in range(heads):
            m = m_ref[h, :, lanes].astype(F32)
            total += jnp.sum(m * m, axis=1, keepdims=True)
        factor = lax.rsqrt(total / (heads * width) + epsilon)
        for h in range(0, heads, 2):
            cols = slice(h * width, (h + 2) * width)
            m = jnp.concatenate([m_ref[h, :, lanes], m_ref[h + 1, :, lanes]], 1).astype(F32)
            g = jnp.concatenate([g_ref[h, :, lanes], g_ref[h + 1, :, lanes]], 1).astype(F32)
            out[half, :, cols] = (m * factor * gain_ref[:, cols] * (g * sigmoid(g))).astype(BF16)


def final(mixed, gates, gain):
    heads, rows, double = mixed.shape
    block = 32
    wide = heads * double // 2
    tokens = pl.BlockSpec((heads, block, double), lambda i: (0, i, 0))
    result = pl.pallas_call(
        final_kernel,
        grid=(rows // block,),
        in_specs=[tokens, tokens, pl.BlockSpec((1, wide), lambda i: (0, 0))],
        out_specs=pl.BlockSpec((2, block, wide), lambda i: (0, i, 0)),
        out_shape=jax.ShapeDtypeStruct((2, rows, wide), BF16),
        compiler_params=params(),
        cost_estimate=pl.CostEstimate(
            flops=20 * rows * wide, bytes_accessed=12 * rows * wide, transcendentals=2 * rows * wide
        ),
    )(mixed, gates, gain.reshape(1, wide))
    return result.reshape(2 * rows, wide)


def reduce_moves(part):
    base = part * RING
    return [
        [(base + (m - s) % RING, base + m) for m in range(3)] for s in range(1, RING)
    ]


def spread_moves(parts):
    return [
        [(p * RING + m, p * RING + (m + s) % RING) for p in parts for m in range(3)]
        for s in range(1, RING)
    ]


def send(array, pairs):
    return lax.ppermute(array, "ctx", pairs)


def shards(
    query_rows,
    key_rows,
    value_rows,
    gate_rows,
    token_rates,
    step_sizes,
    fast_first,
    fast_third,
    fast_second,
    norm_gain,
):
    ctx = lax.axis_index("ctx")
    heads = lax.axis_size("head")
    place = (ctx % RING).reshape(1).astype(jnp.int32)
    part = (ctx // RING).reshape(1).astype(jnp.int32)
    first = (ctx == 0).reshape(1).astype(jnp.int32)
    qt, kt, vt, gt = query_rows.T, key_rows.T, value_rows.T, gate_rows.T
    count = qt.shape[1]
    start = [fast_first[0], fast_third[0], fast_second[0].T]

    tail_k, tail_v = kt[:, count - WINDOW :], vt[:, count - WINDOW :]
    late_pairs = [(i, i + 1) for i in range(3, 7)]
    early_pairs = [(i, i + 1) for i in range(3)]
    rim_late = (send(tail_k, late_pairs), send(tail_v, late_pairs))

    own, *out = grads(place, kt, vt, token_rates, start, True)
    pieces = [own] + [send(o, p) for o, p in zip(out, reduce_moves(0))]
    att_main = attend_main(qt, kt, vt, first)
    gates = pack_gate(gt, heads)
    pieces, att_main, gates, tails = lax.optimization_barrier(
        (pieces, att_main, gates, (tail_k, tail_v))
    )
    rim_early = (send(tails[0], early_pairs), send(tails[1], early_pairs))
    fresh = update(place, step_sizes, pieces, start)
    crossed = send(fresh, [(m, RING + m) for m in range(3)])
    held = jnp.where(part[0] == 0, fresh, crossed)
    early = [held] + [send(held, p) for p in spread_moves((0, 1))]
    rims = [jnp.where(part[0] == 0, a, b) for a, b in zip(rim_early, rim_late)]
    att = attend_rim(qt, kt, vt, rims[0], rims[1], att_main, first)
    early, att = lax.optimization_barrier((early, att))

    own, *out = grads(place, kt, vt, token_rates, early, False)
    pieces = [own] + [send(o, p) for o, p in zip(out, reduce_moves(1))]
    gate_tokens = lax.all_to_all(gates, "head", split_axis=0, concat_axis=0)
    fresh = update(place, step_sizes, pieces, [early[0]])
    late = [fresh] + [send(fresh, p) for p in spread_moves((1,))]
    mixed = apply_mix(place, part, qt, att, early, late, heads)
    mixed_tokens = lax.all_to_all(mixed, "head", split_axis=0, concat_axis=0)
    return final(mixed_tokens, gate_tokens, norm_gain)


def solution(mesh):
    placed = (
        P("ctx", "head"),
        P("ctx", "head"),
        P("ctx", "head"),
        P("ctx", "head"),
        P("head", "ctx"),
        P("head"),
        P("head", None, None),
        P("head", None, None),
        P("head", None, None),
        P(),
    )
    return jax.shard_map(
        shards, mesh=mesh, in_specs=placed, out_specs=P(("ctx", "head"), None), check_vma=False
    )
```

time: 536 us -> 268 us (0.50)
  matrix products: 237 us -> 0 us
  Pallas kernels: 0 us -> 97.4 us
  local copies, waits for them, and re-layouts: 76.9 us -> 6.85 us
  waiting for transfers between devices: 132 us -> 72.8 us
  blocking collectives: 0 us -> 35 us
  starting transfers between devices: 20.6 us -> 47.8 us
  other arithmetic: 29.2 us -> 5.09 us
  between operations: 19.4 us -> 0.91 us
  loops' own time: 14 us -> 0 us
    dot_general x104 -> x0, matrix products: 222 us -> none  [the longest x30 56.6 us: orthogonal(): jnp.dot(mix, current, precision=high, preferred_element_type=jnp.float32)]
    pallas_call x0 -> x9, Pallas kernels: none -> 97.4 us  [the longest x2 34.7 us: grads(): pl.pallas_call(functools.partial(grads_kernel, static), grid_spec=pltpu.P...]
    psum x2 -> x0, waiting for transfers between devices: 42.4 us -> none  [shards(): totals = lax.psum(pieces, 'ctx')]
    all_to_all x0 -> x1, blocking collectives: none -> 35 us  [shards(): mixed_tokens = lax.all_to_all(mixed, 'head', split_axis=0, concat_axis=0)]
    ppermute x2 -> x17, starting transfers between devices: 6.77 us -> 40.8 us  [send(): return lax.ppermute(array, 'ctx', pairs)]
    convert_element_type x5 -> x0, local copies, waits for them, and re-layouts: 23 us -> none  [the longest x2 10.3 us: shards(): gate_tokens.astype(jnp.float32)]
    dynamic_slice x18 -> x0, local copies, waits for them, and re-layouts: 19.8 us -> none  [the longest x6 9.88 us: one_block(): lax.dynamic_slice_in_dim(keys_ext, begin, block + WINDOW, 0)]
    all_to_all x2 -> x1, waiting for transfers between devices: 19.6 us -> 0.01 us  [shards(): gate_tokens = lax.all_to_all(gates, 'head', split_axis=0, concat_axis=0)]
  transfers between devices with their start and end apart: 6 -> 18, of which waited for: 5 -> 5; matrix products, arithmetic and copies ran while one was open for 59% -> 3% of each run, Pallas kernels for 0% -> 24%
where the time goes in v1:
time: 268 us; the launch traced here: 266 us
  Pallas kernels  97.4 us (36%)
  waiting for transfers between devices  72.8 us (27%)
  starting transfers between devices  47.8 us (18%)
  blocking collectives  35 us (13%)
  local copies, waits for them, and re-layouts  6.85 us (3%)
  other arithmetic  5.09 us (2%)
    ppermute x17, waiting for transfers between devices, send(): return lax.ppermute(array, 'ctx', pairs)  72.8 us
    ppermute x17, starting transfers between devices, send(): return lax.ppermute(array, 'ctx', pairs)  40.8 us
    all_to_all x1, blocking collectives, shards(): mixed_tokens = lax.all_to_all(mixed, 'head', split_axis=0, concat_axis=0)  35 us
    pallas_call x2, Pallas kernels, grads(): pl.pallas_call(functools.partial(grads_kernel, static), grid_spec=pltpu.P...  34.7 us
    pallas_call x1, Pallas kernels, attend_main(): pl.pallas_call(functools.partial(attend_kernel, blocks, None), grid_spec=...  15.3 us
    pallas_call x2, Pallas kernels, update(): pl.pallas_call(update_kernel, in_specs=[smem, smem] + [vmem] * (4 + len(o...  14.8 us
    pallas_call x1, Pallas kernels, apply_mix(): pl.pallas_call(functools.partial(apply_kernel, dests), grid_spec=pltpu.Pr...  10.7 us
    pallas_call x1, Pallas kernels, attend_rim(): pl.pallas_call(functools.partial(attend_kernel, blocks, 0), grid_spec=plt...  9.18 us
  transfers between devices with their start and end apart: 18, of which 5 were waited for; matrix products, arithmetic and copies ran while one was open for 3% of the time, Pallas kernels for 24%

profile of v1, /device:TPU:32, one launch (start us, length us, event | category | flops | bytes accessed | tf_op | source)
XLA Modules:
  0.0 265.7 jit_solution(13677529277066751311)
XLA Ops:
  0.0 17.2 %shard_map.100 = (bf16[320,640]{1,0:T(8,128)(2,1)}, bf16[320,640]{1,0:T(8,128)(2,1)}, bf16[320,640]{1,0:T(8,128)(2,1)}, bf16[320,640]{1,0:T(8,128)(2,1)}) custom-call(s32[1]{0:T(128)} %bitcast.place_ref, bf16[320,3072]{1,0:T(8,128)(2,1)} %bitcast.14, bf16[320,3072]{1,0:T(8,128)(2,1)} %bitcast.19, f32[1,3072]{1,0:T(1,128)} %r_ref.3, ...), custom_call_target="tpu_custom_call" | custom-call | flops 7549747200 | bytes 3932160 | tf_op jit(solution)/shard_map/pallas_call | solution.py:94
  17.2 0.7 collective-permute-start
  17.9 0.7 collective-permute-start.1
  18.6 0.7 collective-permute-start.2
  19.3 1.1 slice.8
  20.4 1.1 slice.9
  22.2 4.3 %shard_map.102 = bf16[16,96,640]{2,1,0:T(8,128)(2,1)} custom-call(bf16[320,3072]{1,0:T(8,128)(2,1)} %bitcast.24), custom_call_target="tpu_custom_call" | custom-call | bytes 7864320 | tf_op jit(solution)/shard_map/pallas_call | solution.py:350
  26.5 15.3 %shard_map.101.rest_2_ = f32[320,3072]{1,0:T(8,128)} custom-call(s32[1]{0:T(128)} %bitcast.9.first_ref, bf16[320,3072]{1,0:T(8,128)(2,1)} %bitcast.25, bf16[320,3072]{1,0:T(8,128)(2,1)} %bitcast.16, bf16[320,3072]{1,0:T(8,128)(2,1)} %bitcast.21), custom_call_target="tpu_custom_call" | custom-call | flops 3355443200 | bytes 9830400 | tf_op jit(solution)/shard_map/pallas_call | solution.py:236
  41.8 0.0 collective-permute-done.r1
  41.8 0.0 collective-permute-done.1.r2
  41.8 0.0 copy-start.6
  41.9 0.0 collective-permute-done.2.r3
  41.9 0.7 copy-done.5
  42.6 0.2 copy-done.6
  42.8 0.2 copy-done.8
  42.9 7.6 %shard_map.103 = bf16[320,640]{1,0:T(8,128)(2,1)} custom-call(s32[1]{0:T(128)} %bitcast.place_ref, f32[1]{0:T(128)S(6)} %copy.13.step_ref, bf16[320,640]{1,0:T(8,128)(2,1)} %get-tuple-element.30.own, bf16[320,640]{1,0:T(8,128)(2,1)} %copy-done.5, bf16[320,640]{1,0:T(8,128)(2,1)} %copy-done.6, bf16[320,640]{1,0:T(8,128)(2,1)} %copy-done.8, ...), custom_call_target="tpu_custom_call" | custom-call | flops 1638400000 | bytes 3276800 | tf_op jit(solution)/shard_map/pallas_call | solution.py:148
  50.5 1.3 collective-permute-start.3
  51.8 3.4 %collective-permute-start.8 = (bf16[320,1024]{1,0:T(8,128)(2,1)S(1)}, bf16[320,1024]{1,0:T(8,128)(2,1)}, u32[]{:S(2)}, u32[]{:S(2)}) collective-permute-start(bf16[320,1024]{1,0:T(8,128)(2,1)S(1)} %slice.8), channel_id=1, source_target_pairs={{48,64},{64,80},{80,96},{96,112},{49,65},{65,81},{81,97},{97,113},... | collective-permute-start | bytes 1966088 | tf_op jit(solution)/shard_map/ppermute | solution.py:414
  55.2 1.5 collective-permute-start.7
  56.7 3.4 %collective-permute-start.10 = (bf16[320,1024]{1,0:T(8,128)(2,1)S(1)}, bf16[320,1024]{1,0:T(8,128)(2,1)}, u32[]{:S(2)}, u32[]{:S(2)}) collective-permute-start(bf16[320,1024]{1,0:T(8,128)(2,1)S(1)} %slice.9), channel_id=1, source_target_pairs={{48,64},{64,80},{80,96},{96,112},{49,65},{65,81},{81,97},{97,113},... | collective-permute-start | bytes 1966088 | tf_op jit(solution)/shard_map/ppermute | solution.py:414
  60.1 1.5 collective-permute-start.9
  61.6 7.0 %all-to-all-start.1 = ((bf16[16,96,640]{2,1,0:T(8,128)(2,1)}), bf16[16,96,640]{2,1,0:T(8,128)(2,1)S(1)}, u32[]{:S(2)}, u32[]{:S(2)}) async-start(bf16[16,96,640]{2,1,0:T(8,128)(2,1)} %shard_map.102), calls=%async_computation.1 | async-start | bytes 3932160 | tf_op jit(solution)/shard_map/all_to_all | solution.py:461
  68.6 43.2 %collective-permute-done.3 = bf16[320,640]{1,0:T(8,128)(2,1)} collective-permute-done((bf16[320,640]{1,0:T(8,128)(2,1)}, bf16[320,640]{1,0:T(8,128)(2,1)}, u32[]{:S(2)}, u32[]{:S(2)}) %collective-permute-start.3) | collective-permute-done | bytes 409632 | tf_op jit(solution)/shard_map/ppermute | solution.py:414
  111.9 1.1 broadcast_select_fusion.2.rest_0_
  112.9 1.9 collective-permute-start.6
  114.9 0.0 collective-permute-done.8
  114.9 1.9 collective-permute-start.5
  116.8 0.0 collective-permute-done.7
  116.8 3.5 %collective-permute-start.4 = (bf16[320,640]{1,0:T(8,128)(2,1)S(1)}, bf16[320,640]{1,0:T(8,128)(2,1)S(1)}, u32[]{:S(2)}, u32[]{:S(2)}) collective-permute-start(bf16[320,640]{1,0:T(8,128)(2,1)S(1)} %broadcast_select_fusion.2.rest_0_), channel_id=1, source_target_pairs={{0,16},{16,32},{32,48},{64,80},{80,96},{96,112},{1,17},{17,33},{33... | collective-permute-start | bytes 1228808 | tf_op jit(solution)/shard_map/ppermute | solution.py:414
  120.3 2.0 broadcast_select_fusion.1.rest_0_
  122.3 0.0 collective-permute-done.10
  122.3 0.0 collective-permute-done.9
  122.3 2.0 broadcast_select_fusion.rest_1_
  124.4 0.0 copy-done.1
  124.4 9.2 %shard_map.104.att_ref = f32[320,3072]{1,0:T(8,128)} custom-call(s32[1]{0:T(128)} %bitcast.9.first_ref, bf16[320,3072]{1,0:T(8,128)(2,1)} %bitcast.26, bf16[320,3072]{1,0:T(8,128)(2,1)} %bitcast.17, bf16[320,3072]{1,0:T(8,128)(2,1)} %bitcast.22, bf16[320,1024]{1,0:T(8,128)(2,1)} %broadcast_select_fusion.1.rest_0_, ...), custom_call_target="tpu_custom_call", output_to_operand_aliasing={{}: (6, {})} | custom-call | flops 1677721600 | bytes 5242880 | tf_op jit(solution)/shard_map/pallas_call | solution.py:260
  133.6 0.0 collective-permute-done.6.rest_3_
  133.6 0.0 collective-permute-done.5.rest_2_
  133.6 0.0 collective-permute-done.4.rest_1_
  133.6 0.7 copy-done.2
  134.3 0.2 copy-done.3
  134.5 0.8 copy-done.4
  135.3 17.5 %shard_map.105 = (bf16[320,640]{1,0:T(8,128)(2,1)}, bf16[320,640]{1,0:T(8,128)(2,1)}, bf16[320,640]{1,0:T(8,128)(2,1)}, bf16[320,640]{1,0:T(8,128)(2,1)}) custom-call(s32[1]{0:T(128)} %bitcast.place_ref, bf16[320,3072]{1,0:T(8,128)(2,1)} %bitcast.18, bf16[320,3072]{1,0:T(8,128)(2,1)} %bitcast.23, f32[1,3072]{1,0:T(1,128)} %r_ref.3, ...), custom_call_target="tpu_custom_call" | custom-call | flops 7549747200 | bytes 3932160 | tf_op jit(solution)/shard_map/pallas_call | solution.py:94
  152.8 3.9 %collective-permute-start.11 = (bf16[320,640]{1,0:T(8,128)(2,1)}, bf16[320,640]{1,0:T(8,128)(2,1)S(1)}, u32[]{:S(2)}, u32[]{:S(2)}) collective-permute-start(bf16[320,640]{1,0:T(8,128)(2,1)} %get-tuple-element.43), channel_id=1, source_target_pairs={{112,64},{64,80},{80,96},{113,65},{65,81},{81,97},{114,66},{66,82}... | collective-permute-start | bytes 1228808 | tf_op jit(solution)/shard_map/ppermute | solution.py:414
  156.7 1.9 collective-permute-start.12
  158.6 1.5 collective-permute-start.13
  160.2 13.3 %collective-permute-done.11.r1 = bf16[320,640]{1,0:T(8,128)(2,1)S(1)} collective-permute-done((bf16[320,640]{1,0:T(8,128)(2,1)}, bf16[320,640]{1,0:T(8,128)(2,1)S(1)}, u32[]{:S(2)}, u32[]{:S(2)}) %collective-permute-start.11) | collective-permute-done | bytes 409632 | tf_op jit(solution)/shard_map/ppermute | solution.py:414
  173.5 0.0 collective-permute-done.12.r2
  173.5 0.0 collective-permute-done.13.r3
  173.5 0.8 copy-done.9
  174.3 0.2 copy-done.11
  174.4 0.1 copy-done.13
  174.5 7.3 %shard_map.106.rest_4_ = bf16[320,640]{1,0:T(8,128)(2,1)} custom-call(s32[1]{0:T(128)} %bitcast.place_ref, f32[1]{0:T(128)S(6)} %copy.13.step_ref, bf16[320,640]{1,0:T(8,128)(2,1)} %get-tuple-element.42.own, bf16[320,640]{1,0:T(8,128)(2,1)} %copy-done.9, bf16[320,640]{1,0:T(8,128)(2,1)} %copy-done.11, bf16[320,640]{1,0:T(8,128)(2,1)} %copy-done.13, ...), custom_call_target="tpu_custom_call" | custom-call | flops 1638400000 | bytes 3276800 | tf_op jit(solution)/shard_map/pallas_call | solution.py:148
  181.8 6.6 %collective-permute-start.16 = (bf16[320,640]{1,0:T(8,128)(2,1)}, bf16[320,640]{1,0:T(8,128)(2,1)S(1)}, u32[]{:S(2)}, u32[]{:S(2)}) collective-permute-start(bf16[320,640]{1,0:T(8,128)(2,1)} %shard_map.106.rest_4_), channel_id=1, source_target_pairs={{64,112},{80,64},{96,80},{65,113},{81,65},{97,81},{66,114},{82,66}... | collective-permute-start | bytes 1228808 | tf_op jit(solution)/shard_map/ppermute | solution.py:414
  188.4 5.0 %collective-permute-start.15 = (bf16[320,640]{1,0:T(8,128)(2,1)}, bf16[320,640]{1,0:T(8,128)(2,1)S(1)}, u32[]{:S(2)}, u32[]{:S(2)}) collective-permute-start(bf16[320,640]{1,0:T(8,128)(2,1)} %shard_map.106.rest_4_), channel_id=1, source_target_pairs={{64,96},{80,112},{96,64},{65,97},{81,113},{97,65},{66,98},{82,114}... | collective-permute-start | bytes 1228808 | tf_op jit(solution)/shard_map/ppermute | solution.py:414
  193.4 1.3 collective-permute-start.14
  194.7 5.2 %collective-permute-done.16.rest_7_ = bf16[320,640]{1,0:T(8,128)(2,1)S(1)} collective-permute-done((bf16[320,640]{1,0:T(8,128)(2,1)}, bf16[320,640]{1,0:T(8,128)(2,1)S(1)}, u32[]{:S(2)}, u32[]{:S(2)}) %collective-permute-start.16) | collective-permute-done | bytes 409632 | tf_op jit(solution)/shard_map/ppermute | solution.py:414
  199.9 4.6 %collective-permute-done.15.rest_6_ = bf16[320,640]{1,0:T(8,128)(2,1)S(1)} collective-permute-done((bf16[320,640]{1,0:T(8,128)(2,1)}, bf16[320,640]{1,0:T(8,128)(2,1)S(1)}, u32[]{:S(2)}, u32[]{:S(2)}) %collective-permute-start.15) | collective-permute-done | bytes 409632 | tf_op jit(solution)/shard_map/ppermute | solution.py:414
  204.4 6.5 %collective-permute-done.14.rest_5_ = bf16[320,640]{1,0:T(8,128)(2,1)S(1)} collective-permute-done((bf16[320,640]{1,0:T(8,128)(2,1)}, bf16[320,640]{1,0:T(8,128)(2,1)S(1)}, u32[]{:S(2)}, u32[]{:S(2)}) %collective-permute-start.14) | collective-permute-done | bytes 409632 | tf_op jit(solution)/shard_map/ppermute | solution.py:414
  210.9 0.0 copy-done.7
  210.9 0.8 copy-done.12
  211.7 10.7 %shard_map.107 = bf16[16,96,640]{2,1,0:T(8,128)(2,1)} custom-call(s32[1]{0:T(128)} %bitcast.place_ref, s32[1]{0:T(128)} %bitcast.1.part_ref, bf16[320,3072]{1,0:T(8,128)(2,1)} %bitcast.27, f32[320,3072]{1,0:T(8,128)} %shard_map.104.att_ref, bf16[320,640]{1,0:T(8,128)(2,1)} %copy-done.1, bf16[320,640]{1,0:T(8,128)(2,1)} %copy-done.4, ...), custom_call_target="tpu_custom_call" | custom-call | flops 3774873600 | bytes 7864320 | tf_op jit(solution)/shard_map/pallas_call | solution.py:320
  222.4 0.0 all-to-all-done.1.g_ref
  222.4 35.0 %all_to_all.10.m_ref = bf16[16,96,640]{2,1,0:T(8,128)(2,1)} all-to-all(bf16[16,96,640]{2,1,0:T(8,128)(2,1)} %shard_map.107), channel_id=1, replica_groups=mesh['ctx'=8,'head'=16] {'head'}, dimensions={0} | all-to-all | bytes 3932160 | tf_op jit(solution)/shard_map/all_to_all | solution.py:465
  257.4 8.3 %shard_map.108 = bf16[2,96,5120]{2,1,0:T(8,128)(2,1)} custom-call(bf16[16,96,640]{2,1,0:T(8,128)(2,1)} %all_to_all.10.m_ref, bf16[16,96,640]{2,1,0:T(8,128)(2,1)} %copy-done, f32[1,5120]{1,0:T(1,128)} %bitcast.28), custom_call_target="tpu_custom_call" | custom-call | flops 9830400 | bytes 5898240 | tf_op jit(solution)/shard_map/pallas_call | solution.py:385
  (15 shorter events, 0.0 us)
Async XLA Ops:
  17.2 24.7 %collective-permute-start = (bf16[320,640]{1,0:T(8,128)(2,1)}, bf16[320,640]{1,0:T(8,128)(2,1)S(1)}, u32[]{:S(2)}, u32[]{:S(2)}) collective-permute-start(bf16[320,640]{1,0:T(8,128)(2,1)} %get-tuple-element.27), channel_id=1, source_target_pairs={{48,0},{0,16},{16,32},{49,1},{1,17},{17,33},{50,2},{2,18},{18,34},... | collective-permute-start | bytes 1228808 | tf_op jit(solution)/shard_map/ppermute | solution.py:414
  17.9 24.0 %collective-permute-start.1 = (bf16[320,640]{1,0:T(8,128)(2,1)}, bf16[320,640]{1,0:T(8,128)(2,1)S(1)}, u32[]{:S(2)}, u32[]{:S(2)}) collective-permute-start(bf16[320,640]{1,0:T(8,128)(2,1)} %get-tuple-element.28), channel_id=1, source_target_pairs={{32,0},{48,16},{0,32},{33,1},{49,17},{1,33},{34,2},{50,18},{2,34},... | collective-permute-start | bytes 1228808 | tf_op jit(solution)/shard_map/ppermute | solution.py:414
  18.6 23.3 %collective-permute-start.2 = (bf16[320,640]{1,0:T(8,128)(2,1)}, bf16[320,640]{1,0:T(8,128)(2,1)S(1)}, u32[]{:S(2)}, u32[]{:S(2)}) collective-permute-start(bf16[320,640]{1,0:T(8,128)(2,1)} %get-tuple-element.29), channel_id=1, source_target_pairs={{16,0},{32,16},{48,32},{17,1},{33,17},{49,33},{18,2},{34,18},{50,3... | collective-permute-start | bytes 1228808 | tf_op jit(solution)/shard_map/ppermute | solution.py:414
  41.8 0.8 copy-start.5
  41.8 0.9 copy-start.6
  41.9 1.1 copy-start.8
  50.5 61.4 %collective-permute-start.3 = (bf16[320,640]{1,0:T(8,128)(2,1)}, bf16[320,640]{1,0:T(8,128)(2,1)}, u32[]{:S(2)}, u32[]{:S(2)}) collective-permute-start(bf16[320,640]{1,0:T(8,128)(2,1)} %shard_map.103), channel_id=1, source_target_pairs={{0,64},{16,80},{32,96},{1,65},{17,81},{33,97},{2,66},{18,82},{34,9... | collective-permute-start | bytes 1228808 | tf_op jit(solution)/shard_map/ppermute | solution.py:414
  51.8 63.1 %collective-permute-start.8 = (bf16[320,1024]{1,0:T(8,128)(2,1)S(1)}, bf16[320,1024]{1,0:T(8,128)(2,1)}, u32[]{:S(2)}, u32[]{:S(2)}) collective-permute-start(bf16[320,1024]{1,0:T(8,128)(2,1)S(1)} %slice.8), channel_id=1, source_target_pairs={{48,64},{64,80},{80,96},{96,112},{49,65},{65,81},{81,97},{97,113},... | collective-permute-start | bytes 1966088 | tf_op jit(solution)/shard_map/ppermute | solution.py:414
  55.2 61.6 %collective-permute-start.7 = (bf16[320,1024]{1,0:T(8,128)(2,1)S(1)}, bf16[320,1024]{1,0:T(8,128)(2,1)}, u32[]{:S(2)}, u32[]{:S(2)}) collective-permute-start(bf16[320,1024]{1,0:T(8,128)(2,1)S(1)} %slice.8), channel_id=1, source_target_pairs={{0,16},{16,32},{32,48},{1,17},{17,33},{33,49},{2,18},{18,34},{34,5... | collective-permute-start | bytes 1966088 | tf_op jit(solution)/shard_map/ppermute | solution.py:414
  56.7 65.6 %collective-permute-start.10 = (bf16[320,1024]{1,0:T(8,128)(2,1)S(1)}, bf16[320,1024]{1,0:T(8,128)(2,1)}, u32[]{:S(2)}, u32[]{:S(2)}) collective-permute-start(bf16[320,1024]{1,0:T(8,128)(2,1)S(1)} %slice.9), channel_id=1, source_target_pairs={{48,64},{64,80},{80,96},{96,112},{49,65},{65,81},{81,97},{97,113},... | collective-permute-start | bytes 1966088 | tf_op jit(solution)/shard_map/ppermute | solution.py:414
  60.1 62.2 %collective-permute-start.9 = (bf16[320,1024]{1,0:T(8,128)(2,1)S(1)}, bf16[320,1024]{1,0:T(8,128)(2,1)}, u32[]{:S(2)}, u32[]{:S(2)}) collective-permute-start(bf16[320,1024]{1,0:T(8,128)(2,1)S(1)} %slice.9), channel_id=1, source_target_pairs={{0,16},{16,32},{32,48},{1,17},{17,33},{33,49},{2,18},{18,34},{34,5... | collective-permute-start | bytes 1966088 | tf_op jit(solution)/shard_map/ppermute | solution.py:414
  61.6 160.8 %all-to-all-start.1 = ((bf16[16,96,640]{2,1,0:T(8,128)(2,1)}), bf16[16,96,640]{2,1,0:T(8,128)(2,1)S(1)}, u32[]{:S(2)}, u32[]{:S(2)}) async-start(bf16[16,96,640]{2,1,0:T(8,128)(2,1)} %shard_map.102), calls=%async_computation.1 | async-start | bytes 3932160 | tf_op jit(solution)/shard_map/all_to_all | solution.py:461
  112.9 11.5 %copy-start.1 = (bf16[320,640]{1,0:T(8,128)(2,1)}, bf16[320,640]{1,0:T(8,128)(2,1)S(1)}, u32[]{:S(2)}) copy-start(bf16[320,640]{1,0:T(8,128)(2,1)S(1)} %broadcast_select_fusion.2.rest_0_) | copy-start | bytes 1228804
  112.9 20.6 %collective-permute-start.6 = (bf16[320,640]{1,0:T(8,128)(2,1)S(1)}, bf16[320,640]{1,0:T(8,128)(2,1)S(1)}, u32[]{:S(2)}, u32[]{:S(2)}) collective-permute-start(bf16[320,640]{1,0:T(8,128)(2,1)S(1)} %broadcast_select_fusion.2.rest_0_), channel_id=1, source_target_pairs={{0,48},{16,0},{32,16},{64,112},{80,64},{96,80},{1,49},{17,1},{33,1... | collective-permute-start | bytes 1228808 | tf_op jit(solution)/shard_map/ppermute | solution.py:414
  114.9 18.7 %collective-permute-start.5 = (bf16[320,640]{1,0:T(8,128)(2,1)S(1)}, bf16[320,640]{1,0:T(8,128)(2,1)S(1)}, u32[]{:S(2)}, u32[]{:S(2)}) collective-permute-start(bf16[320,640]{1,0:T(8,128)(2,1)S(1)} %broadcast_select_fusion.2.rest_0_), channel_id=1, source_target_pairs={{0,32},{16,48},{32,0},{64,96},{80,112},{96,64},{1,33},{17,49},{33,... | collective-permute-start | bytes 1228808 | tf_op jit(solution)/shard_map/ppermute | solution.py:414
  116.8 16.8 %collective-permute-start.4 = (bf16[320,640]{1,0:T(8,128)(2,1)S(1)}, bf16[320,640]{1,0:T(8,128)(2,1)S(1)}, u32[]{:S(2)}, u32[]{:S(2)}) collective-permute-start(bf16[320,640]{1,0:T(8,128)(2,1)S(1)} %broadcast_select_fusion.2.rest_0_), channel_id=1, source_target_pairs={{0,16},{16,32},{32,48},{64,80},{80,96},{96,112},{1,17},{17,33},{33... | collective-permute-start | bytes 1228808 | tf_op jit(solution)/shard_map/ppermute | solution.py:414
  133.6 0.8 copy-start.2
  133.6 0.9 copy-start.3
  134.5 0.8 copy-start.4
  152.8 20.7 %collective-permute-start.11 = (bf16[320,640]{1,0:T(8,128)(2,1)}, bf16[320,640]{1,0:T(8,128)(2,1)S(1)}, u32[]{:S(2)}, u32[]{:S(2)}) collective-permute-start(bf16[320,640]{1,0:T(8,128)(2,1)} %get-tuple-element.43), channel_id=1, source_target_pairs={{112,64},{64,80},{80,96},{113,65},{65,81},{81,97},{114,66},{66,82}... | collective-permute-start | bytes 1228808 | tf_op jit(solution)/shard_map/ppermute | solution.py:414
  156.7 16.8 %collective-permute-start.12 = (bf16[320,640]{1,0:T(8,128)(2,1)}, bf16[320,640]{1,0:T(8,128)(2,1)S(1)}, u32[]{:S(2)}, u32[]{:S(2)}) collective-permute-start(bf16[320,640]{1,0:T(8,128)(2,1)} %get-tuple-element.44), channel_id=1, source_target_pairs={{96,64},{112,80},{64,96},{97,65},{113,81},{65,97},{98,66},{114,82}... | collective-permute-start | bytes 1228808 | tf_op jit(solution)/shard_map/ppermute | solution.py:414
  158.6 14.8 %collective-permute-start.13 = (bf16[320,640]{1,0:T(8,128)(2,1)}, bf16[320,640]{1,0:T(8,128)(2,1)S(1)}, u32[]{:S(2)}, u32[]{:S(2)}) collective-permute-start(bf16[320,640]{1,0:T(8,128)(2,1)} %get-tuple-element.45), channel_id=1, source_target_pairs={{80,64},{96,80},{112,96},{81,65},{97,81},{113,97},{82,66},{98,82},... | collective-permute-start | bytes 1228808 | tf_op jit(solution)/shard_map/ppermute | solution.py:414
  173.5 0.8 copy-start.9
  173.5 1.0 copy-start.11
  173.5 1.1 copy-start.13
  181.8 18.1 %collective-permute-start.16 = (bf16[320,640]{1,0:T(8,128)(2,1)}, bf16[320,640]{1,0:T(8,128)(2,1)S(1)}, u32[]{:S(2)}, u32[]{:S(2)}) collective-permute-start(bf16[320,640]{1,0:T(8,128)(2,1)} %shard_map.106.rest_4_), channel_id=1, source_target_pairs={{64,112},{80,64},{96,80},{65,113},{81,65},{97,81},{66,114},{82,66}... | collective-permute-start | bytes 1228808 | tf_op jit(solution)/shard_map/ppermute | solution.py:414
  188.4 16.0 %collective-permute-start.15 = (bf16[320,640]{1,0:T(8,128)(2,1)}, bf16[320,640]{1,0:T(8,128)(2,1)S(1)}, u32[]{:S(2)}, u32[]{:S(2)}) collective-permute-start(bf16[320,640]{1,0:T(8,128)(2,1)} %shard_map.106.rest_4_), channel_id=1, source_target_pairs={{64,96},{80,112},{96,64},{65,97},{81,113},{97,65},{66,98},{82,114}... | collective-permute-start | bytes 1228808 | tf_op jit(solution)/shard_map/ppermute | solution.py:414
  193.4 17.5 %collective-permute-start.14 = (bf16[320,640]{1,0:T(8,128)(2,1)}, bf16[320,640]{1,0:T(8,128)(2,1)S(1)}, u32[]{:S(2)}, u32[]{:S(2)}) collective-permute-start(bf16[320,640]{1,0:T(8,128)(2,1)} %shard_map.106.rest_4_), channel_id=1, source_target_pairs={{64,80},{80,96},{96,112},{65,81},{81,97},{97,113},{66,82},{82,98},... | collective-permute-start | bytes 1228808 | tf_op jit(solution)/shard_map/ppermute | solution.py:414
  199.9 11.0 %copy-start.7 = (bf16[320,640]{1,0:T(8,128)(2,1)}, bf16[320,640]{1,0:T(8,128)(2,1)S(1)}, u32[]{:S(2)}) copy-start(bf16[320,640]{1,0:T(8,128)(2,1)S(1)} %collective-permute-done.16.rest_7_) | copy-start | bytes 1228804
  204.4 6.5 %copy-start.10 = (bf16[320,640]{1,0:T(8,128)(2,1)}, bf16[320,640]{1,0:T(8,128)(2,1)S(1)}, u32[]{:S(2)}) copy-start(bf16[320,640]{1,0:T(8,128)(2,1)S(1)} %collective-permute-done.15.rest_6_) | copy-start | bytes 1228804
  210.9 0.8 copy-start.12
  222.4 35.0 %copy-start = (bf16[16,96,640]{2,1,0:T(8,128)(2,1)}, bf16[16,96,640]{2,1,0:T(8,128)(2,1)S(1)}, u32[]{:S(2)}) copy-start(bf16[16,96,640]{2,1,0:T(8,128)(2,1)S(1)} %all-to-all-done.1.g_ref) | copy-start | bytes 5898244

commit v2 on v1

--- a/solution.py
+++ b/solution.py
@@ -397,17 +397,21 @@
 
 
 def reduce_moves(part):
-    base = part * RING
-    return [
-        [(base + (m - s) % RING, base + m) for m in range(3)] for s in range(1, RING)
-    ]
+    return [[(part, (m - s) % RING, part, m) for m in range(3)] for s in range(1, RING)]
 
 
 def spread_moves(parts):
-    return [
-        [(p * RING + m, p * RING + (m + s) % RING) for p in parts for m in range(3)]
-        for s in range(1, RING)
-    ]
+    return [[(p, m, p, (m + s) % RING) for p in parts for m in range(3)] for s in range(1, RING)]
+
+
+def ring_send(array, moves):
+    heads = lax.axis_size("head")
+
+    def index(part, place, head):
+        return (part * RING + (place + 2 * (head % 2)) % RING) * heads + head
+
+    pairs = [(index(a, b, h), index(c, d, h)) for a, b, c, d in moves for h in range(heads)]
+    return lax.ppermute(array, ("ctx", "head"), pairs)
 
 
 def send(array, pairs):
@@ -428,39 +432,40 @@
 ):
     ctx = lax.axis_index("ctx")
     heads = lax.axis_size("head")
-    place = (ctx % RING).reshape(1).astype(jnp.int32)
+    place = ((ctx + 2 * (lax.axis_index("head") % 2)) % RING).reshape(1).astype(jnp.int32)
     part = (ctx // RING).reshape(1).astype(jnp.int32)
     first = (ctx == 0).reshape(1).astype(jnp.int32)
     qt, kt, vt, gt = query_rows.T, key_rows.T, value_rows.T, gate_rows.T
     count = qt.shape[1]
     start = [fast_first[0], fast_third[0], fast_second[0].T]
-
-    tail_k, tail_v = kt[:, count - WINDOW :], vt[:, count - WINDOW :]
-    late_pairs = [(i, i + 1) for i in range(3, 7)]
-    early_pairs = [(i, i + 1) for i in range(3)]
-    rim_late = (send(tail_k, late_pairs), send(tail_v, late_pairs))
-
+    hold = lax.optimization_barrier
+
+    tails = (kt[:, count - WINDOW :], vt[:, count - WINDOW :])
+    rim_late = [send(t, [(i, i + 1) for i in range(4, 7)]) for t in tails]
     own, *out = grads(place, kt, vt, token_rates, start, True)
-    pieces = [own] + [send(o, p) for o, p in zip(out, reduce_moves(0))]
-    att_main = attend_main(qt, kt, vt, first)
+    pieces = [own] + [ring_send(o, p) for o, p in zip(out, reduce_moves(0))]
+    q_main, rim_late = hold((qt, rim_late))
+    att_main = attend_main(q_main, kt, vt, first)
+    pieces, att_main, tails = hold((pieces, att_main, tails))
+    fresh = update(place, step_sizes, pieces, start)
+    fresh, tails, gt = hold((fresh, tails, gt))
+    crossed = ring_send(fresh, [(0, m, 1, m) for m in range(3)])
+    rim_early = [send(t, [(i, i + 1) for i in range(4)]) for t in tails]
     gates = pack_gate(gt, heads)
-    pieces, att_main, gates, tails = lax.optimization_barrier(
-        (pieces, att_main, gates, (tail_k, tail_v))
-    )
-    rim_early = (send(tails[0], early_pairs), send(tails[1], early_pairs))
-    fresh = update(place, step_sizes, pieces, start)
-    crossed = send(fresh, [(m, RING + m) for m in range(3)])
     held = jnp.where(part[0] == 0, fresh, crossed)
-    early = [held] + [send(held, p) for p in spread_moves((0, 1))]
-    rims = [jnp.where(part[0] == 0, a, b) for a, b in zip(rim_early, rim_late)]
+    held, gates = hold((held, gates))
+    gate_tokens = lax.all_to_all(gates, "head", split_axis=0, concat_axis=0)
+    early = [held] + [ring_send(held, p) for p in spread_moves((0, 1))]
+    early = hold(early)
+
+    own, *out = grads(place, kt, vt, token_rates, early, False)
+    own, out, att_main = hold((own, out, att_main))
+    pieces = [own] + [ring_send(o, p) for o, p in zip(out, reduce_moves(1))]
+    rims = [jnp.where(ctx <= RING, a, b) for a, b in zip(rim_early, rim_late)]
     att = attend_rim(qt, kt, vt, rims[0], rims[1], att_main, first)
-    early, att = lax.optimization_barrier((early, att))
-
-    own, *out = grads(place, kt, vt, token_rates, early, False)
-    pieces = [own] + [send(o, p) for o, p in zip(out, reduce_moves(1))]
-    gate_tokens = lax.all_to_all(gates, "head", split_axis=0, concat_axis=0)
+    pieces, att = hold((pieces, att))
     fresh = update(place, step_sizes, pieces, [early[0]])
-    late = [fresh] + [send(fresh, p) for p in spread_moves((1,))]
+    late = [fresh] + [ring_send(fresh, p) for p in spread_moves((1,))]
     mixed = apply_mix(place, part, qt, att, early, late, heads)
     mixed_tokens = lax.all_to_all(mixed, "head", split_axis=0, concat_axis=0)
     return final(mixed_tokens, gate_tokens, norm_gain)

time: 268 us -> 231 us (0.86)
  waiting for transfers between devices: 72.8 us -> 40.8 us
  starting transfers between devices: 47.8 us -> 43.5 us
    ppermute x17 -> x4, waiting for transfers between devices: 72.8 us -> 2.74 us  [send(): return lax.ppermute(array, 'ctx', pairs)]
    ppermute x0 -> x13, waiting for transfers between devices: none -> 38 us  [ring_send(): return lax.ppermute(array, ('ctx', 'head'), pairs)]
    ppermute x17 -> x4, starting transfers between devices: 40.8 us -> 9.4 us  [send(): return lax.ppermute(array, 'ctx', pairs)]
    ppermute x0 -> x13, starting transfers between devices: none -> 27.1 us  [ring_send(): return lax.ppermute(array, ('ctx', 'head'), pairs)]
  transfers between devices with their start and end apart: 18 -> 18, of which waited for: 5 -> 7; matrix products, arithmetic and copies ran while one was open for 3% -> 3% of each run, Pallas kernels for 24% -> 36%
where the time goes in v2:
time: 231 us; the launch traced here: 229 us
  Pallas kernels  97.7 us (42%)
  starting transfers between devices  43.5 us (19%)
  waiting for transfers between devices  40.8 us (18%)
  blocking collectives  34.7 us (15%)
  local copies, waits for them, and re-layouts  6.6 us (3%)
  other arithmetic  4.85 us (2%)
    ppermute x13, waiting for transfers between devices, ring_send(): return lax.ppermute(array, ('ctx', 'head'), pairs)  38 us
    pallas_call x2, Pallas kernels, grads(): pl.pallas_call(functools.partial(grads_kernel, static), grid_spec=pltpu.P...  34.8 us
    all_to_all x1, blocking collectives, shards(): mixed_tokens = lax.all_to_all(mixed, 'head', split_axis=0, concat_axis=0)  34.7 us
    ppermute x13, starting transfers between devices, ring_send(): return lax.ppermute(array, ('ctx', 'head'), pairs)  27.1 us
    pallas_call x1, Pallas kernels, attend_main(): pl.pallas_call(functools.partial(attend_kernel, blocks, None), grid_spec=...  15.6 us
    pallas_call x2, Pallas kernels, update(): pl.pallas_call(update_kernel, in_specs=[smem, smem] + [vmem] * (4 + len(o...  14.8 us
    pallas_call x1, Pallas kernels, apply_mix(): pl.pallas_call(functools.partial(apply_kernel, dests), grid_spec=pltpu.Pr...  10.7 us
    ppermute x4, starting transfers between devices, send(): return lax.ppermute(array, 'ctx', pairs)  9.4 us
  transfers between devices with their start and end apart: 18, of which 7 were waited for; matrix products, arithmetic and copies ran while one was open for 3% of the time, Pallas kernels for 36%

profile of v2, /device:TPU:32, one launch (start us, length us, event | category | flops | bytes accessed | tf_op | source)
XLA Modules:
  0.0 229.0 jit_solution(4135602374831577126)
XLA Ops:
  0.0 1.1 slice.9
  1.1 3.4 %collective-permute-start.4 = (bf16[320,1024]{1,0:T(8,128)(2,1)S(1)}, bf16[320,1024]{1,0:T(8,128)(2,1)S(1)}, u32[]{:S(2)}, u32[]{:S(2)}) collective-permute-start(bf16[320,1024]{1,0:T(8,128)(2,1)S(1)} %slice.9), channel_id=1, source_target_pairs={{64,80},{80,96},{96,112},{65,81},{81,97},{97,113},{66,82},{82,98},... | collective-permute-start | bytes 1966088 | tf_op jit(solution)/shard_map/ppermute | solution.py:418
  4.6 2.0 slice.8
  6.5 3.4 %collective-permute-start.3 = (bf16[320,1024]{1,0:T(8,128)(2,1)}, bf16[320,1024]{1,0:T(8,128)(2,1)S(1)}, u32[]{:S(2)}, u32[]{:S(2)}) collective-permute-start(bf16[320,1024]{1,0:T(8,128)(2,1)} %slice.8), channel_id=1, source_target_pairs={{64,80},{80,96},{96,112},{65,81},{81,97},{97,113},{66,82},{82,98},... | collective-permute-start | bytes 1966088 | tf_op jit(solution)/shard_map/ppermute | solution.py:418
  10.0 17.2 %shard_map.100 = (bf16[320,640]{1,0:T(8,128)(2,1)}, bf16[320,640]{1,0:T(8,128)(2,1)}, bf16[320,640]{1,0:T(8,128)(2,1)}, bf16[320,640]{1,0:T(8,128)(2,1)}) custom-call(s32[1]{0:T(128)} %bitcast.place_ref, bf16[320,3072]{1,0:T(8,128)(2,1)} %bitcast.15, bf16[320,3072]{1,0:T(8,128)(2,1)} %bitcast.20, f32[1,3072]{1,0:T(1,128)} %r_ref.3, ...), custom_call_target="tpu_custom_call" | custom-call | flops 7549747200 | bytes 3932160 | tf_op jit(solution)/shard_map/pallas_call | solution.py:94
  27.2 0.7 collective-permute-start
  27.9 0.7 collective-permute-start.1
  28.6 0.7 collective-permute-start.2
  29.9 0.0 collective-permute-done.4
  29.9 2.7 %collective-permute-done.3 = bf16[320,1024]{1,0:T(8,128)(2,1)S(1)} collective-permute-done((bf16[320,1024]{1,0:T(8,128)(2,1)}, bf16[320,1024]{1,0:T(8,128)(2,1)S(1)}, u32[]{:S(2)}, u32[]{:S(2)}) %collective-permute-start.3) | collective-permute-done | bytes 655392 | tf_op jit(solution)/shard_map/ppermute | solution.py:418
  32.7 15.6 %shard_map.101.rest_2_ = f32[320,3072]{1,0:T(8,128)} custom-call(s32[1]{0:T(128)} %bitcast.9.first_ref, bf16[320,3072]{1,0:T(8,128)(2,1)} %bitcast.25, bf16[320,3072]{1,0:T(8,128)(2,1)} %bitcast.16, bf16[320,3072]{1,0:T(8,128)(2,1)} %bitcast.21), custom_call_target="tpu_custom_call" | custom-call | flops 3355443200 | bytes 9830400 | tf_op jit(solution)/shard_map/pallas_call | solution.py:236
  48.2 0.0 copy-done.1
  48.2 0.0 collective-permute-done.r1
  48.2 0.0 copy-start.4
  48.2 0.0 collective-permute-done.1.r2
  48.3 0.0 copy-start.6
  48.3 0.0 collective-permute-done.2.r3
  48.3 0.7 copy-done.4
  49.0 0.1 copy-done.6
  49.1 0.2 copy-done.8
  49.3 7.5 %shard_map.102 = bf16[320,640]{1,0:T(8,128)(2,1)} custom-call(s32[1]{0:T(128)} %bitcast.place_ref, f32[1]{0:T(128)S(6)} %copy.13.step_ref, bf16[320,640]{1,0:T(8,128)(2,1)} %get-tuple-element.48.own, bf16[320,640]{1,0:T(8,128)(2,1)} %copy-done.4, bf16[320,640]{1,0:T(8,128)(2,1)} %copy-done.6, bf16[320,640]{1,0:T(8,128)(2,1)} %copy-done.8, ...), custom_call_target="tpu_custom_call" | custom-call | flops 1638400000 | bytes 3276800 | tf_op jit(solution)/shard_map/pallas_call | solution.py:148
  56.8 1.3 collective-permute-start.5
  58.1 1.3 collective-permute-start.12
  59.4 4.3 %shard_map.103 = bf16[16,96,640]{2,1,0:T(8,128)(2,1)} custom-call(bf16[320,3072]{1,0:T(8,128)(2,1)} %bitcast.24), custom_call_target="tpu_custom_call" | custom-call | bytes 7864320 | tf_op jit(solution)/shard_map/pallas_call | solution.py:350
  63.8 19.5 %collective-permute-done.5 = bf16[320,640]{1,0:T(8,128)(2,1)S(1)} collective-permute-done((bf16[320,640]{1,0:T(8,128)(2,1)}, bf16[320,640]{1,0:T(8,128)(2,1)S(1)}, u32[]{:S(2)}, u32[]{:S(2)}) %collective-permute-start.5) | collective-permute-done | bytes 409632 | tf_op jit(solution)/shard_map/ppermute | solution.py:414
  83.3 0.0 copy-done.2
  83.3 0.8 broadcast_select_fusion.2.rest_0_
  84.1 1.9 collective-permute-start.8
  86.0 1.9 collective-permute-start.7
  88.0 4.8 %collective-permute-start.6 = (bf16[320,640]{1,0:T(8,128)(2,1)}, bf16[320,640]{1,0:T(8,128)(2,1)}, u32[]{:S(2)}, u32[]{:S(2)}) collective-permute-start(bf16[320,640]{1,0:T(8,128)(2,1)} %broadcast_select_fusion.2.rest_0_), channel_id=1, source_target_pairs={{0,16},{33,49},{2,18},{35,51},{4,20},{37,53},{6,22},{39,55},{8,24}... | collective-permute-start | bytes 1228808 | tf_op jit(solution)/shard_map/ppermute | solution.py:414
  92.8 1.3 collective-permute-start.13
  94.1 7.0 %all-to-all-start.1 = ((bf16[16,96,640]{2,1,0:T(8,128)(2,1)}), bf16[16,96,640]{2,1,0:T(8,128)(2,1)S(1)}, u32[]{:S(2)}, u32[]{:S(2)}) async-start(bf16[16,96,640]{2,1,0:T(8,128)(2,1)} %shard_map.103), calls=%async_computation.1 | async-start | bytes 3932160 | tf_op jit(solution)/shard_map/all_to_all | solution.py:457
  101.1 0.0 collective-permute-done.12
  101.1 2.0 broadcast_select_fusion.1.rest_0_
  103.1 0.0 collective-permute-done.8.rest_3_
  103.1 0.0 collective-permute-done.7.rest_2_
  103.1 1.3 collective-permute-done.6.rest_1_
  104.4 17.6 %shard_map.104 = (bf16[320,640]{1,0:T(8,128)(2,1)}, bf16[320,640]{1,0:T(8,128)(2,1)}, bf16[320,640]{1,0:T(8,128)(2,1)}, bf16[320,640]{1,0:T(8,128)(2,1)}) custom-call(s32[1]{0:T(128)} %bitcast.place_ref, bf16[320,3072]{1,0:T(8,128)(2,1)} %bitcast.17, bf16[320,3072]{1,0:T(8,128)(2,1)} %bitcast.22, f32[1,3072]{1,0:T(1,128)} %r_ref.3, ...), custom_call_target="tpu_custom_call" | custom-call | flops 7549747200 | bytes 3932160 | tf_op jit(solution)/shard_map/pallas_call | solution.py:94
  121.9 4.4 %collective-permute-start.9 = (bf16[320,640]{1,0:T(8,128)(2,1)}, bf16[320,640]{1,0:T(8,128)(2,1)S(1)}, u32[]{:S(2)}, u32[]{:S(2)}) collective-permute-start(bf16[320,640]{1,0:T(8,128)(2,1)} %get-tuple-element.67), channel_id=1, source_target_pairs={{112,64},{81,97},{114,66},{83,99},{116,68},{85,101},{118,70},{87,1... | collective-permute-start | bytes 1228808 | tf_op jit(solution)/shard_map/ppermute | solution.py:414
  126.3 2.1 collective-permute-start.10
  128.4 1.3 collective-permute-start.11
  129.7 0.0 collective-permute-done.13
  129.7 2.0 broadcast_select_fusion.rest_1_
  131.7 9.2 %shard_map.105.att_ref = f32[320,3072]{1,0:T(8,128)} custom-call(s32[1]{0:T(128)} %bitcast.9.first_ref, bf16[320,3072]{1,0:T(8,128)(2,1)} %bitcast.26, bf16[320,3072]{1,0:T(8,128)(2,1)} %bitcast.18, bf16[320,3072]{1,0:T(8,128)(2,1)} %bitcast.23, bf16[320,1024]{1,0:T(8,128)(2,1)} %broadcast_select_fusion.1.rest_0_, ...), custom_call_target="tpu_custom_call", output_to_operand_aliasing={{}: (6, {})} | custom-call | flops 1677721600 | bytes 5242880 | tf_op jit(solution)/shard_map/pallas_call | solution.py:260
  140.9 3.9 %collective-permute-done.9.r1 = bf16[320,640]{1,0:T(8,128)(2,1)S(1)} collective-permute-done((bf16[320,640]{1,0:T(8,128)(2,1)}, bf16[320,640]{1,0:T(8,128)(2,1)S(1)}, u32[]{:S(2)}, u32[]{:S(2)}) %collective-permute-start.9) | collective-permute-done | bytes 409632 | tf_op jit(solution)/shard_map/ppermute | solution.py:414
  144.8 0.0 collective-permute-done.10.r2
  144.8 0.0 collective-permute-done.11.r3
  144.8 0.7 copy-done.3
  145.5 0.2 copy-done.5
  145.7 0.8 copy-done.7
  146.5 7.3 %shard_map.106.rest_4_ = bf16[320,640]{1,0:T(8,128)(2,1)} custom-call(s32[1]{0:T(128)} %bitcast.place_ref, f32[1]{0:T(128)S(6)} %copy.13.step_ref, bf16[320,640]{1,0:T(8,128)(2,1)} %get-tuple-element.76.own, bf16[320,640]{1,0:T(8,128)(2,1)} %copy-done.3, bf16[320,640]{1,0:T(8,128)(2,1)} %copy-done.5, bf16[320,640]{1,0:T(8,128)(2,1)} %copy-done.7, ...), custom_call_target="tpu_custom_call" | custom-call | flops 1638400000 | bytes 3276800 | tf_op jit(solution)/shard_map/pallas_call | solution.py:148
  153.8 1.9 collective-permute-start.16
  155.7 2.0 collective-permute-start.15
  157.7 3.5 %collective-permute-start.14 = (bf16[320,640]{1,0:T(8,128)(2,1)}, bf16[320,640]{1,0:T(8,128)(2,1)S(1)}, u32[]{:S(2)}, u32[]{:S(2)}) collective-permute-start(bf16[320,640]{1,0:T(8,128)(2,1)} %shard_map.106.rest_4_), channel_id=1, source_target_pairs={{64,80},{97,113},{66,82},{99,115},{68,84},{101,117},{70,86},{103,1... | collective-permute-start | bytes 1228808 | tf_op jit(solution)/shard_map/ppermute | solution.py:414
  161.2 2.6 %collective-permute-done.16.rest_7_ = bf16[320,640]{1,0:T(8,128)(2,1)S(1)} collective-permute-done((bf16[320,640]{1,0:T(8,128)(2,1)}, bf16[320,640]{1,0:T(8,128)(2,1)S(1)}, u32[]{:S(2)}, u32[]{:S(2)}) %collective-permute-start.16) | collective-permute-done | bytes 409632 | tf_op jit(solution)/shard_map/ppermute | solution.py:414
  163.8 7.9 %collective-permute-done.15.rest_6_ = bf16[320,640]{1,0:T(8,128)(2,1)S(1)} collective-permute-done((bf16[320,640]{1,0:T(8,128)(2,1)}, bf16[320,640]{1,0:T(8,128)(2,1)S(1)}, u32[]{:S(2)}, u32[]{:S(2)}) %collective-permute-start.15) | collective-permute-done | bytes 409632 | tf_op jit(solution)/shard_map/ppermute | solution.py:414
  171.8 2.8 %collective-permute-done.14.rest_5_ = bf16[320,640]{1,0:T(8,128)(2,1)S(1)} collective-permute-done((bf16[320,640]{1,0:T(8,128)(2,1)}, bf16[320,640]{1,0:T(8,128)(2,1)S(1)}, u32[]{:S(2)}, u32[]{:S(2)}) %collective-permute-start.14) | collective-permute-done | bytes 409632 | tf_op jit(solution)/shard_map/ppermute | solution.py:414
  174.6 0.0 copy-done.10
  174.6 0.8 copy-done.11
  175.3 10.7 %shard_map.107 = bf16[16,96,640]{2,1,0:T(8,128)(2,1)} custom-call(s32[1]{0:T(128)} %bitcast.place_ref, s32[1]{0:T(128)} %bitcast.1.part_ref, bf16[320,3072]{1,0:T(8,128)(2,1)} %bitcast.27, f32[320,3072]{1,0:T(8,128)} %shard_map.105.att_ref, bf16[320,640]{1,0:T(8,128)(2,1)} %broadcast_select_fusion.2.rest_0_, ...), custom_call_target="tpu_custom_call" | custom-call | flops 3774873600 | bytes 7864320 | tf_op jit(solution)/shard_map/pallas_call | solution.py:320
  186.1 0.0 all-to-all-done.1.g_ref
  186.1 34.7 %all_to_all.10.m_ref = bf16[16,96,640]{2,1,0:T(8,128)(2,1)} all-to-all(bf16[16,96,640]{2,1,0:T(8,128)(2,1)} %shard_map.107), channel_id=1, replica_groups=mesh['ctx'=8,'head'=16] {'head'}, dimensions={0} | all-to-all | bytes 3932160 | tf_op jit(solution)/shard_map/all_to_all | solution.py:470
  220.7 0.0 copy-done
  220.7 8.3 %shard_map.108 = bf16[2,96,5120]{2,1,0:T(8,128)(2,1)} custom-call(bf16[16,96,640]{2,1,0:T(8,128)(2,1)} %all_to_all.10.m_ref, bf16[16,96,640]{2,1,0:T(8,128)(2,1)} %copy-done, f32[1,5120]{1,0:T(1,128)} %bitcast.28), custom_call_target="tpu_custom_call" | custom-call | flops 9830400 | bytes 5898240 | tf_op jit(solution)/shard_map/pallas_call | solution.py:385
  (11 shorter events, 0.0 us)
Async XLA Ops:
  1.1 28.8 %collective-permute-start.4 = (bf16[320,1024]{1,0:T(8,128)(2,1)S(1)}, bf16[320,1024]{1,0:T(8,128)(2,1)S(1)}, u32[]{:S(2)}, u32[]{:S(2)}) collective-permute-start(bf16[320,1024]{1,0:T(8,128)(2,1)S(1)} %slice.9), channel_id=1, source_target_pairs={{64,80},{80,96},{96,112},{65,81},{81,97},{97,113},{66,82},{82,98},... | collective-permute-start | bytes 1966088 | tf_op jit(solution)/shard_map/ppermute | solution.py:418
  6.5 26.1 %collective-permute-start.3 = (bf16[320,1024]{1,0:T(8,128)(2,1)}, bf16[320,1024]{1,0:T(8,128)(2,1)S(1)}, u32[]{:S(2)}, u32[]{:S(2)}) collective-permute-start(bf16[320,1024]{1,0:T(8,128)(2,1)} %slice.8), channel_id=1, source_target_pairs={{64,80},{80,96},{96,112},{65,81},{81,97},{97,113},{66,82},{82,98},... | collective-permute-start | bytes 1966088 | tf_op jit(solution)/shard_map/ppermute | solution.py:418
  27.2 21.0 %collective-permute-start = (bf16[320,640]{1,0:T(8,128)(2,1)}, bf16[320,640]{1,0:T(8,128)(2,1)S(1)}, u32[]{:S(2)}, u32[]{:S(2)}) collective-permute-start(bf16[320,640]{1,0:T(8,128)(2,1)} %get-tuple-element.44), channel_id=1, source_target_pairs={{48,0},{17,33},{50,2},{19,35},{52,4},{21,37},{54,6},{23,39},{56,8}... | collective-permute-start | bytes 1228808 | tf_op jit(solution)/shard_map/ppermute | solution.py:414
  27.9 20.4 %collective-permute-start.1 = (bf16[320,640]{1,0:T(8,128)(2,1)}, bf16[320,640]{1,0:T(8,128)(2,1)S(1)}, u32[]{:S(2)}, u32[]{:S(2)}) collective-permute-start(bf16[320,640]{1,0:T(8,128)(2,1)} %get-tuple-element.45), channel_id=1, source_target_pairs={{32,0},{1,33},{34,2},{3,35},{36,4},{5,37},{38,6},{7,39},{40,8},{9,... | collective-permute-start | bytes 1228808 | tf_op jit(solution)/shard_map/ppermute | solution.py:414
  28.6 19.7 %collective-permute-start.2 = (bf16[320,640]{1,0:T(8,128)(2,1)}, bf16[320,640]{1,0:T(8,128)(2,1)S(1)}, u32[]{:S(2)}, u32[]{:S(2)}) collective-permute-start(bf16[320,640]{1,0:T(8,128)(2,1)} %get-tuple-element.46), channel_id=1, source_target_pairs={{16,0},{49,33},{18,2},{51,35},{20,4},{53,37},{22,6},{55,39},{24,8}... | collective-permute-start | bytes 1228808 | tf_op jit(solution)/shard_map/ppermute | solution.py:414
  32.7 15.6 %copy-start.1 = (bf16[320,1024]{1,0:T(8,128)(2,1)}, bf16[320,1024]{1,0:T(8,128)(2,1)S(1)}, u32[]{:S(2)}) copy-start(bf16[320,1024]{1,0:T(8,128)(2,1)S(1)} %collective-permute-done.3) | copy-start | bytes 1966084
  48.2 0.7 copy-start.4
  48.3 0.9 copy-start.6
  48.3 1.0 copy-start.8
  56.8 26.5 %collective-permute-start.5 = (bf16[320,640]{1,0:T(8,128)(2,1)}, bf16[320,640]{1,0:T(8,128)(2,1)S(1)}, u32[]{:S(2)}, u32[]{:S(2)}) collective-permute-start(bf16[320,640]{1,0:T(8,128)(2,1)} %shard_map.102), channel_id=1, source_target_pairs={{0,64},{33,97},{2,66},{35,99},{4,68},{37,101},{6,70},{39,103},{8,7... | collective-permute-start | bytes 1228808 | tf_op jit(solution)/shard_map/ppermute | solution.py:414
  58.1 43.0 %collective-permute-start.12 = (bf16[320,1024]{1,0:T(8,128)(2,1)}, bf16[320,1024]{1,0:T(8,128)(2,1)}, u32[]{:S(2)}, u32[]{:S(2)}) collective-permute-start(bf16[320,1024]{1,0:T(8,128)(2,1)} %slice.8), channel_id=1, source_target_pairs={{0,16},{16,32},{32,48},{48,64},{1,17},{17,33},{33,49},{49,65},{2,1... | collective-permute-start | bytes 1966088 | tf_op jit(solution)/shard_map/ppermute | solution.py:418
  59.4 23.9 %copy-start.2 = (bf16[320,640]{1,0:T(8,128)(2,1)S(1)}, bf16[320,640]{1,0:T(8,128)(2,1)}, u32[]{:S(2)}) copy-start(bf16[320,640]{1,0:T(8,128)(2,1)} %shard_map.102) | copy-start | bytes 1228804
  84.1 19.0 %collective-permute-start.8 = (bf16[320,640]{1,0:T(8,128)(2,1)}, bf16[320,640]{1,0:T(8,128)(2,1)}, u32[]{:S(2)}, u32[]{:S(2)}) collective-permute-start(bf16[320,640]{1,0:T(8,128)(2,1)} %broadcast_select_fusion.2.rest_0_), channel_id=1, source_target_pairs={{0,48},{33,17},{2,50},{35,19},{4,52},{37,21},{6,54},{39,23},{8,56}... | collective-permute-start | bytes 1228808 | tf_op jit(solution)/shard_map/ppermute | solution.py:414
  86.0 17.1 %collective-permute-start.7 = (bf16[320,640]{1,0:T(8,128)(2,1)}, bf16[320,640]{1,0:T(8,128)(2,1)}, u32[]{:S(2)}, u32[]{:S(2)}) collective-permute-start(bf16[320,640]{1,0:T(8,128)(2,1)} %broadcast_select_fusion.2.rest_0_), channel_id=1, source_target_pairs={{0,32},{33,1},{2,34},{35,3},{4,36},{37,5},{6,38},{39,7},{8,40},{41... | collective-permute-start | bytes 1228808 | tf_op jit(solution)/shard_map/ppermute | solution.py:414
  88.0 16.4 %collective-permute-start.6 = (bf16[320,640]{1,0:T(8,128)(2,1)}, bf16[320,640]{1,0:T(8,128)(2,1)}, u32[]{:S(2)}, u32[]{:S(2)}) collective-permute-start(bf16[320,640]{1,0:T(8,128)(2,1)} %broadcast_select_fusion.2.rest_0_), channel_id=1, source_target_pairs={{0,16},{33,49},{2,18},{35,51},{4,20},{37,53},{6,22},{39,55},{8,24}... | collective-permute-start | bytes 1228808 | tf_op jit(solution)/shard_map/ppermute | solution.py:414
  92.8 36.9 %collective-permute-start.13 = (bf16[320,1024]{1,0:T(8,128)(2,1)S(1)}, bf16[320,1024]{1,0:T(8,128)(2,1)}, u32[]{:S(2)}, u32[]{:S(2)}) collective-permute-start(bf16[320,1024]{1,0:T(8,128)(2,1)S(1)} %slice.9), channel_id=1, source_target_pairs={{0,16},{16,32},{32,48},{48,64},{1,17},{17,33},{33,49},{49,65},{2,1... | collective-permute-start | bytes 1966088 | tf_op jit(solution)/shard_map/ppermute | solution.py:418
  94.1 92.0 %all-to-all-start.1 = ((bf16[16,96,640]{2,1,0:T(8,128)(2,1)}), bf16[16,96,640]{2,1,0:T(8,128)(2,1)S(1)}, u32[]{:S(2)}, u32[]{:S(2)}) async-start(bf16[16,96,640]{2,1,0:T(8,128)(2,1)} %shard_map.103), calls=%async_computation.1 | async-start | bytes 3932160 | tf_op jit(solution)/shard_map/all_to_all | solution.py:457
  121.9 22.9 %collective-permute-start.9 = (bf16[320,640]{1,0:T(8,128)(2,1)}, bf16[320,640]{1,0:T(8,128)(2,1)S(1)}, u32[]{:S(2)}, u32[]{:S(2)}) collective-permute-start(bf16[320,640]{1,0:T(8,128)(2,1)} %get-tuple-element.67), channel_id=1, source_target_pairs={{112,64},{81,97},{114,66},{83,99},{116,68},{85,101},{118,70},{87,1... | collective-permute-start | bytes 1228808 | tf_op jit(solution)/shard_map/ppermute | solution.py:414
  126.3 18.5 %collective-permute-start.10 = (bf16[320,640]{1,0:T(8,128)(2,1)}, bf16[320,640]{1,0:T(8,128)(2,1)S(1)}, u32[]{:S(2)}, u32[]{:S(2)}) collective-permute-start(bf16[320,640]{1,0:T(8,128)(2,1)} %get-tuple-element.68), channel_id=1, source_target_pairs={{96,64},{65,97},{98,66},{67,99},{100,68},{69,101},{102,70},{71,103... | collective-permute-start | bytes 1228808 | tf_op jit(solution)/shard_map/ppermute | solution.py:414
  128.4 16.4 %collective-permute-start.11 = (bf16[320,640]{1,0:T(8,128)(2,1)}, bf16[320,640]{1,0:T(8,128)(2,1)S(1)}, u32[]{:S(2)}, u32[]{:S(2)}) collective-permute-start(bf16[320,640]{1,0:T(8,128)(2,1)} %get-tuple-element.69), channel_id=1, source_target_pairs={{80,64},{113,97},{82,66},{115,99},{84,68},{117,101},{86,70},{119,1... | collective-permute-start | bytes 1228808 | tf_op jit(solution)/shard_map/ppermute | solution.py:414
  144.8 0.8 copy-start.3
  144.8 0.9 copy-start.5
  145.7 0.8 copy-start.7
  153.8 10.0 %collective-permute-start.16 = (bf16[320,640]{1,0:T(8,128)(2,1)}, bf16[320,640]{1,0:T(8,128)(2,1)S(1)}, u32[]{:S(2)}, u32[]{:S(2)}) collective-permute-start(bf16[320,640]{1,0:T(8,128)(2,1)} %shard_map.106.rest_4_), channel_id=1, source_target_pairs={{64,112},{97,81},{66,114},{99,83},{68,116},{101,85},{70,118},{103,... | collective-permute-start | bytes 1228808 | tf_op jit(solution)/shard_map/ppermute | solution.py:414
  155.7 16.1 %collective-permute-start.15 = (bf16[320,640]{1,0:T(8,128)(2,1)}, bf16[320,640]{1,0:T(8,128)(2,1)S(1)}, u32[]{:S(2)}, u32[]{:S(2)}) collective-permute-start(bf16[320,640]{1,0:T(8,128)(2,1)} %shard_map.106.rest_4_), channel_id=1, source_target_pairs={{64,96},{97,65},{66,98},{99,67},{68,100},{101,69},{70,102},{103,71... | collective-permute-start | bytes 1228808 | tf_op jit(solution)/shard_map/ppermute | solution.py:414
  157.7 16.9 %collective-permute-start.14 = (bf16[320,640]{1,0:T(8,128)(2,1)}, bf16[320,640]{1,0:T(8,128)(2,1)S(1)}, u32[]{:S(2)}, u32[]{:S(2)}) collective-permute-start(bf16[320,640]{1,0:T(8,128)(2,1)} %shard_map.106.rest_4_), channel_id=1, source_target_pairs={{64,80},{97,113},{66,82},{99,115},{68,84},{101,117},{70,86},{103,1... | collective-permute-start | bytes 1228808 | tf_op jit(solution)/shard_map/ppermute | solution.py:414
  163.8 10.7 %copy-start.9 = (bf16[320,640]{1,0:T(8,128)(2,1)}, bf16[320,640]{1,0:T(8,128)(2,1)S(1)}, u32[]{:S(2)}) copy-start(bf16[320,640]{1,0:T(8,128)(2,1)S(1)} %collective-permute-done.16.rest_7_) | copy-start | bytes 1228804
  171.8 2.8 %copy-start.10 = (bf16[320,640]{1,0:T(8,128)(2,1)}, bf16[320,640]{1,0:T(8,128)(2,1)S(1)}, u32[]{:S(2)}) copy-start(bf16[320,640]{1,0:T(8,128)(2,1)S(1)} %collective-permute-done.15.rest_6_) | copy-start | bytes 1228804
  174.6 0.8 copy-start.11
  186.1 34.7 %copy-start = (bf16[16,96,640]{2,1,0:T(8,128)(2,1)}, bf16[16,96,640]{2,1,0:T(8,128)(2,1)S(1)}, u32[]{:S(2)}) copy-start(bf16[16,96,640]{2,1,0:T(8,128)(2,1)S(1)} %all-to-all-done.1.g_ref) | copy-start | bytes 5898244

commit v3 on v2

--- a/solution.py
+++ b/solution.py
@@ -13,6 +13,7 @@
 RING = 4
 QB = 256
 TB = 512
+FINAL_ROWS = 32
 
 coef_first = 3.4445
 coef_second = -4.775
@@ -48,7 +49,7 @@
 
 def grads_kernel(static, place_ref, x_ref, v_ref, r_ref, *rest):
     n_src = 3 if static else RING
-    sources, (own, s1, s2, s3), (acc, wt) = rest[:n_src], rest[n_src : n_src + 4], rest[n_src + 4 :]
+    sources, (own, s1, s2, s3), (acc, wt) = rest[:n_src], rest[n_src : n_src + 4], rest[-2:]
     step = pl.program_id(0)
     place = place_ref[0]
 
@@ -65,6 +66,9 @@
         acc[...] = jnp.zeros_like(acc)
 
     x = x_ref[...]
+    if static:
+        rest[-4][...] = x
+        rest[-3][...] = v_ref[...]
     e = (r_ref[...] * v_ref[...].astype(F32)).astype(BF16)
     gate = dot(wt[0], x)
     up = dot(wt[1], x)
@@ -91,20 +95,24 @@
     whole = pl.BlockSpec(matrix, lambda i, p: (0, 0))
     tokens = pl.BlockSpec((width, TB), lambda i, p: (0, i))
     hidden = matrix[1]
+    steps = count // TB
+    rim = WINDOW // TB
+    tails = [pl.BlockSpec((width, TB), lambda i, p: (0, jnp.maximum(i - (steps - rim), 0)))] * 2
     return pl.pallas_call(
         functools.partial(grads_kernel, static),
         grid_spec=pltpu.PrefetchScalarGridSpec(
             num_scalar_prefetch=1,
-            grid=(count // TB,),
+            grid=(steps,),
             in_specs=[tokens, tokens, pl.BlockSpec((1, TB), lambda i, p: (0, i))]
             + [whole] * len(sources),
-            out_specs=[whole] * 4,
+            out_specs=[whole] * 4 + (tails if static else []),
             scratch_shapes=[
                 pltpu.VMEM((3,) + matrix, F32),
                 pltpu.VMEM((3, hidden, width), BF16),
             ],
         ),
-        out_shape=[jax.ShapeDtypeStruct(matrix, BF16)] * 4,
+        out_shape=[jax.ShapeDtypeStruct(matrix, BF16)] * 4
+        + [jax.ShapeDtypeStruct((width, WINDOW), BF16)] * (2 if static else 0),
         compiler_params=params(),
         cost_estimate=pl.CostEstimate(
             flops=12 * width * hidden * count,
@@ -361,38 +369,45 @@
 
 
 def final_kernel(m_ref, g_ref, gain_ref, out):
-    heads, _, double = m_ref.shape
+    heads, rows, double = m_ref.shape
     width = double // 2
-    for half in range(2):
-        lanes = slice(half * width, (half + 1) * width)
-        total = 0.0
-        for h in range(heads):
-            m = m_ref[h, :, lanes].astype(F32)
-            total += jnp.sum(m * m, axis=1, keepdims=True)
-        factor = lax.rsqrt(total / (heads * width) + epsilon)
-        for h in range(0, heads, 2):
-            cols = slice(h * width, (h + 2) * width)
-            m = jnp.concatenate([m_ref[h, :, lanes], m_ref[h + 1, :, lanes]], 1).astype(F32)
-            g = jnp.concatenate([g_ref[h, :, lanes], g_ref[h + 1, :, lanes]], 1).astype(F32)
-            out[half, :, cols] = (m * factor * gain_ref[:, cols] * (g * sigmoid(g))).astype(BF16)
+    squares = jnp.zeros((rows, double), F32)
+    for h in range(heads):
+        m = m_ref[h].astype(F32)
+        squares += m * m
+    left = lax.broadcasted_iota(jnp.int32, (1, double), 1) < width
+    mean = 1.0 / (heads * width)
+    early = lax.rsqrt(jnp.sum(squares[:, :width], 1, keepdims=True) * mean + epsilon)
+    late = lax.rsqrt(jnp.sum(squares[:, width:], 1, keepdims=True) * mean + epsilon)
+    factor = jnp.where(left, early, late)
+    for h in range(0, heads, 2):
+        pair = []
+        for j in (h, h + 1):
+            g = g_ref[j].astype(F32)
+            scale = factor * gain_ref[j : j + 1]
+            pair.append((m_ref[j].astype(F32) * scale * (g * sigmoid(g))).astype(BF16))
+        cols = slice(h * width, (h + 2) * width)
+        out[0, :, cols] = jnp.concatenate([y[:, :width] for y in pair], 1)
+        out[1, :, cols] = jnp.concatenate([y[:, width:] for y in pair], 1)
 
 
 def final(mixed, gates, gain):
     heads, rows, double = mixed.shape
-    block = 32
+    block = FINAL_ROWS
     wide = heads * double // 2
+    gain = gain.reshape(heads, double // 2)
     tokens = pl.BlockSpec((heads, block, double), lambda i: (0, i, 0))
     result = pl.pallas_call(
         final_kernel,
         grid=(rows // block,),
-        in_specs=[tokens, tokens, pl.BlockSpec((1, wide), lambda i: (0, 0))],
+        in_specs=[tokens, tokens, pl.BlockSpec((heads, double), lambda i: (0, 0))],
         out_specs=pl.BlockSpec((2, block, wide), lambda i: (0, i, 0)),
         out_shape=jax.ShapeDtypeStruct((2, rows, wide), BF16),
         compiler_params=params(),
         cost_estimate=pl.CostEstimate(
             flops=20 * rows * wide, bytes_accessed=12 * rows * wide, transcendentals=2 * rows * wide
         ),
-    )(mixed, gates, gain.reshape(1, wide))
+    )(mixed, gates, jnp.concatenate([gain, gain], 1))
     return result.reshape(2 * rows, wide)
 
 
@@ -436,27 +451,25 @@
     part = (ctx // RING).reshape(1).astype(jnp.int32)
     first = (ctx == 0).reshape(1).astype(jnp.int32)
     qt, kt, vt, gt = query_rows.T, key_rows.T, value_rows.T, gate_rows.T
-    count = qt.shape[1]
     start = [fast_first[0], fast_third[0], fast_second[0].T]
     hold = lax.optimization_barrier
 
-    tails = (kt[:, count - WINDOW :], vt[:, count - WINDOW :])
+    own, *out = grads(place, kt, vt, token_rates, start, True)
+    out, tails = out[:3], out[3:]
+    pieces = [own] + [ring_send(o, p) for o, p in zip(out, reduce_moves(0))]
     rim_late = [send(t, [(i, i + 1) for i in range(4, 7)]) for t in tails]
-    own, *out = grads(place, kt, vt, token_rates, start, True)
-    pieces = [own] + [ring_send(o, p) for o, p in zip(out, reduce_moves(0))]
-    q_main, rim_late = hold((qt, rim_late))
-    att_main = attend_main(q_main, kt, vt, first)
-    pieces, att_main, tails = hold((pieces, att_main, tails))
+    att_main = attend_main(qt, kt, vt, first)
+    pieces, att_main = hold((pieces, att_main))
     fresh = update(place, step_sizes, pieces, start)
-    fresh, tails, gt = hold((fresh, tails, gt))
+    fresh, gt, rim_late = hold((fresh, gt, rim_late))
     crossed = ring_send(fresh, [(0, m, 1, m) for m in range(3)])
-    rim_early = [send(t, [(i, i + 1) for i in range(4)]) for t in tails]
     gates = pack_gate(gt, heads)
     held = jnp.where(part[0] == 0, fresh, crossed)
     held, gates = hold((held, gates))
     gate_tokens = lax.all_to_all(gates, "head", split_axis=0, concat_axis=0)
     early = [held] + [ring_send(held, p) for p in spread_moves((0, 1))]
-    early = hold(early)
+    early, tails = hold((early, tails))
+    rim_early = [send(t, [(i, i + 1) for i in range(4)]) for t in tails]
 
     own, *out = grads(place, kt, vt, token_rates, early, False)
     own, out, att_main = hold((own, out, att_main))

time: 231 us -> 220 us (0.952)
  blocking collectives: 34.7 us -> 0 us
  waiting for transfers between devices: 40.8 us -> 68.2 us
  Pallas kernels: 97.7 us -> 94.6 us
  starting transfers between devices: 43.5 us -> 46.1 us
    all_to_all x1 -> x0, blocking collectives: 34.7 us -> none  [shards(): mixed_tokens = lax.all_to_all(mixed, 'head', split_axis=0, concat_axis=0)]
    all_to_all x0 -> x1, waiting for transfers between devices: none -> 27.1 us  [shards(): mixed_tokens = lax.all_to_all(mixed, 'head', split_axis=0, concat_axis=0)]
    ppermute x4, waiting for transfers between devices: 2.74 us -> 16.4 us  [send(): return lax.ppermute(array, 'ctx', pairs)]
    ppermute x13, waiting for transfers between devices: 38 us -> 24.7 us  [ring_send(): return lax.ppermute(array, ('ctx', 'head'), pairs)]
    all_to_all x0 -> x1, starting transfers between devices: none -> 6.28 us  [shards(): mixed_tokens = lax.all_to_all(mixed, 'head', split_axis=0, concat_axis=0)]
    ppermute x13, starting transfers between devices: 27.1 us -> 22.4 us  [ring_send(): return lax.ppermute(array, ('ctx', 'head'), pairs)]
    pallas_call x1, Pallas kernels: 8.31 us -> 4.96 us  [final(): pl.pallas_call(final_kernel, grid=(rows // block,), in_specs=[tokens, tok...]
    slice x2 -> x0, local copies, waits for them, and re-layouts: 3.1 us -> none  [shards(): tails = (kt[:, count - WINDOW:], vt[:, count - WINDOW:])]
  transfers between devices with their start and end apart: 18 -> 19, of which waited for: 7 -> 7; matrix products, arithmetic and copies ran while one was open for 3% -> 1% of each run, Pallas kernels for 36% -> 33%
where the time goes in v3:
time: 220 us; the launch traced here: 218 us
  Pallas kernels  94.6 us (43%)
  waiting for transfers between devices  68.2 us (31%)
  starting transfers between devices  46.1 us (21%)
  local copies, waits for them, and re-layouts  4.92 us (2%)
  other arithmetic  3.31 us (2%)
    pallas_call x2, Pallas kernels, grads(): pl.pallas_call(functools.partial(grads_kernel, static), grid_spec=pltpu.P...  35.2 us
    all_to_all x1, waiting for transfers between devices, shards(): mixed_tokens = lax.all_to_all(mixed, 'head', split_axis=0, concat_axis=0)  27.1 us
    ppermute x13, waiting for transfers between devices, ring_send(): return lax.ppermute(array, ('ctx', 'head'), pairs)  24.7 us
    ppermute x13, starting transfers between devices, ring_send(): return lax.ppermute(array, ('ctx', 'head'), pairs)  22.4 us
    ppermute x4, waiting for transfers between devices, send(): return lax.ppermute(array, 'ctx', pairs)  16.4 us
    pallas_call x1, Pallas kernels, attend_main(): pl.pallas_call(functools.partial(attend_kernel, blocks, None), grid_spec=...  15.4 us
    pallas_call x2, Pallas kernels, update(): pl.pallas_call(update_kernel, in_specs=[smem, smem] + [vmem] * (4 + len(o...  14.8 us
    pallas_call x1, Pallas kernels, apply_mix(): pl.pallas_call(functools.partial(apply_kernel, dests), grid_spec=pltpu.Pr...  10.7 us
  transfers between devices with their start and end apart: 19, of which 7 were waited for; matrix products, arithmetic and copies ran while one was open for 1% of the time, Pallas kernels for 33%

profile of v3, /device:TPU:32, one launch (start us, length us, event | category | flops | bytes accessed | tf_op | source)
XLA Modules:
  0.0 218.0 jit_solution(4320166232730757209)
XLA Ops:
  0.0 17.6 %shard_map.100 = (bf16[320,640]{1,0:T(8,128)(2,1)}, bf16[320,640]{1,0:T(8,128)(2,1)}, bf16[320,640]{1,0:T(8,128)(2,1)}, bf16[320,640]{1,0:T(8,128)(2,1)}, bf16[3...) custom-call(s32[1]{0:T(128)} %bitcast.place_ref, bf16[320,3072]{1,0:T(8,128)(2,1)} %bitcast.14, ...), custom_call_target="tpu_custom_call" | custom-call | flops 7549747200 | bytes 3932160 | tf_op jit(solution)/shard_map/pallas_call | solution.py:101
  17.6 3.4 %collective-permute-start.3 = (bf16[320,1024]{1,0:T(8,128)(2,1)}, bf16[320,1024]{1,0:T(8,128)(2,1)S(1)}, u32[]{:S(2)}, u32[]{:S(2)}) collective-permute-start(bf16[320,1024]{1,0:T(8,128)(2,1)} %get-tuple-element.68), channel_id=1, source_target_pairs={{64,80},{80,96},{96,112},{65,81},{81,97},{97,113},{66,82},{82,98},... | collective-permute-start | bytes 1966088 | tf_op jit(solution)/shard_map/ppermute | solution.py:433
  21.1 3.4 %collective-permute-start.4 = (bf16[320,1024]{1,0:T(8,128)(2,1)}, bf16[320,1024]{1,0:T(8,128)(2,1)S(1)}, u32[]{:S(2)}, u32[]{:S(2)}) collective-permute-start(bf16[320,1024]{1,0:T(8,128)(2,1)} %get-tuple-element.70), channel_id=1, source_target_pairs={{64,80},{80,96},{96,112},{65,81},{81,97},{97,113},{66,82},{82,98},... | collective-permute-start | bytes 1966088 | tf_op jit(solution)/shard_map/ppermute | solution.py:433
  24.5 0.7 collective-permute-start
  25.2 0.7 collective-permute-start.1
  25.9 0.7 collective-permute-start.2
  27.2 15.4 %shard_map.101.rest_2_ = f32[320,3072]{1,0:T(8,128)} custom-call(s32[1]{0:T(128)} %bitcast.9.first_ref, bf16[320,3072]{1,0:T(8,128)(2,1)} %bitcast.22, bf16[320,3072]{1,0:T(8,128)(2,1)} %bitcast.15, bf16[320,3072]{1,0:T(8,128)(2,1)} %bitcast.19), custom_call_target="tpu_custom_call" | custom-call | flops 3355443200 | bytes 9830400 | tf_op jit(solution)/shard_map/pallas_call | solution.py:244
  42.6 0.0 collective-permute-done.r1
  42.6 0.0 collective-permute-done.1.r2
  42.6 0.0 copy-start.8
  42.6 0.0 collective-permute-done.2.r3
  42.6 0.0 copy-start.10
  42.6 0.7 copy-done.6
  43.3 0.2 copy-done.8
  43.5 0.2 copy-done.10
  43.7 7.5 %shard_map.102 = bf16[320,640]{1,0:T(8,128)(2,1)} custom-call(s32[1]{0:T(128)} %bitcast.place_ref, f32[1]{0:T(128)S(6)} %copy.13.step_ref, bf16[320,640]{1,0:T(8,128)(2,1)} %get-tuple-element.46.own, bf16[320,640]{1,0:T(8,128)(2,1)} %copy-done.6, bf16[320,640]{1,0:T(8,128)(2,1)} %copy-done.8, bf16[320,640]{1,0:T(8,128)(2,1)} %copy-done.10, ...), custom_call_target="tpu_custom_call" | custom-call | flops 1638400000 | bytes 3276800 | tf_op jit(solution)/shard_map/pallas_call | solution.py:156
  51.2 0.0 collective-permute-done.3
  51.2 0.0 collective-permute-done.4
  51.2 1.3 collective-permute-start.5
  52.5 0.0 copy-start.1
  52.5 4.4 %shard_map.103 = bf16[16,96,640]{2,1,0:T(8,128)(2,1)} custom-call(bf16[320,3072]{1,0:T(8,128)(2,1)} %bitcast.13), custom_call_target="tpu_custom_call" | custom-call | bytes 7864320 | tf_op jit(solution)/shard_map/pallas_call | solution.py:358
  56.9 7.3 %collective-permute-done.5 = bf16[320,640]{1,0:T(8,128)(2,1)S(1)} collective-permute-done((bf16[320,640]{1,0:T(8,128)(2,1)}, bf16[320,640]{1,0:T(8,128)(2,1)S(1)}, u32[]{:S(2)}, u32[]{:S(2)}) %collective-permute-start.5) | collective-permute-done | bytes 409632 | tf_op jit(solution)/shard_map/ppermute | solution.py:429
  64.1 0.8 broadcast_select_fusion.2.rest_0_
  64.9 2.0 collective-permute-start.6
  67.0 3.4 %collective-permute-start.7 = (bf16[320,640]{1,0:T(8,128)(2,1)}, bf16[320,640]{1,0:T(8,128)(2,1)}, u32[]{:S(2)}, u32[]{:S(2)}) collective-permute-start(bf16[320,640]{1,0:T(8,128)(2,1)} %broadcast_select_fusion.2.rest_0_), channel_id=1, source_target_pairs={{0,32},{33,1},{2,34},{35,3},{4,36},{37,5},{6,38},{39,7},{8,40},{41... | collective-permute-start | bytes 1228808 | tf_op jit(solution)/shard_map/ppermute | solution.py:429
  70.3 1.9 collective-permute-start.8
  72.3 7.8 %all-to-all-start.1 = ((bf16[16,96,640]{2,1,0:T(8,128)(2,1)}), bf16[16,96,640]{2,1,0:T(8,128)(2,1)S(1)}, u32[]{:S(2)}, u32[]{:S(2)}) async-start(bf16[16,96,640]{2,1,0:T(8,128)(2,1)} %shard_map.103), calls=%async_computation.1 | async-start | bytes 3932160 | tf_op jit(solution)/shard_map/all_to_all | solution.py:469
  80.1 0.0 collective-permute-done.6.rest_1_
  80.1 4.5 %collective-permute-done.7.rest_2_ = bf16[320,640]{1,0:T(8,128)(2,1)} collective-permute-done((bf16[320,640]{1,0:T(8,128)(2,1)}, bf16[320,640]{1,0:T(8,128)(2,1)}, u32[]{:S(2)}, u32[]{:S(2)}) %collective-permute-start.7) | collective-permute-done | bytes 409632 | tf_op jit(solution)/shard_map/ppermute | solution.py:429
  84.5 0.0 collective-permute-done.8.rest_3_
  84.5 1.3 collective-permute-start.12
  85.8 1.5 collective-permute-start.13
  87.3 17.6 %shard_map.104 = (bf16[320,640]{1,0:T(8,128)(2,1)}, bf16[320,640]{1,0:T(8,128)(2,1)}, bf16[320,640]{1,0:T(8,128)(2,1)}, bf16[320,640]{1,0:T(8,128)(2,1)}) custom-call(s32[1]{0:T(128)} %bitcast.place_ref, bf16[320,3072]{1,0:T(8,128)(2,1)} %bitcast.16, bf16[320,3072]{1,0:T(8,128)(2,1)} %bitcast.20, f32[1,3072]{1,0:T(1,128)} %r_ref.3, ...), custom_call_target="tpu_custom_call" | custom-call | flops 7549747200 | bytes 3932160 | tf_op jit(solution)/shard_map/pallas_call | solution.py:101
  104.9 1.9 collective-permute-start.9
  106.8 3.2 %collective-permute-start.10 = (bf16[320,640]{1,0:T(8,128)(2,1)}, bf16[320,640]{1,0:T(8,128)(2,1)S(1)}, u32[]{:S(2)}, u32[]{:S(2)}) collective-permute-start(bf16[320,640]{1,0:T(8,128)(2,1)} %get-tuple-element.66), channel_id=1, source_target_pairs={{96,64},{65,97},{98,66},{67,99},{100,68},{69,101},{102,70},{71,103... | collective-permute-start | bytes 1228808 | tf_op jit(solution)/shard_map/ppermute | solution.py:429
  110.0 1.3 collective-permute-start.11
  111.3 5.1 %collective-permute-done.12 = bf16[320,1024]{1,0:T(8,128)(2,1)S(1)} collective-permute-done((bf16[320,1024]{1,0:T(8,128)(2,1)}, bf16[320,1024]{1,0:T(8,128)(2,1)S(1)}, u32[]{:S(2)}, u32[]{:S(2)}) %collective-permute-start.12) | collective-permute-done | bytes 655392 | tf_op jit(solution)/shard_map/ppermute | solution.py:433
  116.5 0.9 broadcast_select_fusion.1.rest_0_
  117.4 11.3 %collective-permute-done.13 = bf16[320,1024]{1,0:T(8,128)(2,1)S(1)} collective-permute-done((bf16[320,1024]{1,0:T(8,128)(2,1)}, bf16[320,1024]{1,0:T(8,128)(2,1)S(1)}, u32[]{:S(2)}, u32[]{:S(2)}) %collective-permute-start.13) | collective-permute-done | bytes 655392 | tf_op jit(solution)/shard_map/ppermute | solution.py:433
  128.6 0.9 broadcast_select_fusion.rest_1_
  129.5 9.2 %shard_map.105.att_ref = f32[320,3072]{1,0:T(8,128)} custom-call(s32[1]{0:T(128)} %bitcast.9.first_ref, bf16[320,3072]{1,0:T(8,128)(2,1)} %bitcast.23, bf16[320,3072]{1,0:T(8,128)(2,1)} %bitcast.17, bf16[320,3072]{1,0:T(8,128)(2,1)} %bitcast.21, bf16[320,1024]{1,0:T(8,128)(2,1)} %broadcast_select_fusion.1.rest_0_, ...), custom_call_target="tpu_custom_call", output_to_operand_aliasing={{}: (6, {})} | custom-call | flops 1677721600 | bytes 5242880 | tf_op jit(solution)/shard_map/pallas_call | solution.py:268
  138.7 0.0 collective-permute-done.9.r1
  138.7 0.0 collective-permute-done.10.r2
  138.7 0.0 collective-permute-done.11.r3
  138.7 0.7 copy-done.3
  139.4 0.1 copy-done.4
  139.6 0.8 copy-done.5
  140.4 7.3 %shard_map.106.rest_4_ = bf16[320,640]{1,0:T(8,128)(2,1)} custom-call(s32[1]{0:T(128)} %bitcast.place_ref, f32[1]{0:T(128)S(6)} %copy.13.step_ref, bf16[320,640]{1,0:T(8,128)(2,1)} %get-tuple-element.74.own, bf16[320,640]{1,0:T(8,128)(2,1)} %copy-done.3, bf16[320,640]{1,0:T(8,128)(2,1)} %copy-done.4, bf16[320,640]{1,0:T(8,128)(2,1)} %copy-done.5, ...), custom_call_target="tpu_custom_call" | custom-call | flops 1638400000 | bytes 3276800 | tf_op jit(solution)/shard_map/pallas_call | solution.py:156
  147.6 1.3 collective-permute-start.14
  148.9 1.9 collective-permute-start.15
  150.9 2.1 collective-permute-start.16
  153.0 6.1 %collective-permute-done.14.rest_5_ = bf16[320,640]{1,0:T(8,128)(2,1)S(1)} collective-permute-done((bf16[320,640]{1,0:T(8,128)(2,1)}, bf16[320,640]{1,0:T(8,128)(2,1)S(1)}, u32[]{:S(2)}, u32[]{:S(2)}) %collective-permute-start.14) | collective-permute-done | bytes 409632 | tf_op jit(solution)/shard_map/ppermute | solution.py:429
  159.1 6.8 %collective-permute-done.15.rest_6_ = bf16[320,640]{1,0:T(8,128)(2,1)S(1)} collective-permute-done((bf16[320,640]{1,0:T(8,128)(2,1)}, bf16[320,640]{1,0:T(8,128)(2,1)S(1)}, u32[]{:S(2)}, u32[]{:S(2)}) %collective-permute-start.15) | collective-permute-done | bytes 409632 | tf_op jit(solution)/shard_map/ppermute | solution.py:429
  166.0 0.0 collective-permute-done.16.rest_7_
  166.0 0.8 copy-done.9
  166.7 0.1 copy-done.11
  166.9 10.7 %shard_map.107 = bf16[16,96,640]{2,1,0:T(8,128)(2,1)} custom-call(s32[1]{0:T(128)} %bitcast.place_ref, s32[1]{0:T(128)} %bitcast.1.part_ref, bf16[320,3072]{1,0:T(8,128)(2,1)} %bitcast.24, f32[320,3072]{1,0:T(8,128)} %shard_map.105.att_ref, bf16[320,640]{1,0:T(8,128)(2,1)} %broadcast_select_fusion.2.rest_0_, ...), custom_call_target="tpu_custom_call" | custom-call | flops 3774873600 | bytes 7864320 | tf_op jit(solution)/shard_map/pallas_call | solution.py:328
  177.6 0.0 all-to-all-done.1.g_ref
  177.6 1.3 copy-done
  178.9 6.3 %all-to-all-start = ((bf16[16,96,640]{2,1,0:T(8,128)(2,1)}), bf16[16,96,640]{2,1,0:T(8,128)(2,1)}, u32[]{:S(2)}, u32[]{:S(2)}) async-start(bf16[16,96,640]{2,1,0:T(8,128)(2,1)} %shard_map.107), calls=%async_computation | async-start | bytes 3932160 | tf_op jit(solution)/shard_map/all_to_all | solution.py:483
  185.2 0.1 reshape.17
  185.2 0.7 pad_maximum_fusion.gain_ref
  185.9 27.1 %all-to-all-done.m_ref = bf16[16,96,640]{2,1,0:T(8,128)(2,1)} async-done(((bf16[16,96,640]{2,1,0:T(8,128)(2,1)}), bf16[16,96,640]{2,1,0:T(8,128)(2,1)}, u32[]{:S(2)}, u32[]{:S(2)}) %all-to-all-start) | async-done | bytes 1966112 | tf_op jit(solution)/shard_map/all_to_all | solution.py:483
  213.0 5.0 %shard_map.108 = bf16[2,96,5120]{2,1,0:T(8,128)(2,1)} custom-call(bf16[16,96,640]{2,1,0:T(8,128)(2,1)} %all-to-all-done.m_ref, bf16[16,96,640]{2,1,0:T(8,128)(2,1)} %copy-done, f32[16,640]{1,0:T(8,128)} %pad_maximum_fusion.gain_ref), custom_call_target="tpu_custom_call" | custom-call | flops 9830400 | bytes 5898240 | tf_op jit(solution)/shard_map/pallas_call | solution.py:400
  (12 shorter events, 0.0 us)
Async XLA Ops:
  17.6 33.5 %collective-permute-start.3 = (bf16[320,1024]{1,0:T(8,128)(2,1)}, bf16[320,1024]{1,0:T(8,128)(2,1)S(1)}, u32[]{:S(2)}, u32[]{:S(2)}) collective-permute-start(bf16[320,1024]{1,0:T(8,128)(2,1)} %get-tuple-element.68), channel_id=1, source_target_pairs={{64,80},{80,96},{96,112},{65,81},{81,97},{97,113},{66,82},{82,98},... | collective-permute-start | bytes 1966088 | tf_op jit(solution)/shard_map/ppermute | solution.py:433
  21.1 30.1 %collective-permute-start.4 = (bf16[320,1024]{1,0:T(8,128)(2,1)}, bf16[320,1024]{1,0:T(8,128)(2,1)S(1)}, u32[]{:S(2)}, u32[]{:S(2)}) collective-permute-start(bf16[320,1024]{1,0:T(8,128)(2,1)} %get-tuple-element.70), channel_id=1, source_target_pairs={{64,80},{80,96},{96,112},{65,81},{81,97},{97,113},{66,82},{82,98},... | collective-permute-start | bytes 1966088 | tf_op jit(solution)/shard_map/ppermute | solution.py:433
  24.5 18.1 %collective-permute-start = (bf16[320,640]{1,0:T(8,128)(2,1)}, bf16[320,640]{1,0:T(8,128)(2,1)S(1)}, u32[]{:S(2)}, u32[]{:S(2)}) collective-permute-start(bf16[320,640]{1,0:T(8,128)(2,1)} %get-tuple-element.43), channel_id=1, source_target_pairs={{48,0},{17,33},{50,2},{19,35},{52,4},{21,37},{54,6},{23,39},{56,8}... | collective-permute-start | bytes 1228808 | tf_op jit(solution)/shard_map/ppermute | solution.py:429
  25.2 17.4 %collective-permute-start.1 = (bf16[320,640]{1,0:T(8,128)(2,1)}, bf16[320,640]{1,0:T(8,128)(2,1)S(1)}, u32[]{:S(2)}, u32[]{:S(2)}) collective-permute-start(bf16[320,640]{1,0:T(8,128)(2,1)} %get-tuple-element.44), channel_id=1, source_target_pairs={{32,0},{1,33},{34,2},{3,35},{36,4},{5,37},{38,6},{7,39},{40,8},{9,... | collective-permute-start | bytes 1228808 | tf_op jit(solution)/shard_map/ppermute | solution.py:429
  25.9 16.7 %collective-permute-start.2 = (bf16[320,640]{1,0:T(8,128)(2,1)}, bf16[320,640]{1,0:T(8,128)(2,1)S(1)}, u32[]{:S(2)}, u32[]{:S(2)}) collective-permute-start(bf16[320,640]{1,0:T(8,128)(2,1)} %get-tuple-element.45), channel_id=1, source_target_pairs={{16,0},{49,33},{18,2},{51,35},{20,4},{53,37},{22,6},{55,39},{24,8}... | collective-permute-start | bytes 1228808 | tf_op jit(solution)/shard_map/ppermute | solution.py:429
  42.6 0.8 copy-start.6
  42.6 0.9 copy-start.8
  42.6 1.0 copy-start.10
  51.2 13.0 %collective-permute-start.5 = (bf16[320,640]{1,0:T(8,128)(2,1)}, bf16[320,640]{1,0:T(8,128)(2,1)S(1)}, u32[]{:S(2)}, u32[]{:S(2)}) collective-permute-start(bf16[320,640]{1,0:T(8,128)(2,1)} %shard_map.102), channel_id=1, source_target_pairs={{0,64},{33,97},{2,66},{35,99},{4,68},{37,101},{6,70},{39,103},{8,7... | collective-permute-start | bytes 1228808 | tf_op jit(solution)/shard_map/ppermute | solution.py:429
  52.5 11.6 %copy-start.1 = (bf16[320,640]{1,0:T(8,128)(2,1)S(1)}, bf16[320,640]{1,0:T(8,128)(2,1)}, u32[]{:S(2)}) copy-start(bf16[320,640]{1,0:T(8,128)(2,1)} %shard_map.102) | copy-start | bytes 1228804
  64.9 15.1 %collective-permute-start.6 = (bf16[320,640]{1,0:T(8,128)(2,1)}, bf16[320,640]{1,0:T(8,128)(2,1)}, u32[]{:S(2)}, u32[]{:S(2)}) collective-permute-start(bf16[320,640]{1,0:T(8,128)(2,1)} %broadcast_select_fusion.2.rest_0_), channel_id=1, source_target_pairs={{0,16},{33,49},{2,18},{35,51},{4,20},{37,53},{6,22},{39,55},{8,24}... | collective-permute-start | bytes 1228808 | tf_op jit(solution)/shard_map/ppermute | solution.py:429
  67.0 17.5 %collective-permute-start.7 = (bf16[320,640]{1,0:T(8,128)(2,1)}, bf16[320,640]{1,0:T(8,128)(2,1)}, u32[]{:S(2)}, u32[]{:S(2)}) collective-permute-start(bf16[320,640]{1,0:T(8,128)(2,1)} %broadcast_select_fusion.2.rest_0_), channel_id=1, source_target_pairs={{0,32},{33,1},{2,34},{35,3},{4,36},{37,5},{6,38},{39,7},{8,40},{41... | collective-permute-start | bytes 1228808 | tf_op jit(solution)/shard_map/ppermute | solution.py:429
  70.3 14.2 %collective-permute-start.8 = (bf16[320,640]{1,0:T(8,128)(2,1)}, bf16[320,640]{1,0:T(8,128)(2,1)}, u32[]{:S(2)}, u32[]{:S(2)}) collective-permute-start(bf16[320,640]{1,0:T(8,128)(2,1)} %broadcast_select_fusion.2.rest_0_), channel_id=1, source_target_pairs={{0,48},{33,17},{2,50},{35,19},{4,52},{37,21},{6,54},{39,23},{8,56}... | collective-permute-start | bytes 1228808 | tf_op jit(solution)/shard_map/ppermute | solution.py:429
  72.3 105.3 %all-to-all-start.1 = ((bf16[16,96,640]{2,1,0:T(8,128)(2,1)}), bf16[16,96,640]{2,1,0:T(8,128)(2,1)S(1)}, u32[]{:S(2)}, u32[]{:S(2)}) async-start(bf16[16,96,640]{2,1,0:T(8,128)(2,1)} %shard_map.103), calls=%async_computation.1 | async-start | bytes 3932160 | tf_op jit(solution)/shard_map/all_to_all | solution.py:469
  84.5 31.9 %collective-permute-start.12 = (bf16[320,1024]{1,0:T(8,128)(2,1)}, bf16[320,1024]{1,0:T(8,128)(2,1)S(1)}, u32[]{:S(2)}, u32[]{:S(2)}) collective-permute-start(bf16[320,1024]{1,0:T(8,128)(2,1)} %get-tuple-element.68), channel_id=1, source_target_pairs={{0,16},{16,32},{32,48},{48,64},{1,17},{17,33},{33,49},{49,65},{2,1... | collective-permute-start | bytes 1966088 | tf_op jit(solution)/shard_map/ppermute | solution.py:433
  85.8 42.8 %collective-permute-start.13 = (bf16[320,1024]{1,0:T(8,128)(2,1)}, bf16[320,1024]{1,0:T(8,128)(2,1)S(1)}, u32[]{:S(2)}, u32[]{:S(2)}) collective-permute-start(bf16[320,1024]{1,0:T(8,128)(2,1)} %get-tuple-element.70), channel_id=1, source_target_pairs={{0,16},{16,32},{32,48},{48,64},{1,17},{17,33},{33,49},{49,65},{2,1... | collective-permute-start | bytes 1966088 | tf_op jit(solution)/shard_map/ppermute | solution.py:433
  104.9 33.8 %collective-permute-start.9 = (bf16[320,640]{1,0:T(8,128)(2,1)}, bf16[320,640]{1,0:T(8,128)(2,1)S(1)}, u32[]{:S(2)}, u32[]{:S(2)}) collective-permute-start(bf16[320,640]{1,0:T(8,128)(2,1)} %get-tuple-element.65), channel_id=1, source_target_pairs={{112,64},{81,97},{114,66},{83,99},{116,68},{85,101},{118,70},{87,1... | collective-permute-start | bytes 1228808 | tf_op jit(solution)/shard_map/ppermute | solution.py:429
  106.8 31.9 %collective-permute-start.10 = (bf16[320,640]{1,0:T(8,128)(2,1)}, bf16[320,640]{1,0:T(8,128)(2,1)S(1)}, u32[]{:S(2)}, u32[]{:S(2)}) collective-permute-start(bf16[320,640]{1,0:T(8,128)(2,1)} %get-tuple-element.66), channel_id=1, source_target_pairs={{96,64},{65,97},{98,66},{67,99},{100,68},{69,101},{102,70},{71,103... | collective-permute-start | bytes 1228808 | tf_op jit(solution)/shard_map/ppermute | solution.py:429
  110.0 28.7 %collective-permute-start.11 = (bf16[320,640]{1,0:T(8,128)(2,1)}, bf16[320,640]{1,0:T(8,128)(2,1)S(1)}, u32[]{:S(2)}, u32[]{:S(2)}) collective-permute-start(bf16[320,640]{1,0:T(8,128)(2,1)} %get-tuple-element.67), channel_id=1, source_target_pairs={{80,64},{113,97},{82,66},{115,99},{84,68},{117,101},{86,70},{119,1... | collective-permute-start | bytes 1228808 | tf_op jit(solution)/shard_map/ppermute | solution.py:429
  138.7 0.8 copy-start.3
  138.7 0.9 copy-start.4
  139.6 0.8 copy-start.5
  147.6 11.5 %collective-permute-start.14 = (bf16[320,640]{1,0:T(8,128)(2,1)}, bf16[320,640]{1,0:T(8,128)(2,1)S(1)}, u32[]{:S(2)}, u32[]{:S(2)}) collective-permute-start(bf16[320,640]{1,0:T(8,128)(2,1)} %shard_map.106.rest_4_), channel_id=1, source_target_pairs={{64,80},{97,113},{66,82},{99,115},{68,84},{101,117},{70,86},{103,1... | collective-permute-start | bytes 1228808 | tf_op jit(solution)/shard_map/ppermute | solution.py:429
  148.9 17.0 %collective-permute-start.15 = (bf16[320,640]{1,0:T(8,128)(2,1)}, bf16[320,640]{1,0:T(8,128)(2,1)S(1)}, u32[]{:S(2)}, u32[]{:S(2)}) collective-permute-start(bf16[320,640]{1,0:T(8,128)(2,1)} %shard_map.106.rest_4_), channel_id=1, source_target_pairs={{64,96},{97,65},{66,98},{99,67},{68,100},{101,69},{70,102},{103,71... | collective-permute-start | bytes 1228808 | tf_op jit(solution)/shard_map/ppermute | solution.py:429
  150.9 15.1 %collective-permute-start.16 = (bf16[320,640]{1,0:T(8,128)(2,1)}, bf16[320,640]{1,0:T(8,128)(2,1)S(1)}, u32[]{:S(2)}, u32[]{:S(2)}) collective-permute-start(bf16[320,640]{1,0:T(8,128)(2,1)} %shard_map.106.rest_4_), channel_id=1, source_target_pairs={{64,112},{97,81},{66,114},{99,83},{68,116},{101,85},{70,118},{103,... | collective-permute-start | bytes 1228808 | tf_op jit(solution)/shard_map/ppermute | solution.py:429
  159.1 6.8 %copy-start.7 = (bf16[320,640]{1,0:T(8,128)(2,1)}, bf16[320,640]{1,0:T(8,128)(2,1)S(1)}, u32[]{:S(2)}) copy-start(bf16[320,640]{1,0:T(8,128)(2,1)S(1)} %collective-permute-done.14.rest_5_) | copy-start | bytes 1228804
  166.0 0.8 copy-start.9
  166.0 0.9 copy-start.11
  177.6 7.6 %copy-start.2 = (f32[5120]{0:T(1024)S(1)}, f32[5120]{0:T(1024)}, u32[]{:S(2)}) copy-start(f32[5120]{0:T(1024)} %param.19) | copy-start | bytes 61444
  177.6 1.3 copy-start
  178.9 34.2 %all-to-all-start = ((bf16[16,96,640]{2,1,0:T(8,128)(2,1)}), bf16[16,96,640]{2,1,0:T(8,128)(2,1)}, u32[]{:S(2)}, u32[]{:S(2)}) async-start(bf16[16,96,640]{2,1,0:T(8,128)(2,1)} %shard_map.107), calls=%async_computation | async-start | bytes 3932160 | tf_op jit(solution)/shard_map/all_to_all | solution.py:483

commit v4 on v3

--- a/solution.py
+++ b/solution.py
@@ -14,6 +14,7 @@
 QB = 256
 TB = 512
 FINAL_ROWS = 32
+CUT = 256
 
 coef_first = 3.4445
 coef_second = -4.775
@@ -47,7 +48,8 @@
                 put(j, sources[s][...])
 
 
-def grads_kernel(static, place_ref, x_ref, v_ref, r_ref, *rest):
+def grads_kernel(span, tails, place_ref, x_ref, v_ref, r_ref, *rest):
+    static = span is not None
     n_src = 3 if static else RING
     sources, (own, s1, s2, s3), (acc, wt) = rest[:n_src], rest[n_src : n_src + 4], rest[-2:]
     step = pl.program_id(0)
@@ -60,13 +62,13 @@
 
         if static:
             for j in range(3):
-                put(j, sources[j][...])
+                put(j, sources[j][:, span])
         else:
             pick_weights(place, sources, put)
         acc[...] = jnp.zeros_like(acc)
 
     x = x_ref[...]
-    if static:
+    if tails:
         rest[-4][...] = x
         rest[-3][...] = v_ref[...]
     e = (r_ref[...] * v_ref[...].astype(F32)).astype(BF16)
@@ -89,30 +91,30 @@
             out[...] = acc[jnp.minimum(lax.rem(place + shift, RING), 2)].astype(BF16)
 
 
-def grads(place, xt, vt, rates, sources, static):
+def grads(place, xt, vt, rates, sources, span=None, tails=False):
     width, count = xt.shape
     matrix = sources[0].shape
-    whole = pl.BlockSpec(matrix, lambda i, p: (0, 0))
+    hidden = matrix[1] if span is None else span.stop - span.start
+    part = (width, hidden)
     tokens = pl.BlockSpec((width, TB), lambda i, p: (0, i))
-    hidden = matrix[1]
     steps = count // TB
     rim = WINDOW // TB
-    tails = [pl.BlockSpec((width, TB), lambda i, p: (0, jnp.maximum(i - (steps - rim), 0)))] * 2
+    rims = [pl.BlockSpec((width, TB), lambda i, p: (0, jnp.maximum(i - (steps - rim), 0)))] * 2
     return pl.pallas_call(
-        functools.partial(grads_kernel, static),
+        functools.partial(grads_kernel, span, tails),
         grid_spec=pltpu.PrefetchScalarGridSpec(
             num_scalar_prefetch=1,
             grid=(steps,),
             in_specs=[tokens, tokens, pl.BlockSpec((1, TB), lambda i, p: (0, i))]
-            + [whole] * len(sources),
-            out_specs=[whole] * 4 + (tails if static else []),
+            + [pl.BlockSpec(matrix, lambda i, p: (0, 0))] * len(sources),
+            out_specs=[pl.BlockSpec(part, lambda i, p: (0, 0))] * 4 + (rims if tails else []),
             scratch_shapes=[
-                pltpu.VMEM((3,) + matrix, F32),
+                pltpu.VMEM((3,) + part, F32),
                 pltpu.VMEM((3, hidden, width), BF16),
             ],
         ),
-        out_shape=[jax.ShapeDtypeStruct(matrix, BF16)] * 4
-        + [jax.ShapeDtypeStruct((width, WINDOW), BF16)] * (2 if static else 0),
+        out_shape=[jax.ShapeDtypeStruct(part, BF16)] * 4
+        + [jax.ShapeDtypeStruct((width, WINDOW), BF16)] * (2 if tails else 0),
         compiler_params=params(),
         cost_estimate=pl.CostEstimate(
             flops=12 * width * hidden * count,
@@ -122,16 +124,17 @@
     )(place, xt, vt, rates, *sources)
 
 
-def update_kernel(place_ref, step_ref, own, r1, r2, r3, *rest):
-    olds, out = rest[:-1], rest[-1]
+def update_kernel(place_ref, step_ref, *refs):
+    pieces, olds, outs = refs[: 2 * RING], refs[2 * RING : -2], refs[-2:]
     place = place_ref[0]
     if len(olds) == 3:
         old = jnp.where(
             place == 0, olds[0][...], jnp.where(place == 1, olds[1][...], olds[2][...])
         )
     else:
-        old = olds[0][...]
-    g = own[...].astype(F32) + r1[...].astype(F32) + r2[...].astype(F32) + r3[...].astype(F32)
+        old = jnp.concatenate([olds[0][...], olds[1][...]], 1)
+    sums = [sum(p[...].astype(F32) for p in pieces[i * RING : (i + 1) * RING]) for i in range(2)]
+    g = jnp.concatenate(sums, 1)
     x = g * lax.rsqrt(jnp.sum(g * g) + epsilon)
     rows = g.shape[0]
     diagonal = lax.broadcasted_iota(jnp.int32, (rows, rows), 0) == lax.broadcasted_iota(
@@ -146,22 +149,25 @@
         mix = (coef_second + 2.0 * c * coef_third) * e + coef_third * dot(eb, eb)
         k = coef_first + coef_second * c + coef_third * c * c
         x = k * x + dot(mix.astype(BF16), xb)
-    out[...] = (old.astype(F32) + step_ref[0] * x).astype(BF16)
+    new = (old.astype(F32) + step_ref[0] * x).astype(BF16)
+    outs[0][...] = new[:, :CUT]
+    outs[1][...] = new[:, CUT:]
 
 
 def update(place, step, pieces, olds):
-    matrix = pieces[0].shape
+    rows = pieces[0].shape[0]
+    widths = (CUT, pieces[-1].shape[1])
     smem = pl.BlockSpec(memory_space=pltpu.SMEM)
     vmem = pl.BlockSpec(memory_space=pltpu.VMEM)
     return pl.pallas_call(
         update_kernel,
-        in_specs=[smem, smem] + [vmem] * (4 + len(olds)),
-        out_specs=vmem,
-        out_shape=jax.ShapeDtypeStruct(matrix, BF16),
-        compiler_params=params(),
-        cost_estimate=pl.CostEstimate(
-            flops=5 * 2 * 5 * matrix[0] * matrix[0] * matrix[0],
-            bytes_accessed=16 * matrix[0] * matrix[1],
+        in_specs=[smem, smem] + [vmem] * (len(pieces) + len(olds)),
+        out_specs=[vmem] * 2,
+        out_shape=[jax.ShapeDtypeStruct((rows, w), BF16) for w in widths],
+        compiler_params=params(),
+        cost_estimate=pl.CostEstimate(
+            flops=5 * 2 * 5 * rows * rows * rows,
+            bytes_accessed=16 * rows * sum(widths),
             transcendentals=0,
         ),
     )(place, step, *pieces, *olds)
@@ -295,21 +301,23 @@
 
 
 def apply_kernel(dests, place_ref, part_ref, q_ref, att_ref, *rest):
-    sources, out, (wt, w2) = rest[: 2 * RING], rest[2 * RING], rest[2 * RING + 1 :]
+    sources, out, (wt, w2) = rest[: 4 * RING], rest[4 * RING], rest[4 * RING + 1 :]
+    spans = (slice(0, CUT), slice(CUT, w2.shape[1]))
 
     @pl.when(pl.program_id(0) == 0)
     def _():
-        def put(j, w):
-            if j < 2:
-                wt[j] = w.T
-            else:
-                w2[...] = w
-
         for part in range(2):
-
-            @pl.when(part_ref[0] == part)
-            def _(part=part):
-                pick_weights(place_ref[0], sources[part * RING : (part + 1) * RING], put)
+            for half, span in enumerate(spans):
+
+                def put(j, w, span=span):
+                    if j < 2:
+                        wt[j, span, :] = w.T
+                    else:
+                        w2[:, span] = w
+
+                @pl.when(part_ref[0] == part)
+                def _(begin=(2 * part + half) * RING, put=put):
+                    pick_weights(place_ref[0], sources[begin : begin + RING], put)
 
     q = q_ref[...]
     gate = dot(wt[0], q)
@@ -319,9 +327,9 @@
     pack((fast + att_ref[...]).astype(BF16).T, out, dests)
 
 
-def apply_mix(place, part, qt, att, early, late, parts_out):
+def apply_mix(place, part, qt, att, sources, parts_out):
     width, count = qt.shape
-    matrix = early[0].shape
+    matrix = (width, sources[0].shape[1] + sources[RING].shape[1])
     rows = count // parts_out
     dests = 4
     tokens = pl.BlockSpec((width, dests * rows), lambda i, p, g: (0, i))
@@ -330,7 +338,8 @@
         grid_spec=pltpu.PrefetchScalarGridSpec(
             num_scalar_prefetch=2,
             grid=(parts_out // dests,),
-            in_specs=[tokens, tokens] + [pl.BlockSpec(matrix, lambda i, p, g: (0, 0))] * 8,
+            in_specs=[tokens, tokens]
+            + [pl.BlockSpec(w.shape, lambda i, p, g: (0, 0)) for w in sources],
             out_specs=pl.BlockSpec((dests, rows // 2, 2 * width), lambda i, p, g: (i, 0, 0)),
             scratch_shapes=[
                 pltpu.VMEM((2, matrix[1], width), BF16),
@@ -344,7 +353,7 @@
             bytes_accessed=8 * width * count,
             transcendentals=matrix[1] * count,
         ),
-    )(place, part, qt, att, *early, *late)
+    )(place, part, qt, att, *sources)
 
 
 def gate_kernel(dests, g_ref, out):
@@ -454,32 +463,41 @@
     start = [fast_first[0], fast_third[0], fast_second[0].T]
     hold = lax.optimization_barrier
 
-    own, *out = grads(place, kt, vt, token_rates, start, True)
-    out, tails = out[:3], out[3:]
-    pieces = [own] + [ring_send(o, p) for o, p in zip(out, reduce_moves(0))]
+    hidden = start[0].shape[1]
+
+    own_a, *out_a = grads(place, kt, vt, token_rates, start, slice(0, CUT), True)
+    out_a, tails = out_a[:3], out_a[3:]
+    pieces_a = [own_a] + [ring_send(o, p) for o, p in zip(out_a, reduce_moves(0))]
+    own_a, v_next = hold((own_a, vt))
+    own_b, *out_b = grads(place, kt, v_next, token_rates, start, slice(CUT, hidden))
+    pieces_b = [own_b] + [ring_send(o, p) for o, p in zip(out_b, reduce_moves(0))]
     rim_late = [send(t, [(i, i + 1) for i in range(4, 7)]) for t in tails]
-    att_main = attend_main(qt, kt, vt, first)
-    pieces, att_main = hold((pieces, att_main))
-    fresh = update(place, step_sizes, pieces, start)
+    q_main, own_b = hold((qt, own_b))
+    att_main = attend_main(q_main, kt, vt, first)
+    pieces_a, pieces_b, att_main = hold((pieces_a, pieces_b, att_main))
+    fresh = update(place, step_sizes, pieces_a + pieces_b, start)
     fresh, gt, rim_late = hold((fresh, gt, rim_late))
-    crossed = ring_send(fresh, [(0, m, 1, m) for m in range(3)])
     gates = pack_gate(gt, heads)
-    held = jnp.where(part[0] == 0, fresh, crossed)
-    held, gates = hold((held, gates))
+    crossed = [ring_send(f, [(0, m, 1, m) for m in range(3)]) for f in fresh]
+    held = [jnp.where(part[0] == 0, f, c) for f, c in zip(fresh, crossed)]
+    moves = spread_moves((0, 1))
+    early_a = [held[0]] + [ring_send(held[0], p) for p in moves]
+    early_b = [held[1]] + [ring_send(held[1], p) for p in moves]
+    early_b[0], gates = hold((early_b[0], gates))
     gate_tokens = lax.all_to_all(gates, "head", split_axis=0, concat_axis=0)
-    early = [held] + [ring_send(held, p) for p in spread_moves((0, 1))]
-    early, tails = hold((early, tails))
+
+    own_a, *out_a = grads(place, kt, vt, token_rates, early_a)
+    pieces_a = [own_a] + [ring_send(o, p) for o, p in zip(out_a, reduce_moves(1))]
+    own_a, early_b, tails = hold((own_a, early_b, tails))
     rim_early = [send(t, [(i, i + 1) for i in range(4)]) for t in tails]
-
-    own, *out = grads(place, kt, vt, token_rates, early, False)
-    own, out, att_main = hold((own, out, att_main))
-    pieces = [own] + [ring_send(o, p) for o, p in zip(out, reduce_moves(1))]
+    own_b, *out_b = grads(place, kt, vt, token_rates, early_b)
+    pieces_b = [own_b] + [ring_send(o, p) for o, p in zip(out_b, reduce_moves(1))]
+    fresh = update(place, step_sizes, pieces_a + pieces_b, [early_a[0], early_b[0]])
+    fresh, att_main = hold((fresh, att_main))
+    late = [[f] + [ring_send(f, p) for p in spread_moves((1,))] for f in fresh]
     rims = [jnp.where(ctx <= RING, a, b) for a, b in zip(rim_early, rim_late)]
     att = attend_rim(qt, kt, vt, rims[0], rims[1], att_main, first)
-    pieces, att = hold((pieces, att))
-    fresh = update(place, step_sizes, pieces, [early[0]])
-    late = [fresh] + [ring_send(fresh, p) for p in spread_moves((1,))]
-    mixed = apply_mix(place, part, qt, att, early, late, heads)
+    mixed = apply_mix(place, part, qt, att, early_a + early_b + late[0] + late[1], heads)
     mixed_tokens = lax.all_to_all(mixed, "head", split_axis=0, concat_axis=0)
     return final(mixed_tokens, gate_tokens, norm_gain)
 

time: 220 us -> 244 us (1.11)
  starting transfers between devices: 46.1 us -> 86.5 us
  waiting for transfers between devices: 68.2 us -> 42.4 us
  Pallas kernels: 94.6 us -> 103 us
    ppermute x13 -> x26, starting transfers between devices: 22.4 us -> 60.9 us  [ring_send(): return lax.ppermute(array, ('ctx', 'head'), pairs)]
    ppermute x4, waiting for transfers between devices: 16.4 us -> 0.01 us  [send(): return lax.ppermute(array, 'ctx', pairs)]
    ppermute x13 -> x26, waiting for transfers between devices: 24.7 us -> 15.3 us  [ring_send(): return lax.ppermute(array, ('ctx', 'head'), pairs)]
    pallas_call x4 -> x6, Pallas kernels: 50 us -> 58.6 us  [the longest x4 43.7 us: grads(): pl.pallas_call(functools.partial(grads_kernel, span, tails), grid_spec=pl...]
    all_to_all x1, starting transfers between devices: 6.28 us -> 8.89 us  [shards(): mixed_tokens = lax.all_to_all(mixed, 'head', split_axis=0, concat_axis=0)]
  transfers between devices with their start and end apart: 19 -> 32, of which waited for: 7 -> 5; matrix products, arithmetic and copies ran while one was open for 1% -> 2% of each run, Pallas kernels for 33% -> 37%
where the time goes in v4:
time: 244 us; the launch traced here: 243 us
  Pallas kernels  103 us (42%)
  starting transfers between devices  86.5 us (35%)
  waiting for transfers between devices  42.4 us (17%)
  other arithmetic  5.41 us (2%)
  local copies, waits for them, and re-layouts  3.85 us (2%)
    ppermute x26, starting transfers between devices, ring_send(): return lax.ppermute(array, ('ctx', 'head'), pairs)  60.9 us
    pallas_call x4, Pallas kernels, grads(): pl.pallas_call(functools.partial(grads_kernel, span, tails), grid_spec=pl...  43.7 us
    all_to_all x1, waiting for transfers between devices, shards(): mixed_tokens = lax.all_to_all(mixed, 'head', split_axis=0, concat_axis=0)  27.1 us
    pallas_call x1, Pallas kernels, attend_main(): pl.pallas_call(functools.partial(attend_kernel, blocks, None), grid_spec=...  15.4 us
    ppermute x26, waiting for transfers between devices, ring_send(): return lax.ppermute(array, ('ctx', 'head'), pairs)  15.3 us
    pallas_call x2, Pallas kernels, update(): pl.pallas_call(update_kernel, in_specs=[smem, smem] + [vmem] * (len(piece...  14.8 us
    pallas_call x1, Pallas kernels, apply_mix(): pl.pallas_call(functools.partial(apply_kernel, dests), grid_spec=pltpu.Pr...  10.9 us
    ppermute x4, starting transfers between devices, send(): return lax.ppermute(array, 'ctx', pairs)  9.41 us
  transfers between devices with their start and end apart: 32, of which 5 were waited for; matrix products, arithmetic and copies ran while one was open for 2% of the time, Pallas kernels for 37%

profile of v4, /device:TPU:32, one launch (start us, length us, event | category | flops | bytes accessed | tf_op | source)
XLA Modules:
  0.0 242.8 jit_solution(4984044142205272909)
XLA Ops:
  0.0 9.7 %shard_map.100 = (bf16[320,256]{1,0:T(8,128)(2,1)}, bf16[320,256]{1,0:T(8,128)(2,1)}, bf16[320,256]{1,0:T(8,128)(2,1)}, bf16[320,256]{1,0:T(8,128)(2,1)}, bf16[3...) custom-call(s32[1]{0:T(128)} %bitcast.place_ref, bf16[320,3072]{1,0:T(8,128)(2,1)} %bitcast.14, ...), custom_call_target="tpu_custom_call" | custom-call | flops 3019898880 | bytes 3932160 | tf_op jit(solution)/shard_map/pallas_call | solution.py:103
  9.7 0.7 collective-permute-start
  10.3 0.7 collective-permute-start.1
  11.0 0.7 collective-permute-start.2
  11.7 3.4 %collective-permute-start.6 = (bf16[320,1024]{1,0:T(8,128)(2,1)}, bf16[320,1024]{1,0:T(8,128)(2,1)S(1)}, u32[]{:S(2)}, u32[]{:S(2)}) collective-permute-start(bf16[320,1024]{1,0:T(8,128)(2,1)} %get-tuple-element.81), channel_id=1, source_target_pairs={{64,80},{80,96},{96,112},{65,81},{81,97},{97,113},{66,82},{82,98},... | collective-permute-start | bytes 1966088 | tf_op jit(solution)/shard_map/ppermute | solution.py:442
  15.1 3.4 %collective-permute-start.7 = (bf16[320,1024]{1,0:T(8,128)(2,1)}, bf16[320,1024]{1,0:T(8,128)(2,1)S(1)}, u32[]{:S(2)}, u32[]{:S(2)}) collective-permute-start(bf16[320,1024]{1,0:T(8,128)(2,1)} %get-tuple-element.83), channel_id=1, source_target_pairs={{64,80},{80,96},{96,112},{65,81},{81,97},{97,113},{66,82},{82,98},... | collective-permute-start | bytes 1966088 | tf_op jit(solution)/shard_map/ppermute | solution.py:442
  18.5 12.3 %shard_map.101 = (bf16[320,384]{1,0:T(8,128)(2,1)}, bf16[320,384]{1,0:T(8,128)(2,1)}, bf16[320,384]{1,0:T(8,128)(2,1)}, bf16[320,384]{1,0:T(8,128)(2,1)}) custom-call(s32[1]{0:T(128)} %bitcast.place_ref, bf16[320,3072]{1,0:T(8,128)(2,1)} %bitcast.15, bf16[320,3072]{1,0:T(8,128)(2,1)} %bitcast.21, f32[1,3072]{1,0:T(1,128)} %r_ref.7, ...), custom_call_target="tpu_custom_call" | custom-call | flops 4529848320 | bytes 3932160 | tf_op jit(solution)/shard_map/pallas_call | solution.py:103
  31.5 0.0 collective-permute-done.refs_1_
  31.6 0.7 collective-permute-start.3
  32.3 0.7 collective-permute-start.4
  33.0 0.7 collective-permute-start.5
  33.7 15.4 %shard_map.102.rest_2_ = f32[320,3072]{1,0:T(8,128)} custom-call(s32[1]{0:T(128)} %bitcast.3.first_ref, bf16[320,3072]{1,0:T(8,128)(2,1)} %bitcast.26, bf16[320,3072]{1,0:T(8,128)(2,1)} %bitcast.16, bf16[320,3072]{1,0:T(8,128)(2,1)} %bitcast.22), custom_call_target="tpu_custom_call" | custom-call | flops 3355443200 | bytes 9830400 | tf_op jit(solution)/shard_map/pallas_call | solution.py:250
  49.1 0.7 copy-done.10
  49.7 0.1 copy-done.11
  49.8 0.7 copy-done.12
  50.5 7.5 %shard_map.103 = (bf16[320,256]{1,0:T(8,128)(2,1)}, bf16[320,384]{1,0:T(8,128)(2,1)}) custom-call(s32[1]{0:T(128)} %bitcast.place_ref, f32[1]{0:T(128)S(6)} %copy.13.step_ref, bf16[320,256]{1,0:T(8,128)(2,1)} %get-tuple-element.64.refs_0_, bf16[320,256]{1,0:T(8,128)(2,1)} %copy-done.14, bf16[320,256]{1,0:T(8,128)(2,1)} %copy-done.15, ...), custom_call_target="tpu_custom_call" | custom-call | flops 1638400000 | bytes 3276800 | tf_op jit(solution)/shard_map/pallas_call | solution.py:162
  58.1 1.3 collective-permute-start.8
  59.4 1.3 collective-permute-start.12
  60.7 4.3 %shard_map.105 = bf16[16,96,640]{2,1,0:T(8,128)(2,1)} custom-call(bf16[320,3072]{1,0:T(8,128)(2,1)} %bitcast.13), custom_call_target="tpu_custom_call" | custom-call | bytes 7864320 | tf_op jit(solution)/shard_map/pallas_call | solution.py:367
  65.1 4.4 %collective-permute-done.8 = bf16[320,256]{1,0:T(8,128)(2,1)S(1)} collective-permute-done((bf16[320,256]{1,0:T(8,128)(2,1)}, bf16[320,256]{1,0:T(8,128)(2,1)S(1)}, u32[]{:S(2)}, u32[]{:S(2)}) %collective-permute-start.8) | collective-permute-done | bytes 163872 | tf_op jit(solution)/shard_map/ppermute | solution.py:438
  69.5 0.7 broadcast_select_fusion.3.rest_0_.refs_8_
  70.2 6.6 %collective-permute-start.10 = (bf16[320,256]{1,0:T(8,128)(2,1)}, bf16[320,256]{1,0:T(8,128)(2,1)}, u32[]{:S(2)}, u32[]{:S(2)}) collective-permute-start(bf16[320,256]{1,0:T(8,128)(2,1)} %broadcast_select_fusion.3.rest_0_.refs_8_), channel_id=1, source_target_pairs={{0,32},{33,1},{2,34},{35,3},{4,36},{37,5},{6,38},{39,7},{8,40},{41... | collective-permute-start | bytes 491528 | tf_op jit(solution)/shard_map/ppermute | solution.py:438
  76.8 1.9 collective-permute-start.11
  78.7 4.6 %collective-permute-start.9 = (bf16[320,256]{1,0:T(8,128)(2,1)}, bf16[320,256]{1,0:T(8,128)(2,1)}, u32[]{:S(2)}, u32[]{:S(2)}) collective-permute-start(bf16[320,256]{1,0:T(8,128)(2,1)} %broadcast_select_fusion.3.rest_0_.refs_8_), channel_id=1, source_target_pairs={{0,16},{33,49},{2,18},{35,51},{4,20},{37,53},{6,22},{39,55},{8,24}... | collective-permute-start | bytes 491528 | tf_op jit(solution)/shard_map/ppermute | solution.py:438
  83.3 2.0 collective-permute-start.13
  85.4 1.9 collective-permute-start.14
  87.3 7.3 %all-to-all-start.1 = ((bf16[16,96,640]{2,1,0:T(8,128)(2,1)}), bf16[16,96,640]{2,1,0:T(8,128)(2,1)S(1)}, u32[]{:S(2)}, u32[]{:S(2)}) async-start(bf16[16,96,640]{2,1,0:T(8,128)(2,1)} %shard_map.105), calls=%async_computation.1 | async-start | bytes 3932160 | tf_op jit(solution)/shard_map/all_to_all | solution.py:487
  94.6 2.1 collective-permute-start.15
  96.7 9.2 %shard_map.104 = (bf16[320,256]{1,0:T(8,128)(2,1)}, bf16[320,256]{1,0:T(8,128)(2,1)}, bf16[320,256]{1,0:T(8,128)(2,1)}, bf16[320,256]{1,0:T(8,128)(2,1)}) custom-call(s32[1]{0:T(128)} %bitcast.place_ref, bf16[320,3072]{1,0:T(8,128)(2,1)} %bitcast.17, bf16[320,3072]{1,0:T(8,128)(2,1)} %bitcast.23, f32[1,3072]{1,0:T(1,128)} %r_ref.7, ...), custom_call_target="tpu_custom_call" | custom-call | flops 3019898880 | bytes 3932160 | tf_op jit(solution)/shard_map/pallas_call | solution.py:103
  106.0 3.9 %collective-permute-start.18 = (bf16[320,256]{1,0:T(8,128)(2,1)}, bf16[320,256]{1,0:T(8,128)(2,1)}, u32[]{:S(2)}, u32[]{:S(2)}) collective-permute-start(bf16[320,256]{1,0:T(8,128)(2,1)} %get-tuple-element.85), channel_id=1, source_target_pairs={{112,64},{81,97},{114,66},{83,99},{116,68},{85,101},{118,70},{87,1... | collective-permute-start | bytes 491528 | tf_op jit(solution)/shard_map/ppermute | solution.py:438
  109.9 2.2 collective-permute-start.19
  112.1 1.3 collective-permute-start.20
  113.4 1.3 collective-permute-start.17
  114.7 12.5 %shard_map.106 = (bf16[320,384]{1,0:T(8,128)(2,1)}, bf16[320,384]{1,0:T(8,128)(2,1)}, bf16[320,384]{1,0:T(8,128)(2,1)}, bf16[320,384]{1,0:T(8,128)(2,1)}) custom-call(s32[1]{0:T(128)} %bitcast.place_ref, bf16[320,3072]{1,0:T(8,128)(2,1)} %bitcast.18, bf16[320,3072]{1,0:T(8,128)(2,1)} %bitcast.24, f32[1,3072]{1,0:T(1,128)} %r_ref.7, ...), custom_call_target="tpu_custom_call" | custom-call | flops 4529848320 | bytes 3932160 | tf_op jit(solution)/shard_map/pallas_call | solution.py:103
  127.2 4.7 %collective-permute-start.21 = (bf16[320,384]{1,0:T(8,128)(2,1)}, bf16[320,384]{1,0:T(8,128)(2,1)S(1)}, u32[]{:S(2)}, u32[]{:S(2)}) collective-permute-start(bf16[320,384]{1,0:T(8,128)(2,1)} %get-tuple-element.93), channel_id=1, source_target_pairs={{112,64},{81,97},{114,66},{83,99},{116,68},{85,101},{118,70},{87,1... | collective-permute-start | bytes 737288 | tf_op jit(solution)/shard_map/ppermute | solution.py:438
  131.9 2.6 %collective-permute-start.22 = (bf16[320,384]{1,0:T(8,128)(2,1)}, bf16[320,384]{1,0:T(8,128)(2,1)}, u32[]{:S(2)}, u32[]{:S(2)}) collective-permute-start(bf16[320,384]{1,0:T(8,128)(2,1)} %get-tuple-element.94), channel_id=1, source_target_pairs={{96,64},{65,97},{98,66},{67,99},{100,68},{69,101},{102,70},{71,103... | collective-permute-start | bytes 737288 | tf_op jit(solution)/shard_map/ppermute | solution.py:438
  134.5 1.3 collective-permute-start.23
  135.8 1.3 collective-permute-start.16
  137.1 7.9 %collective-permute-done.21.refs_5_ = bf16[320,384]{1,0:T(8,128)(2,1)S(1)} collective-permute-done((bf16[320,384]{1,0:T(8,128)(2,1)}, bf16[320,384]{1,0:T(8,128)(2,1)S(1)}, u32[]{:S(2)}, u32[]{:S(2)}) %collective-permute-start.21) | collective-permute-done | bytes 245792 | tf_op jit(solution)/shard_map/ppermute | solution.py:438
  145.0 0.6 collective-permute-done.23.refs_7_
  145.5 0.1 copy-done.9
  145.7 7.3 %shard_map.107 = (bf16[320,256]{1,0:T(8,128)(2,1)}, bf16[320,384]{1,0:T(8,128)(2,1)}) custom-call(s32[1]{0:T(128)} %bitcast.place_ref, f32[1]{0:T(128)S(6)} %copy.13.step_ref, bf16[320,256]{1,0:T(8,128)(2,1)} %get-tuple-element.77.refs_0_, bf16[320,256]{1,0:T(8,128)(2,1)} %collective-permute-done.18.refs_1_, ...), custom_call_target="tpu_custom_call" | custom-call | flops 1638400000 | bytes 3276800 | tf_op jit(solution)/shard_map/pallas_call | solution.py:162
  153.0 2.0 collective-permute-start.27
  155.0 5.1 %collective-permute-start.28 = (bf16[320,384]{1,0:T(8,128)(2,1)}, bf16[320,384]{1,0:T(8,128)(2,1)S(1)}, u32[]{:S(2)}, u32[]{:S(2)}) collective-permute-start(bf16[320,384]{1,0:T(8,128)(2,1)} %get-tuple-element.101.rest_12_), channel_id=1, source_target_pairs={{64,96},{97,65},{66,98},{99,67},{68,100},{101,69},{70,102},{103,71... | collective-permute-start | bytes 737288 | tf_op jit(solution)/shard_map/ppermute | solution.py:438
  160.2 1.9 collective-permute-start.29
  162.1 3.9 %collective-permute-start.24 = (bf16[320,256]{1,0:T(8,128)(2,1)}, bf16[320,256]{1,0:T(8,128)(2,1)S(1)}, u32[]{:S(2)}, u32[]{:S(2)}) collective-permute-start(bf16[320,256]{1,0:T(8,128)(2,1)} %get-tuple-element.100.rest_8_), channel_id=1, source_target_pairs={{64,80},{97,113},{66,82},{99,115},{68,84},{101,117},{70,86},{103,1... | collective-permute-start | bytes 491528 | tf_op jit(solution)/shard_map/ppermute | solution.py:438
  166.0 2.0 broadcast_select_fusion.rest_1_
  168.0 2.4 collective-permute-done.24.rest_9_
  170.4 4.0 %collective-permute-start.25 = (bf16[320,256]{1,0:T(8,128)(2,1)S(1)}, bf16[320,256]{1,0:T(8,128)(2,1)S(1)}, u32[]{:S(2)}, u32[]{:S(2)}) collective-permute-start(bf16[320,256]{1,0:T(8,128)(2,1)S(1)} %copy-done.13), channel_id=1, source_target_pairs={{64,96},{97,65},{66,98},{99,67},{68,100},{101,69},{70,102},{103,71... | collective-permute-start | bytes 491528 | tf_op jit(solution)/shard_map/ppermute | solution.py:438
  174.5 2.1 collective-permute-start.26
  176.6 2.0 broadcast_select_fusion.1.rest_0_
  178.6 9.2 %shard_map.108.att_ref = f32[320,3072]{1,0:T(8,128)} custom-call(s32[1]{0:T(128)} %bitcast.3.first_ref, bf16[320,3072]{1,0:T(8,128)(2,1)} %bitcast.27, bf16[320,3072]{1,0:T(8,128)(2,1)} %bitcast.19, bf16[320,3072]{1,0:T(8,128)(2,1)} %bitcast.25, bf16[320,1024]{1,0:T(8,128)(2,1)} %broadcast_select_fusion.1.rest_0_, ...), custom_call_target="tpu_custom_call", output_to_operand_aliasing={{}: (6, {})} | custom-call | flops 1677721600 | bytes 5242880 | tf_op jit(solution)/shard_map/pallas_call | solution.py:274
  187.9 0.6 copy-done.18
  188.5 0.1 copy-done.19
  188.5 0.1 copy-done.6
  188.7 0.1 copy-done.7
  188.7 0.1 copy-done.8
  188.8 10.9 %shard_map.109 = bf16[16,96,640]{2,1,0:T(8,128)(2,1)} custom-call(s32[1]{0:T(128)} %bitcast.place_ref, s32[1]{0:T(128)} %bitcast.1.part_ref, bf16[320,3072]{1,0:T(8,128)(2,1)} %bitcast.28, f32[320,3072]{1,0:T(8,128)} %shard_map.108.att_ref, bf16[320,256]{1,0:T(8,128)(2,1)} %broadcast_select_fusion.3.rest_0_.refs_8_, ...), custom_call_target="tpu_custom_call" | custom-call | flops 3774873600 | bytes 7864320 | tf_op jit(solution)/shard_map/pallas_call | solution.py:336
  199.8 1.3 copy-done
  201.1 8.9 %all-to-all-start = ((bf16[16,96,640]{2,1,0:T(8,128)(2,1)}), bf16[16,96,640]{2,1,0:T(8,128)(2,1)}, u32[]{:S(2)}, u32[]{:S(2)}) async-start(bf16[16,96,640]{2,1,0:T(8,128)(2,1)} %shard_map.109), calls=%async_computation | async-start | bytes 3932160 | tf_op jit(solution)/shard_map/all_to_all | solution.py:501
  210.0 0.1 reshape.17
  210.0 0.7 pad_maximum_fusion.gain_ref
  210.7 27.1 %all-to-all-done.m_ref = bf16[16,96,640]{2,1,0:T(8,128)(2,1)} async-done(((bf16[16,96,640]{2,1,0:T(8,128)(2,1)}), bf16[16,96,640]{2,1,0:T(8,128)(2,1)}, u32[]{:S(2)}, u32[]{:S(2)}) %all-to-all-start) | async-done | bytes 1966112 | tf_op jit(solution)/shard_map/all_to_all | solution.py:501
  237.8 5.0 %shard_map.110 = bf16[2,96,5120]{2,1,0:T(8,128)(2,1)} custom-call(bf16[16,96,640]{2,1,0:T(8,128)(2,1)} %all-to-all-done.m_ref, bf16[16,96,640]{2,1,0:T(8,128)(2,1)} %copy-done, f32[16,640]{1,0:T(8,128)} %pad_maximum_fusion.gain_ref), custom_call_target="tpu_custom_call" | custom-call | flops 9830400 | bytes 5898240 | tf_op jit(solution)/shard_map/pallas_call | solution.py:409
  (57 shorter events, 0.2 us)
Async XLA Ops:
  9.7 21.9 %collective-permute-start = (bf16[320,256]{1,0:T(8,128)(2,1)}, bf16[320,256]{1,0:T(8,128)(2,1)S(1)}, u32[]{:S(2)}, u32[]{:S(2)}) collective-permute-start(bf16[320,256]{1,0:T(8,128)(2,1)} %get-tuple-element.55), channel_id=1, source_target_pairs={{48,0},{17,33},{50,2},{19,35},{52,4},{21,37},{54,6},{23,39},{56,8}... | collective-permute-start | bytes 491528 | tf_op jit(solution)/shard_map/ppermute | solution.py:438
  10.3 21.9 %collective-permute-start.1 = (bf16[320,256]{1,0:T(8,128)(2,1)}, bf16[320,256]{1,0:T(8,128)(2,1)S(1)}, u32[]{:S(2)}, u32[]{:S(2)}) collective-permute-start(bf16[320,256]{1,0:T(8,128)(2,1)} %get-tuple-element.56), channel_id=1, source_target_pairs={{32,0},{1,33},{34,2},{3,35},{36,4},{5,37},{38,6},{7,39},{40,8},{9,... | collective-permute-start | bytes 491528 | tf_op jit(solution)/shard_map/ppermute | solution.py:438
  11.0 21.9 %collective-permute-start.2 = (bf16[320,256]{1,0:T(8,128)(2,1)}, bf16[320,256]{1,0:T(8,128)(2,1)S(1)}, u32[]{:S(2)}, u32[]{:S(2)}) collective-permute-start(bf16[320,256]{1,0:T(8,128)(2,1)} %get-tuple-element.57), channel_id=1, source_target_pairs={{16,0},{49,33},{18,2},{51,35},{20,4},{53,37},{22,6},{55,39},{24,8}... | collective-permute-start | bytes 491528 | tf_op jit(solution)/shard_map/ppermute | solution.py:438
  11.7 46.4 %collective-permute-start.6 = (bf16[320,1024]{1,0:T(8,128)(2,1)}, bf16[320,1024]{1,0:T(8,128)(2,1)S(1)}, u32[]{:S(2)}, u32[]{:S(2)}) collective-permute-start(bf16[320,1024]{1,0:T(8,128)(2,1)} %get-tuple-element.81), channel_id=1, source_target_pairs={{64,80},{80,96},{96,112},{65,81},{81,97},{97,113},{66,82},{82,98},... | collective-permute-start | bytes 1966088 | tf_op jit(solution)/shard_map/ppermute | solution.py:442
  15.1 42.9 %collective-permute-start.7 = (bf16[320,1024]{1,0:T(8,128)(2,1)}, bf16[320,1024]{1,0:T(8,128)(2,1)S(1)}, u32[]{:S(2)}, u32[]{:S(2)}) collective-permute-start(bf16[320,1024]{1,0:T(8,128)(2,1)} %get-tuple-element.83), channel_id=1, source_target_pairs={{64,80},{80,96},{96,112},{65,81},{81,97},{97,113},{66,82},{82,98},... | collective-permute-start | bytes 1966088 | tf_op jit(solution)/shard_map/ppermute | solution.py:442
  31.6 17.5 %copy-start.14 = (bf16[320,256]{1,0:T(8,128)(2,1)}, bf16[320,256]{1,0:T(8,128)(2,1)S(1)}, u32[]{:S(2)}) copy-start(bf16[320,256]{1,0:T(8,128)(2,1)S(1)} %collective-permute-done.refs_1_) | copy-start | bytes 491524
  31.6 17.5 %collective-permute-start.3 = (bf16[320,384]{1,0:T(8,128)(2,1)}, bf16[320,384]{1,0:T(8,128)(2,1)S(1)}, u32[]{:S(2)}, u32[]{:S(2)}) collective-permute-start(bf16[320,384]{1,0:T(8,128)(2,1)} %get-tuple-element.60), channel_id=1, source_target_pairs={{48,0},{17,33},{50,2},{19,35},{52,4},{21,37},{54,6},{23,39},{56,8}... | collective-permute-start | bytes 737288 | tf_op jit(solution)/shard_map/ppermute | solution.py:438
  32.3 16.8 %copy-start.15 = (bf16[320,256]{1,0:T(8,128)(2,1)}, bf16[320,256]{1,0:T(8,128)(2,1)S(1)}, u32[]{:S(2)}) copy-start(bf16[320,256]{1,0:T(8,128)(2,1)S(1)} %collective-permute-done.1.refs_2_) | copy-start | bytes 491524
  32.3 16.8 %collective-permute-start.4 = (bf16[320,384]{1,0:T(8,128)(2,1)}, bf16[320,384]{1,0:T(8,128)(2,1)S(1)}, u32[]{:S(2)}, u32[]{:S(2)}) collective-permute-start(bf16[320,384]{1,0:T(8,128)(2,1)} %get-tuple-element.61), channel_id=1, source_target_pairs={{32,0},{1,33},{34,2},{3,35},{36,4},{5,37},{38,6},{7,39},{40,8},{9,... | collective-permute-start | bytes 737288 | tf_op jit(solution)/shard_map/ppermute | solution.py:438
  33.0 16.1 %copy-start.16 = (bf16[320,256]{1,0:T(8,128)(2,1)}, bf16[320,256]{1,0:T(8,128)(2,1)S(1)}, u32[]{:S(2)}) copy-start(bf16[320,256]{1,0:T(8,128)(2,1)S(1)} %collective-permute-done.2.refs_3_) | copy-start | bytes 491524
  33.0 16.1 %collective-permute-start.5 = (bf16[320,384]{1,0:T(8,128)(2,1)}, bf16[320,384]{1,0:T(8,128)(2,1)S(1)}, u32[]{:S(2)}, u32[]{:S(2)}) collective-permute-start(bf16[320,384]{1,0:T(8,128)(2,1)} %get-tuple-element.62), channel_id=1, source_target_pairs={{16,0},{49,33},{18,2},{51,35},{20,4},{53,37},{22,6},{55,39},{24,8}... | collective-permute-start | bytes 737288 | tf_op jit(solution)/shard_map/ppermute | solution.py:438
  49.0 0.7 copy-start.10
  49.1 0.8 copy-start.11
  49.8 0.7 copy-start.12
  58.1 11.4 %collective-permute-start.8 = (bf16[320,256]{1,0:T(8,128)(2,1)}, bf16[320,256]{1,0:T(8,128)(2,1)S(1)}, u32[]{:S(2)}, u32[]{:S(2)}) collective-permute-start(bf16[320,256]{1,0:T(8,128)(2,1)} %get-tuple-element.76), channel_id=1, source_target_pairs={{0,64},{33,97},{2,66},{35,99},{4,68},{37,101},{6,70},{39,103},{8,7... | collective-permute-start | bytes 491528 | tf_op jit(solution)/shard_map/ppermute | solution.py:438
  59.4 23.9 %collective-permute-start.12 = (bf16[320,384]{1,0:T(8,128)(2,1)}, bf16[320,384]{1,0:T(8,128)(2,1)S(1)}, u32[]{:S(2)}, u32[]{:S(2)}) collective-permute-start(bf16[320,384]{1,0:T(8,128)(2,1)} %get-tuple-element.78), channel_id=1, source_target_pairs={{0,64},{33,97},{2,66},{35,99},{4,68},{37,101},{6,70},{39,103},{8,7... | collective-permute-start | bytes 737288 | tf_op jit(solution)/shard_map/ppermute | solution.py:438
  60.7 8.8 %copy-start.3 = (bf16[320,256]{1,0:T(8,128)(2,1)S(1)}, bf16[320,256]{1,0:T(8,128)(2,1)}, u32[]{:S(2)}) copy-start(bf16[320,256]{1,0:T(8,128)(2,1)} %get-tuple-element.76) | copy-start | bytes 491524
  60.7 22.6 %copy-start.2 = (bf16[320,384]{1,0:T(8,128)(2,1)S(1)}, bf16[320,384]{1,0:T(8,128)(2,1)}, u32[]{:S(2)}) copy-start(bf16[320,384]{1,0:T(8,128)(2,1)} %get-tuple-element.78) | copy-start | bytes 737284
  70.2 24.4 %collective-permute-start.10 = (bf16[320,256]{1,0:T(8,128)(2,1)}, bf16[320,256]{1,0:T(8,128)(2,1)}, u32[]{:S(2)}, u32[]{:S(2)}) collective-permute-start(bf16[320,256]{1,0:T(8,128)(2,1)} %broadcast_select_fusion.3.rest_0_.refs_8_), channel_id=1, source_target_pairs={{0,32},{33,1},{2,34},{35,3},{4,36},{37,5},{6,38},{39,7},{8,40},{41... | collective-permute-start | bytes 491528 | tf_op jit(solution)/shard_map/ppermute | solution.py:438
  76.8 19.9 %collective-permute-start.11 = (bf16[320,256]{1,0:T(8,128)(2,1)}, bf16[320,256]{1,0:T(8,128)(2,1)}, u32[]{:S(2)}, u32[]{:S(2)}) collective-permute-start(bf16[320,256]{1,0:T(8,128)(2,1)} %broadcast_select_fusion.3.rest_0_.refs_8_), channel_id=1, source_target_pairs={{0,48},{33,17},{2,50},{35,19},{4,52},{37,21},{6,54},{39,23},{8,56}... | collective-permute-start | bytes 491528 | tf_op jit(solution)/shard_map/ppermute | solution.py:438
  78.7 18.0 %collective-permute-start.9 = (bf16[320,256]{1,0:T(8,128)(2,1)}, bf16[320,256]{1,0:T(8,128)(2,1)}, u32[]{:S(2)}, u32[]{:S(2)}) collective-permute-start(bf16[320,256]{1,0:T(8,128)(2,1)} %broadcast_select_fusion.3.rest_0_.refs_8_), channel_id=1, source_target_pairs={{0,16},{33,49},{2,18},{35,51},{4,20},{37,53},{6,22},{39,55},{8,24}... | collective-permute-start | bytes 491528 | tf_op jit(solution)/shard_map/ppermute | solution.py:438
  83.3 11.3 %copy-start.1 = (bf16[320,384]{1,0:T(8,128)(2,1)}, bf16[320,384]{1,0:T(8,128)(2,1)S(1)}, u32[]{:S(2)}) copy-start(bf16[320,384]{1,0:T(8,128)(2,1)S(1)} %broadcast_select_fusion.2.rest_0_.refs_9_.rest_4_) | copy-start | bytes 737284
  83.3 28.7 %collective-permute-start.13 = (bf16[320,384]{1,0:T(8,128)(2,1)S(1)}, bf16[320,384]{1,0:T(8,128)(2,1)}, u32[]{:S(2)}, u32[]{:S(2)}) collective-permute-start(bf16[320,384]{1,0:T(8,128)(2,1)S(1)} %broadcast_select_fusion.2.rest_0_.refs_9_.rest_4_), channel_id=1, source_target_pairs={{0,16},{33,49},{2,18},{35,51},{4,20},{37,53},{6,22},{39,55},{8,24}... | collective-permute-start | bytes 737288 | tf_op jit(solution)/shard_map/ppermute | solution.py:438
  85.4 28.0 %collective-permute-start.14 = (bf16[320,384]{1,0:T(8,128)(2,1)S(1)}, bf16[320,384]{1,0:T(8,128)(2,1)}, u32[]{:S(2)}, u32[]{:S(2)}) collective-permute-start(bf16[320,384]{1,0:T(8,128)(2,1)S(1)} %broadcast_select_fusion.2.rest_0_.refs_9_.rest_4_), channel_id=1, source_target_pairs={{0,32},{33,1},{2,34},{35,3},{4,36},{37,5},{6,38},{39,7},{8,40},{41... | collective-permute-start | bytes 737288 | tf_op jit(solution)/shard_map/ppermute | solution.py:438
  87.3 112.5 %all-to-all-start.1 = ((bf16[16,96,640]{2,1,0:T(8,128)(2,1)}), bf16[16,96,640]{2,1,0:T(8,128)(2,1)S(1)}, u32[]{:S(2)}, u32[]{:S(2)}) async-start(bf16[16,96,640]{2,1,0:T(8,128)(2,1)} %shard_map.105), calls=%async_computation.1 | async-start | bytes 3932160 | tf_op jit(solution)/shard_map/all_to_all | solution.py:487
  94.6 18.8 %collective-permute-start.15 = (bf16[320,384]{1,0:T(8,128)(2,1)S(1)}, bf16[320,384]{1,0:T(8,128)(2,1)S(1)}, u32[]{:S(2)}, u32[]{:S(2)}) collective-permute-start(bf16[320,384]{1,0:T(8,128)(2,1)S(1)} %broadcast_select_fusion.2.rest_0_.refs_9_.rest_4_), channel_id=1, source_target_pairs={{0,48},{33,17},{2,50},{35,19},{4,52},{37,21},{6,54},{39,23},{8,56}... | collective-permute-start | bytes 737288 | tf_op jit(solution)/shard_map/ppermute | solution.py:438
  106.0 25.9 %collective-permute-start.18 = (bf16[320,256]{1,0:T(8,128)(2,1)}, bf16[320,256]{1,0:T(8,128)(2,1)}, u32[]{:S(2)}, u32[]{:S(2)}) collective-permute-start(bf16[320,256]{1,0:T(8,128)(2,1)} %get-tuple-element.85), channel_id=1, source_target_pairs={{112,64},{81,97},{114,66},{83,99},{116,68},{85,101},{118,70},{87,1... | collective-permute-start | bytes 491528 | tf_op jit(solution)/shard_map/ppermute | solution.py:438
  109.9 24.6 %collective-permute-start.19 = (bf16[320,256]{1,0:T(8,128)(2,1)}, bf16[320,256]{1,0:T(8,128)(2,1)}, u32[]{:S(2)}, u32[]{:S(2)}) collective-permute-start(bf16[320,256]{1,0:T(8,128)(2,1)} %get-tuple-element.86), channel_id=1, source_target_pairs={{96,64},{65,97},{98,66},{67,99},{100,68},{69,101},{102,70},{71,103... | collective-permute-start | bytes 491528 | tf_op jit(solution)/shard_map/ppermute | solution.py:438
  112.1 23.7 %collective-permute-start.20 = (bf16[320,256]{1,0:T(8,128)(2,1)}, bf16[320,256]{1,0:T(8,128)(2,1)}, u32[]{:S(2)}, u32[]{:S(2)}) collective-permute-start(bf16[320,256]{1,0:T(8,128)(2,1)} %get-tuple-element.87), channel_id=1, source_target_pairs={{80,64},{113,97},{82,66},{115,99},{84,68},{117,101},{86,70},{119,1... | collective-permute-start | bytes 491528 | tf_op jit(solution)/shard_map/ppermute | solution.py:438
  113.4 1.3 copy-start.5
  113.4 48.7 %collective-permute-start.17 = (bf16[320,1024]{1,0:T(8,128)(2,1)}, bf16[320,1024]{1,0:T(8,128)(2,1)}, u32[]{:S(2)}, u32[]{:S(2)}) collective-permute-start(bf16[320,1024]{1,0:T(8,128)(2,1)} %get-tuple-element.83), channel_id=1, source_target_pairs={{0,16},{16,32},{32,48},{48,64},{1,17},{17,33},{33,49},{49,65},{2,1... | collective-permute-start | bytes 1966088 | tf_op jit(solution)/shard_map/ppermute | solution.py:442
  127.2 17.8 %collective-permute-start.21 = (bf16[320,384]{1,0:T(8,128)(2,1)}, bf16[320,384]{1,0:T(8,128)(2,1)S(1)}, u32[]{:S(2)}, u32[]{:S(2)}) collective-permute-start(bf16[320,384]{1,0:T(8,128)(2,1)} %get-tuple-element.93), channel_id=1, source_target_pairs={{112,64},{81,97},{114,66},{83,99},{116,68},{85,101},{118,70},{87,1... | collective-permute-start | bytes 737288 | tf_op jit(solution)/shard_map/ppermute | solution.py:438
  131.9 13.1 %collective-permute-start.22 = (bf16[320,384]{1,0:T(8,128)(2,1)}, bf16[320,384]{1,0:T(8,128)(2,1)}, u32[]{:S(2)}, u32[]{:S(2)}) collective-permute-start(bf16[320,384]{1,0:T(8,128)(2,1)} %get-tuple-element.94), channel_id=1, source_target_pairs={{96,64},{65,97},{98,66},{67,99},{100,68},{69,101},{102,70},{71,103... | collective-permute-start | bytes 737288 | tf_op jit(solution)/shard_map/ppermute | solution.py:438
  134.5 11.1 %collective-permute-start.23 = (bf16[320,384]{1,0:T(8,128)(2,1)}, bf16[320,384]{1,0:T(8,128)(2,1)}, u32[]{:S(2)}, u32[]{:S(2)}) collective-permute-start(bf16[320,384]{1,0:T(8,128)(2,1)} %get-tuple-element.95), channel_id=1, source_target_pairs={{80,64},{113,97},{82,66},{115,99},{84,68},{117,101},{86,70},{119,1... | collective-permute-start | bytes 737288 | tf_op jit(solution)/shard_map/ppermute | solution.py:438
  135.8 38.7 %collective-permute-start.16 = (bf16[320,1024]{1,0:T(8,128)(2,1)}, bf16[320,1024]{1,0:T(8,128)(2,1)}, u32[]{:S(2)}, u32[]{:S(2)}) collective-permute-start(bf16[320,1024]{1,0:T(8,128)(2,1)} %get-tuple-element.81), channel_id=1, source_target_pairs={{0,16},{16,32},{32,48},{48,64},{1,17},{17,33},{33,49},{49,65},{2,1... | collective-permute-start | bytes 1966088 | tf_op jit(solution)/shard_map/ppermute | solution.py:442
  145.0 0.7 copy-start.9
  153.0 17.5 %copy-start.13 = (bf16[320,256]{1,0:T(8,128)(2,1)S(1)}, bf16[320,256]{1,0:T(8,128)(2,1)}, u32[]{:S(2)}) copy-start(bf16[320,256]{1,0:T(8,128)(2,1)} %get-tuple-element.100.rest_8_) | copy-start | bytes 491524
  153.0 34.9 %collective-permute-start.27 = (bf16[320,384]{1,0:T(8,128)(2,1)}, bf16[320,384]{1,0:T(8,128)(2,1)S(1)}, u32[]{:S(2)}, u32[]{:S(2)}) collective-permute-start(bf16[320,384]{1,0:T(8,128)(2,1)} %get-tuple-element.101.rest_12_), channel_id=1, source_target_pairs={{64,80},{97,113},{66,82},{99,115},{68,84},{101,117},{70,86},{103,1... | collective-permute-start | bytes 737288 | tf_op jit(solution)/shard_map/ppermute | solution.py:438
  155.0 32.9 %collective-permute-start.28 = (bf16[320,384]{1,0:T(8,128)(2,1)}, bf16[320,384]{1,0:T(8,128)(2,1)S(1)}, u32[]{:S(2)}, u32[]{:S(2)}) collective-permute-start(bf16[320,384]{1,0:T(8,128)(2,1)} %get-tuple-element.101.rest_12_), channel_id=1, source_target_pairs={{64,96},{97,65},{66,98},{99,67},{68,100},{101,69},{70,102},{103,71... | collective-permute-start | bytes 737288 | tf_op jit(solution)/shard_map/ppermute | solution.py:438
  160.2 27.7 %collective-permute-start.29 = (bf16[320,384]{1,0:T(8,128)(2,1)}, bf16[320,384]{1,0:T(8,128)(2,1)S(1)}, u32[]{:S(2)}, u32[]{:S(2)}) collective-permute-start(bf16[320,384]{1,0:T(8,128)(2,1)} %get-tuple-element.101.rest_12_), channel_id=1, source_target_pairs={{64,112},{97,81},{66,114},{99,83},{68,116},{101,85},{70,118},{103,... | collective-permute-start | bytes 737288 | tf_op jit(solution)/shard_map/ppermute | solution.py:438
  162.1 8.3 %collective-permute-start.24 = (bf16[320,256]{1,0:T(8,128)(2,1)}, bf16[320,256]{1,0:T(8,128)(2,1)S(1)}, u32[]{:S(2)}, u32[]{:S(2)}) collective-permute-start(bf16[320,256]{1,0:T(8,128)(2,1)} %get-tuple-element.100.rest_8_), channel_id=1, source_target_pairs={{64,80},{97,113},{66,82},{99,115},{68,84},{101,117},{70,86},{103,1... | collective-permute-start | bytes 491528 | tf_op jit(solution)/shard_map/ppermute | solution.py:438
  170.4 17.4 %copy-start.17 = (bf16[320,256]{1,0:T(8,128)(2,1)}, bf16[320,256]{1,0:T(8,128)(2,1)S(1)}, u32[]{:S(2)}) copy-start(bf16[320,256]{1,0:T(8,128)(2,1)S(1)} %collective-permute-done.24.rest_9_) | copy-start | bytes 491524
  170.4 17.4 %collective-permute-start.25 = (bf16[320,256]{1,0:T(8,128)(2,1)S(1)}, bf16[320,256]{1,0:T(8,128)(2,1)S(1)}, u32[]{:S(2)}, u32[]{:S(2)}) collective-permute-start(bf16[320,256]{1,0:T(8,128)(2,1)S(1)} %copy-done.13), channel_id=1, source_target_pairs={{64,96},{97,65},{66,98},{99,67},{68,100},{101,69},{70,102},{103,71... | collective-permute-start | bytes 491528 | tf_op jit(solution)/shard_map/ppermute | solution.py:438
  174.5 13.4 %collective-permute-start.26 = (bf16[320,256]{1,0:T(8,128)(2,1)S(1)}, bf16[320,256]{1,0:T(8,128)(2,1)S(1)}, u32[]{:S(2)}, u32[]{:S(2)}) collective-permute-start(bf16[320,256]{1,0:T(8,128)(2,1)S(1)} %copy-done.13), channel_id=1, source_target_pairs={{64,112},{97,81},{66,114},{99,83},{68,116},{101,85},{70,118},{103,... | collective-permute-start | bytes 491528 | tf_op jit(solution)/shard_map/ppermute | solution.py:438
  187.8 0.7 copy-start.18
  187.8 0.7 copy-start.19
  187.9 0.8 copy-start.6
  187.9 0.9 copy-start.7
  187.9 0.9 copy-start.8
  199.7 10.2 %copy-start.4 = (f32[5120]{0:T(1024)S(1)}, f32[5120]{0:T(1024)}, u32[]{:S(2)}) copy-start(f32[5120]{0:T(1024)} %param.19) | copy-start | bytes 61444
  199.8 1.3 copy-start
  201.1 36.8 %all-to-all-start = ((bf16[16,96,640]{2,1,0:T(8,128)(2,1)}), bf16[16,96,640]{2,1,0:T(8,128)(2,1)}, u32[]{:S(2)}, u32[]{:S(2)}) async-start(bf16[16,96,640]{2,1,0:T(8,128)(2,1)} %shard_map.109), calls=%async_computation | async-start | bytes 3932160 | tf_op jit(solution)/shard_map/all_to_all | solution.py:501

commit v5 on v3

--- a/solution.py
+++ b/solution.py
@@ -12,7 +12,8 @@
 WINDOW = 1024
 RING = 4
 QB = 256
-TB = 512
+TB = 1536
+SB = 512
 FINAL_ROWS = 32
 
 coef_first = 3.4445
@@ -49,14 +50,17 @@
 
 def grads_kernel(static, place_ref, x_ref, v_ref, r_ref, *rest):
     n_src = 3 if static else RING
-    sources, (own, s1, s2, s3), (acc, wt) = rest[:n_src], rest[n_src : n_src + 4], rest[-2:]
+    sources, outs, rest = rest[:n_src], rest[n_src : n_src + 4], rest[n_src + 4 :]
+    acc, wt, d_gate, d_up, hidden, scaled = rest[-6:]
     step = pl.program_id(0)
+    last = pl.num_programs(0) - 1
     place = place_ref[0]
+    width, count = x_ref.shape
 
     @pl.when(step == 0)
     def _():
         def put(j, w):
-            wt[j] = w.T
+            wt[j] = (w * 0.5 if j == 0 else w).T
 
         if static:
             for j in range(3):
@@ -65,28 +69,43 @@
             pick_weights(place, sources, put)
         acc[...] = jnp.zeros_like(acc)
 
-    x = x_ref[...]
-    if static:
-        rest[-4][...] = x
-        rest[-3][...] = v_ref[...]
-    e = (r_ref[...] * v_ref[...].astype(F32)).astype(BF16)
-    gate = dot(wt[0], x)
-    up = dot(wt[1], x)
-    back = dot(wt[2], e)
-    sig = sigmoid(gate)
-    gated = gate * sig
-    hidden = (gated * up).astype(BF16)
-    d_gate = (back * up * (sig + gated * (1.0 - sig))).astype(BF16)
-    d_up = (back * gated).astype(BF16)
-    nt = ((1,), (1,))
-    acc[0] += dot(x, d_gate, nt)
-    acc[1] += dot(x, d_up, nt)
-    acc[2] += dot(e, hidden, nt)
-
-    @pl.when(step == pl.num_programs(0) - 1)
+    def forward(span):
+        x = x_ref[:, span]
+        e = (r_ref[:, span] * v_ref[:, span].astype(F32)).astype(BF16)
+        scaled[:, span] = e
+        half = dot(wt[0], x)
+        up = dot(wt[1], x)
+        back = dot(wt[2], e)
+        both = 1.0 + jnp.tanh(half)
+        gated = half * both
+        slope = both * (half + half + 1.0 - gated)
+        hidden[:, span] = (gated * up).astype(BF16)
+        d_up[:, span] = (back * gated).astype(BF16)
+        d_gate[:, span] = (back * up * slope).astype(BF16)
+
+    def backward(span):
+        nt = ((1,), (1,))
+        x = x_ref[:, span]
+        acc[0] += dot(x, d_gate[:, span], nt)
+        acc[1] += dot(x, d_up[:, span], nt)
+        acc[2] += dot(scaled[:, span], hidden[:, span], nt)
+
+    spans = [slice(b, b + SB) for b in range(0, count, SB)]
+    for i, span in enumerate(spans):
+        forward(span)
+        if i:
+            backward(spans[i - 1])
+    backward(spans[-1])
+
+    @pl.when(step == last)
     def _():
-        for shift, out in enumerate((own, s1, s2, s3)):
-            out[...] = acc[jnp.minimum(lax.rem(place + shift, RING), 2)].astype(BF16)
+        if static:
+            rim = slice(count - WINDOW, count)
+            rest[0][:width] = x_ref[:, rim]
+            rest[0][width:] = v_ref[:, rim]
+        for shift, out in enumerate(outs):
+            j = jnp.minimum(lax.rem(place + shift, RING), 2)
+            out[...] = (acc[j] * jnp.where(j == 0, 0.5, 1.0)).astype(BF16)
 
 
 def grads(place, xt, vt, rates, sources, static):
@@ -95,24 +114,24 @@
     whole = pl.BlockSpec(matrix, lambda i, p: (0, 0))
     tokens = pl.BlockSpec((width, TB), lambda i, p: (0, i))
     hidden = matrix[1]
-    steps = count // TB
-    rim = WINDOW // TB
-    tails = [pl.BlockSpec((width, TB), lambda i, p: (0, jnp.maximum(i - (steps - rim), 0)))] * 2
+    rim = (2 * width, WINDOW)
     return pl.pallas_call(
         functools.partial(grads_kernel, static),
         grid_spec=pltpu.PrefetchScalarGridSpec(
             num_scalar_prefetch=1,
-            grid=(steps,),
+            grid=(count // TB,),
             in_specs=[tokens, tokens, pl.BlockSpec((1, TB), lambda i, p: (0, i))]
             + [whole] * len(sources),
-            out_specs=[whole] * 4 + (tails if static else []),
+            out_specs=[whole] * 4 + ([pl.BlockSpec(rim, lambda i, p: (0, 0))] if static else []),
             scratch_shapes=[
                 pltpu.VMEM((3,) + matrix, F32),
                 pltpu.VMEM((3, hidden, width), BF16),
-            ],
+            ]
+            + [pltpu.VMEM((hidden, TB), BF16)] * 3
+            + [pltpu.VMEM((width, TB), BF16)],
         ),
         out_shape=[jax.ShapeDtypeStruct(matrix, BF16)] * 4
-        + [jax.ShapeDtypeStruct((width, WINDOW), BF16)] * (2 if static else 0),
+        + ([jax.ShapeDtypeStruct(rim, BF16)] if static else []),
         compiler_params=params(),
         cost_estimate=pl.CostEstimate(
             flops=12 * width * hidden * count,
@@ -172,8 +191,9 @@
         (out, k_nat) = rest
         rims = ()
     else:
-        (rim_k, rim_v, _, out, k_nat) = rest
-        rims = (rim_k, rim_v)
+        (rim, _, out, k_nat) = rest
+        width = q_ref.shape[0]
+        rims = (rim.at[:width], rim.at[width:])
     step = pl.program_id(0)
     heads = q_ref.shape[0] // ATT_DIM
     chunks = WINDOW // QB + 1
@@ -260,7 +280,7 @@
     )(first, qt, kt, vt)
 
 
-def attend_rim(qt, kt, vt, rim_k, rim_v, main, first):
+def attend_rim(qt, kt, vt, rim, main, first):
     width = qt.shape[0]
     blocks = WINDOW // QB
     heads = width // ATT_DIM
@@ -270,20 +290,23 @@
         grid_spec=pltpu.PrefetchScalarGridSpec(
             num_scalar_prefetch=1,
             grid=(blocks,),
-            in_specs=[pl.BlockSpec((width, QB), lambda i, f: (0, i))] + [whole] * 4
-            + [pl.BlockSpec(memory_space=pl.ANY)],
+            in_specs=[pl.BlockSpec((width, QB), lambda i, f: (0, i))] + [whole] * 2
+            + [
+                pl.BlockSpec(rim.shape, lambda i, f: (0, 0)),
+                pl.BlockSpec(memory_space=pl.ANY),
+            ],
             out_specs=pl.BlockSpec((width, QB), lambda i, f: (0, i)),
             scratch_shapes=[pltpu.VMEM((heads, 2 * WINDOW, ATT_DIM), BF16)],
         ),
         out_shape=jax.ShapeDtypeStruct(main.shape, F32),
-        input_output_aliases={6: 0},
+        input_output_aliases={5: 0},
         compiler_params=params(),
         cost_estimate=pl.CostEstimate(
             flops=4 * blocks * QB * (WINDOW + QB) * width,
             bytes_accessed=16 * width * WINDOW,
             transcendentals=blocks * QB * (WINDOW + QB) * heads,
         ),
-    )(first, qt, kt, vt, rim_k, rim_v, main)
+    )(first, qt, kt, vt, rim, main)
 
 
 def pack(rows, out, dests):
@@ -301,7 +324,7 @@
     def _():
         def put(j, w):
             if j < 2:
-                wt[j] = w.T
+                wt[j] = (w * 0.5 if j == 0 else w).T
             else:
                 w2[...] = w
 
@@ -312,9 +335,9 @@
                 pick_weights(place_ref[0], sources[part * RING : (part + 1) * RING], put)
 
     q = q_ref[...]
-    gate = dot(wt[0], q)
+    half = dot(wt[0], q)
     up = dot(wt[1], q)
-    hidden = (gate * sigmoid(gate) * up).astype(BF16)
+    hidden = (half * (1.0 + jnp.tanh(half)) * up).astype(BF16)
     fast = dot(w2[...], hidden)
     pack((fast + att_ref[...]).astype(BF16).T, out, dests)
 
@@ -455,9 +478,9 @@
     hold = lax.optimization_barrier
 
     own, *out = grads(place, kt, vt, token_rates, start, True)
-    out, tails = out[:3], out[3:]
+    out, tail = out[:3], out[3]
     pieces = [own] + [ring_send(o, p) for o, p in zip(out, reduce_moves(0))]
-    rim_late = [send(t, [(i, i + 1) for i in range(4, 7)]) for t in tails]
+    rim_late = send(tail, [(i, i + 1) for i in range(4, 7)])
     att_main = attend_main(qt, kt, vt, first)
     pieces, att_main = hold((pieces, att_main))
     fresh = update(place, step_sizes, pieces, start)
@@ -468,17 +491,15 @@
     held, gates = hold((held, gates))
     gate_tokens = lax.all_to_all(gates, "head", split_axis=0, concat_axis=0)
     early = [held] + [ring_send(held, p) for p in spread_moves((0, 1))]
-    early, tails = hold((early, tails))
-    rim_early = [send(t, [(i, i + 1) for i in range(4)]) for t in tails]
+    early[1], tail = hold((early[1], tail))
+    rim_early = send(tail, [(i, i + 1) for i in range(4)])
 
     own, *out = grads(place, kt, vt, token_rates, early, False)
-    own, out, att_main = hold((own, out, att_main))
     pieces = [own] + [ring_send(o, p) for o, p in zip(out, reduce_moves(1))]
-    rims = [jnp.where(ctx <= RING, a, b) for a, b in zip(rim_early, rim_late)]
-    att = attend_rim(qt, kt, vt, rims[0], rims[1], att_main, first)
-    pieces, att = hold((pieces, att))
     fresh = update(place, step_sizes, pieces, [early[0]])
+    fresh, att_main = hold((fresh, att_main))
     late = [fresh] + [ring_send(fresh, p) for p in spread_moves((1,))]
+    att = attend_rim(qt, kt, vt, jnp.where(ctx <= RING, rim_early, rim_late), att_main, first)
     mixed = apply_mix(place, part, qt, att, early, late, heads)
     mixed_tokens = lax.all_to_all(mixed, "head", split_axis=0, concat_axis=0)
     return final(mixed_tokens, gate_tokens, norm_gain)

time: 220 us -> 208 us (0.945)
  waiting for transfers between devices: 68.2 us -> 55.8 us
  starting transfers between devices: 46.1 us -> 51.5 us
  Pallas kernels: 94.6 us -> 91.9 us
    ppermute x4 -> x2, waiting for transfers between devices: 16.4 us -> 1.36 us  [send(): return lax.ppermute(array, 'ctx', pairs)]
    ppermute x13, starting transfers between devices: 22.4 us -> 32.1 us  [ring_send(): return lax.ppermute(array, ('ctx', 'head'), pairs)]
    ppermute x4 -> x2, starting transfers between devices: 9.58 us -> 4.75 us  [send(): return lax.ppermute(array, 'ctx', pairs)]
    pallas_call x2, Pallas kernels: 35.2 us -> 32.5 us  [grads(): pl.pallas_call(functools.partial(grads_kernel, static), grid_spec=pltpu.P...]
    ppermute x13, waiting for transfers between devices: 24.7 us -> 27.3 us  [ring_send(): return lax.ppermute(array, ('ctx', 'head'), pairs)]
    unnamed x24 -> x18, local copies, waits for them, and re-layouts: 4.85 us -> 3.23 us
  transfers between devices with their start and end apart: 19 -> 17, of which waited for: 7 -> 8; matrix products, arithmetic and copies ran while one was open for 1% -> 2% of each run, Pallas kernels for 33% -> 34%
where the time goes in v5:
time: 208 us; the launch traced here: 207 us
  Pallas kernels  91.9 us (44%)
  waiting for transfers between devices  55.8 us (27%)
  starting transfers between devices  51.5 us (25%)
  other arithmetic  4.01 us (2%)
  local copies, waits for them, and re-layouts  3.31 us (2%)
    pallas_call x2, Pallas kernels, grads(): pl.pallas_call(functools.partial(grads_kernel, static), grid_spec=pltpu.P...  32.5 us
    ppermute x13, starting transfers between devices, ring_send(): return lax.ppermute(array, ('ctx', 'head'), pairs)  32.1 us
    ppermute x13, waiting for transfers between devices, ring_send(): return lax.ppermute(array, ('ctx', 'head'), pairs)  27.3 us
    all_to_all x1, waiting for transfers between devices, shards(): mixed_tokens = lax.all_to_all(mixed, 'head', split_axis=0, concat_axis=0)  27.1 us
    pallas_call x1, Pallas kernels, attend_main(): pl.pallas_call(functools.partial(attend_kernel, blocks, None), grid_spec=...  15.4 us
    pallas_call x2, Pallas kernels, update(): pl.pallas_call(update_kernel, in_specs=[smem, smem] + [vmem] * (4 + len(o...  14.8 us
    pallas_call x1, Pallas kernels, apply_mix(): pl.pallas_call(functools.partial(apply_kernel, dests), grid_spec=pltpu.Pr...  10.7 us
    pallas_call x1, Pallas kernels, attend_rim(): pl.pallas_call(functools.partial(attend_kernel, blocks, 0), grid_spec=plt...  9.25 us
  transfers between devices with their start and end apart: 17, of which 8 were waited for; matrix products, arithmetic and copies ran while one was open for 2% of the time, Pallas kernels for 34%

profile of v5, /device:TPU:32, one launch (start us, length us, event | category | flops | bytes accessed | tf_op | source)
XLA Modules:
  0.0 207.4 jit_solution(10002198289871068588)
XLA Ops:
  0.0 16.3 %shard_map.100 = (bf16[320,640]{1,0:T(8,128)(2,1)}, bf16[320,640]{1,0:T(8,128)(2,1)}, bf16[320,640]{1,0:T(8,128)(2,1)}, bf16[320,640]{1,0:T(8,128)(2,1)}, bf16[640,1024]{1,0:T(8,128)(2,1)}) custom-call(s32[1]{0:T(128)} %bitcast.place_ref, bf16[320,3072]{1,0:T(8,128)(2,1)} %bitcast.14, bf16[320,3072]{1,0:T(8,128)(2,1)} %bitcast.18, f32[1,3072]{1,0:T(1,128)} %r_ref.3, ...), custom_call_target="tpu_custom_call" | custom-call | flops 7549747200 | bytes 3932160 | tf_op jit(solution)/shard_map/pallas_call | solution.py:118
  16.3 3.5 %collective-permute-start.3 = (bf16[640,1024]{1,0:T(8,128)(2,1)}, bf16[640,1024]{1,0:T(8,128)(2,1)S(1)}, u32[]{:S(2)}, u32[]{:S(2)}) collective-permute-start(bf16[640,1024]{1,0:T(8,128)(2,1)} %get-tuple-element.40), channel_id=1, source_target_pairs={{64,80},{80,96},{96,112},{65,81},{81,97},{97,113},{66,82},{82,98},... | collective-permute-start | bytes 3932168 | tf_op jit(solution)/shard_map/ppermute | solution.py:456
  19.8 0.7 collective-permute-start
  20.5 0.7 collective-permute-start.1
  21.2 0.9 collective-permute-start.2
  22.7 15.4 %shard_map.101.rest_1_ = f32[320,3072]{1,0:T(8,128)} custom-call(s32[1]{0:T(128)} %bitcast.3.first_ref, bf16[320,3072]{1,0:T(8,128)(2,1)} %bitcast.22, bf16[320,3072]{1,0:T(8,128)(2,1)} %bitcast.15, bf16[320,3072]{1,0:T(8,128)(2,1)} %bitcast.19), custom_call_target="tpu_custom_call" | custom-call | flops 3355443200 | bytes 9830400 | tf_op jit(solution)/shard_map/pallas_call | solution.py:264
  38.1 0.0 collective-permute-done.r1
  38.1 0.0 copy-start.6
  38.1 0.0 collective-permute-done.1.r2
  38.1 0.0 copy-start.7
  38.1 0.0 collective-permute-done.2.r3
  38.1 0.0 copy-start.8
  38.1 0.7 copy-done.6
  38.9 0.1 copy-done.7
  39.0 0.2 copy-done.8
  39.2 7.5 %shard_map.102 = bf16[320,640]{1,0:T(8,128)(2,1)} custom-call(s32[1]{0:T(128)} %bitcast.place_ref, f32[1]{0:T(128)S(6)} %copy.13.step_ref, bf16[320,640]{1,0:T(8,128)(2,1)} %get-tuple-element.32.own, bf16[320,640]{1,0:T(8,128)(2,1)} %copy-done.6, bf16[320,640]{1,0:T(8,128)(2,1)} %copy-done.7, bf16[320,640]{1,0:T(8,128)(2,1)} %copy-done.8, ...), custom_call_target="tpu_custom_call" | custom-call | flops 1638400000 | bytes 3276800 | tf_op jit(solution)/shard_map/pallas_call | solution.py:175
  46.7 1.4 collective-permute-done.3
  48.1 1.3 collective-permute-start.4
  49.4 0.0 copy-start.1
  49.4 4.3 %shard_map.103 = bf16[16,96,640]{2,1,0:T(8,128)(2,1)} custom-call(bf16[320,3072]{1,0:T(8,128)(2,1)} %bitcast.13), custom_call_target="tpu_custom_call" | custom-call | bytes 7864320 | tf_op jit(solution)/shard_map/pallas_call | solution.py:381
  53.7 8.7 %collective-permute-done.4 = bf16[320,640]{1,0:T(8,128)(2,1)S(1)} collective-permute-done((bf16[320,640]{1,0:T(8,128)(2,1)}, bf16[320,640]{1,0:T(8,128)(2,1)S(1)}, u32[]{:S(2)}, u32[]{:S(2)}) %collective-permute-start.4) | collective-permute-done | bytes 409632 | tf_op jit(solution)/shard_map/ppermute | solution.py:452
  62.4 0.0 copy-done.1
  62.4 0.8 broadcast_select_fusion.1.rest_0_
  63.2 2.1 %collective-permute-start.5 = (bf16[320,640]{1,0:T(8,128)(2,1)}, bf16[320,640]{1,0:T(8,128)(2,1)}, u32[]{:S(2)}, u32[]{:S(2)}) collective-permute-start(bf16[320,640]{1,0:T(8,128)(2,1)} %broadcast_select_fusion.1.rest_0_), channel_id=1, source_target_pairs={{0,16},{33,49},{2,18},{35,51},{4,20},{37,53},{6,22},{39,55},{8,24}... | collective-permute-start | bytes 1228808 | tf_op jit(solution)/shard_map/ppermute | solution.py:452
  65.3 3.8 %collective-permute-start.7 = (bf16[320,640]{1,0:T(8,128)(2,1)}, bf16[320,640]{1,0:T(8,128)(2,1)}, u32[]{:S(2)}, u32[]{:S(2)}) collective-permute-start(bf16[320,640]{1,0:T(8,128)(2,1)} %broadcast_select_fusion.1.rest_0_), channel_id=1, source_target_pairs={{0,32},{33,1},{2,34},{35,3},{4,36},{37,5},{6,38},{39,7},{8,40},{41... | collective-permute-start | bytes 1228808 | tf_op jit(solution)/shard_map/ppermute | solution.py:452
  69.1 1.9 collective-permute-start.8
  71.0 3.6 %collective-permute-done.5.rest_1_ = bf16[320,640]{1,0:T(8,128)(2,1)} collective-permute-done((bf16[320,640]{1,0:T(8,128)(2,1)}, bf16[320,640]{1,0:T(8,128)(2,1)}, u32[]{:S(2)}, u32[]{:S(2)}) %collective-permute-start.5) | collective-permute-done | bytes 409632 | tf_op jit(solution)/shard_map/ppermute | solution.py:452
  74.6 1.3 collective-permute-start.6
  75.9 7.6 %all-to-all-start.1 = ((bf16[16,96,640]{2,1,0:T(8,128)(2,1)}), bf16[16,96,640]{2,1,0:T(8,128)(2,1)S(1)}, u32[]{:S(2)}, u32[]{:S(2)}) async-start(bf16[16,96,640]{2,1,0:T(8,128)(2,1)} %shard_map.103), calls=%async_computation.1 | async-start | bytes 3932160 | tf_op jit(solution)/shard_map/all_to_all | solution.py:492
  83.5 0.0 collective-permute-done.7.rest_2_
  83.5 0.0 collective-permute-done.8.rest_3_
  83.5 16.2 %shard_map.104 = (bf16[320,640]{1,0:T(8,128)(2,1)}, bf16[320,640]{1,0:T(8,128)(2,1)}, bf16[320,640]{1,0:T(8,128)(2,1)}, bf16[320,640]{1,0:T(8,128)(2,1)}) custom-call(s32[1]{0:T(128)} %bitcast.place_ref, bf16[320,3072]{1,0:T(8,128)(2,1)} %bitcast.16, bf16[320,3072]{1,0:T(8,128)(2,1)} %bitcast.20, f32[1,3072]{1,0:T(1,128)} %r_ref.3, ...), custom_call_target="tpu_custom_call" | custom-call | flops 7549747200 | bytes 3932160 | tf_op jit(solution)/shard_map/pallas_call | solution.py:118
  99.7 5.7 %collective-permute-start.10 = (bf16[320,640]{1,0:T(8,128)(2,1)}, bf16[320,640]{1,0:T(8,128)(2,1)}, u32[]{:S(2)}, u32[]{:S(2)}) collective-permute-start(bf16[320,640]{1,0:T(8,128)(2,1)} %get-tuple-element.45), channel_id=1, source_target_pairs={{96,64},{65,97},{98,66},{67,99},{100,68},{69,101},{102,70},{71,103... | collective-permute-start | bytes 1228808 | tf_op jit(solution)/shard_map/ppermute | solution.py:452
  105.4 1.3 collective-permute-start.11
  106.7 4.6 %collective-permute-start.9 = (bf16[320,640]{1,0:T(8,128)(2,1)}, bf16[320,640]{1,0:T(8,128)(2,1)}, u32[]{:S(2)}, u32[]{:S(2)}) collective-permute-start(bf16[320,640]{1,0:T(8,128)(2,1)} %get-tuple-element.44), channel_id=1, source_target_pairs={{112,64},{81,97},{114,66},{83,99},{116,68},{85,101},{118,70},{87,1... | collective-permute-start | bytes 1228808 | tf_op jit(solution)/shard_map/ppermute | solution.py:452
  111.2 4.7 %collective-permute-done.10.r2 = bf16[320,640]{1,0:T(8,128)(2,1)} collective-permute-done((bf16[320,640]{1,0:T(8,128)(2,1)}, bf16[320,640]{1,0:T(8,128)(2,1)}, u32[]{:S(2)}, u32[]{:S(2)}) %collective-permute-start.10) | collective-permute-done | bytes 409632 | tf_op jit(solution)/shard_map/ppermute | solution.py:452
  115.9 4.0 %collective-permute-done.11.r3 = bf16[320,640]{1,0:T(8,128)(2,1)} collective-permute-done((bf16[320,640]{1,0:T(8,128)(2,1)}, bf16[320,640]{1,0:T(8,128)(2,1)}, u32[]{:S(2)}, u32[]{:S(2)}) %collective-permute-start.11) | collective-permute-done | bytes 409632 | tf_op jit(solution)/shard_map/ppermute | solution.py:452
  120.0 4.1 %collective-permute-done.9.r1 = bf16[320,640]{1,0:T(8,128)(2,1)} collective-permute-done((bf16[320,640]{1,0:T(8,128)(2,1)}, bf16[320,640]{1,0:T(8,128)(2,1)}, u32[]{:S(2)}, u32[]{:S(2)}) %collective-permute-start.9) | collective-permute-done | bytes 409632 | tf_op jit(solution)/shard_map/ppermute | solution.py:452
  124.1 7.3 %shard_map.105.rest_4_ = bf16[320,640]{1,0:T(8,128)(2,1)} custom-call(s32[1]{0:T(128)} %bitcast.place_ref, f32[1]{0:T(128)S(6)} %copy.13.step_ref, bf16[320,640]{1,0:T(8,128)(2,1)} %get-tuple-element.43.own, bf16[320,640]{1,0:T(8,128)(2,1)} %collective-permute-done.9.r1, bf16[320,640]{1,0:T(8,128)(2,1)} %collective-permute-done.10.r2, ...), custom_call_target="tpu_custom_call" | custom-call | flops 1638400000 | bytes 3276800 | tf_op jit(solution)/shard_map/pallas_call | solution.py:175
  131.4 2.6 %collective-permute-start.12 = (bf16[320,640]{1,0:T(8,128)(2,1)}, bf16[320,640]{1,0:T(8,128)(2,1)S(1)}, u32[]{:S(2)}, u32[]{:S(2)}) collective-permute-start(bf16[320,640]{1,0:T(8,128)(2,1)} %shard_map.105.rest_4_), channel_id=1, source_target_pairs={{64,80},{97,113},{66,82},{99,115},{68,84},{101,117},{70,86},{103,1... | collective-permute-start | bytes 1228808 | tf_op jit(solution)/shard_map/ppermute | solution.py:452
  134.0 4.4 %collective-permute-start.13 = (bf16[320,640]{1,0:T(8,128)(2,1)}, bf16[320,640]{1,0:T(8,128)(2,1)S(1)}, u32[]{:S(2)}, u32[]{:S(2)}) collective-permute-start(bf16[320,640]{1,0:T(8,128)(2,1)} %shard_map.105.rest_4_), channel_id=1, source_target_pairs={{64,96},{97,65},{66,98},{99,67},{68,100},{101,69},{70,102},{103,71... | collective-permute-start | bytes 1228808 | tf_op jit(solution)/shard_map/ppermute | solution.py:452
  138.5 2.2 %collective-permute-start.14 = (bf16[320,640]{1,0:T(8,128)(2,1)}, bf16[320,640]{1,0:T(8,128)(2,1)S(1)}, u32[]{:S(2)}, u32[]{:S(2)}) collective-permute-start(bf16[320,640]{1,0:T(8,128)(2,1)} %shard_map.105.rest_4_), channel_id=1, source_target_pairs={{64,112},{97,81},{66,114},{99,83},{68,116},{101,85},{70,118},{103,... | collective-permute-start | bytes 1228808 | tf_op jit(solution)/shard_map/ppermute | solution.py:452
  140.7 0.0 collective-permute-done.6
  140.7 2.5 %broadcast_select_fusion.rest_0_ = bf16[640,1024]{1,0:T(8,128)(2,1)} fusion(bf16[640,1024]{1,0:T(8,128)(2,1)} %collective-permute-done.6, bf16[640,1024]{1,0:T(8,128)(2,1)S(1)} %collective-permute-done.3, pred[]{:T(512)S(6)} %le.3), kind=kLoop, calls=%fused_computation | loop fusion | flops 655360 | bytes 3932161 | tf_op jit(solution)/shard_map/jit(_where)/select_n | solution.py:502
  143.2 9.2 %shard_map.106.att_ref = f32[320,3072]{1,0:T(8,128)} custom-call(s32[1]{0:T(128)} %bitcast.3.first_ref, bf16[320,3072]{1,0:T(8,128)(2,1)} %bitcast.23, bf16[320,3072]{1,0:T(8,128)(2,1)} %bitcast.17, bf16[320,3072]{1,0:T(8,128)(2,1)} %bitcast.21, bf16[640,1024]{1,0:T(8,128)(2,1)} %broadcast_select_fusion.rest_0_, ...), custom_call_target="tpu_custom_call", output_to_operand_aliasing={{}: (5, {})} | custom-call | flops 1677721600 | bytes 5242880 | tf_op jit(solution)/shard_map/pallas_call | solution.py:288
  152.4 0.0 collective-permute-done.12.rest_5_
  152.4 0.0 copy-start.3
  152.4 2.1 %collective-permute-done.13.rest_6_ = bf16[320,640]{1,0:T(8,128)(2,1)S(1)} collective-permute-done((bf16[320,640]{1,0:T(8,128)(2,1)}, bf16[320,640]{1,0:T(8,128)(2,1)S(1)}, u32[]{:S(2)}, u32[]{:S(2)}) %collective-permute-start.13) | collective-permute-done | bytes 409632 | tf_op jit(solution)/shard_map/ppermute | solution.py:452
  154.5 0.0 copy-start.4
  154.5 0.0 collective-permute-done.14.rest_7_
  154.5 0.0 copy-start.5
  154.5 0.0 copy-done.3
  154.6 0.7 copy-done.4
  155.3 0.1 copy-done.5
  155.4 10.7 %shard_map.107 = bf16[16,96,640]{2,1,0:T(8,128)(2,1)} custom-call(s32[1]{0:T(128)} %bitcast.place_ref, s32[1]{0:T(128)} %bitcast.1.part_ref, bf16[320,3072]{1,0:T(8,128)(2,1)} %bitcast.24, f32[320,3072]{1,0:T(8,128)} %shard_map.106.att_ref, bf16[320,640]{1,0:T(8,128)(2,1)} %broadcast_select_fusion.1.rest_0_, ...), custom_call_target="tpu_custom_call" | custom-call | flops 3774873600 | bytes 7864320 | tf_op jit(solution)/shard_map/pallas_call | solution.py:351
  166.2 0.0 all-to-all-done.1.g_ref
  166.2 0.0 copy-start
  166.2 1.3 copy-done
  167.4 7.1 %all-to-all-start = ((bf16[16,96,640]{2,1,0:T(8,128)(2,1)}), bf16[16,96,640]{2,1,0:T(8,128)(2,1)}, u32[]{:S(2)}, u32[]{:S(2)}) async-start(bf16[16,96,640]{2,1,0:T(8,128)(2,1)} %shard_map.107), calls=%async_computation | async-start | bytes 3932160 | tf_op jit(solution)/shard_map/all_to_all | solution.py:504
  174.5 0.0 copy-done.2
  174.5 0.1 reshape.17
  174.6 0.7 pad_maximum_fusion.gain_ref
  175.3 27.1 %all-to-all-done.m_ref = bf16[16,96,640]{2,1,0:T(8,128)(2,1)} async-done(((bf16[16,96,640]{2,1,0:T(8,128)(2,1)}), bf16[16,96,640]{2,1,0:T(8,128)(2,1)}, u32[]{:S(2)}, u32[]{:S(2)}) %all-to-all-start) | async-done | bytes 1966112 | tf_op jit(solution)/shard_map/all_to_all | solution.py:504
  202.4 5.0 %shard_map.108 = bf16[2,96,5120]{2,1,0:T(8,128)(2,1)} custom-call(bf16[16,96,640]{2,1,0:T(8,128)(2,1)} %all-to-all-done.m_ref, bf16[16,96,640]{2,1,0:T(8,128)(2,1)} %copy-done, f32[16,640]{1,0:T(8,128)} %pad_maximum_fusion.gain_ref), custom_call_target="tpu_custom_call" | custom-call | flops 9830400 | bytes 5898240 | tf_op jit(solution)/shard_map/pallas_call | solution.py:423
  (1 shorter events, 0.0 us)
Async XLA Ops:
  16.3 31.7 %collective-permute-start.3 = (bf16[640,1024]{1,0:T(8,128)(2,1)}, bf16[640,1024]{1,0:T(8,128)(2,1)S(1)}, u32[]{:S(2)}, u32[]{:S(2)}) collective-permute-start(bf16[640,1024]{1,0:T(8,128)(2,1)} %get-tuple-element.40), channel_id=1, source_target_pairs={{64,80},{80,96},{96,112},{65,81},{81,97},{97,113},{66,82},{82,98},... | collective-permute-start | bytes 3932168 | tf_op jit(solution)/shard_map/ppermute | solution.py:456
  19.8 18.3 %collective-permute-start = (bf16[320,640]{1,0:T(8,128)(2,1)}, bf16[320,640]{1,0:T(8,128)(2,1)S(1)}, u32[]{:S(2)}, u32[]{:S(2)}) collective-permute-start(bf16[320,640]{1,0:T(8,128)(2,1)} %get-tuple-element.29), channel_id=1, source_target_pairs={{48,0},{17,33},{50,2},{19,35},{52,4},{21,37},{54,6},{23,39},{56,8}... | collective-permute-start | bytes 1228808 | tf_op jit(solution)/shard_map/ppermute | solution.py:452
  20.5 17.6 %collective-permute-start.1 = (bf16[320,640]{1,0:T(8,128)(2,1)}, bf16[320,640]{1,0:T(8,128)(2,1)S(1)}, u32[]{:S(2)}, u32[]{:S(2)}) collective-permute-start(bf16[320,640]{1,0:T(8,128)(2,1)} %get-tuple-element.30), channel_id=1, source_target_pairs={{32,0},{1,33},{34,2},{3,35},{36,4},{5,37},{38,6},{7,39},{40,8},{9,... | collective-permute-start | bytes 1228808 | tf_op jit(solution)/shard_map/ppermute | solution.py:452
  21.2 16.9 %collective-permute-start.2 = (bf16[320,640]{1,0:T(8,128)(2,1)}, bf16[320,640]{1,0:T(8,128)(2,1)S(1)}, u32[]{:S(2)}, u32[]{:S(2)}) collective-permute-start(bf16[320,640]{1,0:T(8,128)(2,1)} %get-tuple-element.31), channel_id=1, source_target_pairs={{16,0},{49,33},{18,2},{51,35},{20,4},{53,37},{22,6},{55,39},{24,8}... | collective-permute-start | bytes 1228808 | tf_op jit(solution)/shard_map/ppermute | solution.py:452
  38.1 0.8 copy-start.6
  38.1 0.9 copy-start.7
  38.1 1.1 copy-start.8
  48.1 14.3 %collective-permute-start.4 = (bf16[320,640]{1,0:T(8,128)(2,1)}, bf16[320,640]{1,0:T(8,128)(2,1)S(1)}, u32[]{:S(2)}, u32[]{:S(2)}) collective-permute-start(bf16[320,640]{1,0:T(8,128)(2,1)} %shard_map.102), channel_id=1, source_target_pairs={{0,64},{33,97},{2,66},{35,99},{4,68},{37,101},{6,70},{39,103},{8,7... | collective-permute-start | bytes 1228808 | tf_op jit(solution)/shard_map/ppermute | solution.py:452
  49.4 13.0 %copy-start.1 = (bf16[320,640]{1,0:T(8,128)(2,1)S(1)}, bf16[320,640]{1,0:T(8,128)(2,1)}, u32[]{:S(2)}) copy-start(bf16[320,640]{1,0:T(8,128)(2,1)} %shard_map.102) | copy-start | bytes 1228804
  63.2 11.4 %collective-permute-start.5 = (bf16[320,640]{1,0:T(8,128)(2,1)}, bf16[320,640]{1,0:T(8,128)(2,1)}, u32[]{:S(2)}, u32[]{:S(2)}) collective-permute-start(bf16[320,640]{1,0:T(8,128)(2,1)} %broadcast_select_fusion.1.rest_0_), channel_id=1, source_target_pairs={{0,16},{33,49},{2,18},{35,51},{4,20},{37,53},{6,22},{39,55},{8,24}... | collective-permute-start | bytes 1228808 | tf_op jit(solution)/shard_map/ppermute | solution.py:452
  65.3 18.2 %collective-permute-start.7 = (bf16[320,640]{1,0:T(8,128)(2,1)}, bf16[320,640]{1,0:T(8,128)(2,1)}, u32[]{:S(2)}, u32[]{:S(2)}) collective-permute-start(bf16[320,640]{1,0:T(8,128)(2,1)} %broadcast_select_fusion.1.rest_0_), channel_id=1, source_target_pairs={{0,32},{33,1},{2,34},{35,3},{4,36},{37,5},{6,38},{39,7},{8,40},{41... | collective-permute-start | bytes 1228808 | tf_op jit(solution)/shard_map/ppermute | solution.py:452
  69.1 14.4 %collective-permute-start.8 = (bf16[320,640]{1,0:T(8,128)(2,1)}, bf16[320,640]{1,0:T(8,128)(2,1)}, u32[]{:S(2)}, u32[]{:S(2)}) collective-permute-start(bf16[320,640]{1,0:T(8,128)(2,1)} %broadcast_select_fusion.1.rest_0_), channel_id=1, source_target_pairs={{0,48},{33,17},{2,50},{35,19},{4,52},{37,21},{6,54},{39,23},{8,56}... | collective-permute-start | bytes 1228808 | tf_op jit(solution)/shard_map/ppermute | solution.py:452
  74.6 66.0 %collective-permute-start.6 = (bf16[640,1024]{1,0:T(8,128)(2,1)}, bf16[640,1024]{1,0:T(8,128)(2,1)}, u32[]{:S(2)}, u32[]{:S(2)}) collective-permute-start(bf16[640,1024]{1,0:T(8,128)(2,1)} %get-tuple-element.40), channel_id=1, source_target_pairs={{0,16},{16,32},{32,48},{48,64},{1,17},{17,33},{33,49},{49,65},{2,1... | collective-permute-start | bytes 3932168 | tf_op jit(solution)/shard_map/ppermute | solution.py:456
  75.9 90.3 %all-to-all-start.1 = ((bf16[16,96,640]{2,1,0:T(8,128)(2,1)}), bf16[16,96,640]{2,1,0:T(8,128)(2,1)S(1)}, u32[]{:S(2)}, u32[]{:S(2)}) async-start(bf16[16,96,640]{2,1,0:T(8,128)(2,1)} %shard_map.103), calls=%async_computation.1 | async-start | bytes 3932160 | tf_op jit(solution)/shard_map/all_to_all | solution.py:492
  99.7 16.3 %collective-permute-start.10 = (bf16[320,640]{1,0:T(8,128)(2,1)}, bf16[320,640]{1,0:T(8,128)(2,1)}, u32[]{:S(2)}, u32[]{:S(2)}) collective-permute-start(bf16[320,640]{1,0:T(8,128)(2,1)} %get-tuple-element.45), channel_id=1, source_target_pairs={{96,64},{65,97},{98,66},{67,99},{100,68},{69,101},{102,70},{71,103... | collective-permute-start | bytes 1228808 | tf_op jit(solution)/shard_map/ppermute | solution.py:452
  105.4 14.6 %collective-permute-start.11 = (bf16[320,640]{1,0:T(8,128)(2,1)}, bf16[320,640]{1,0:T(8,128)(2,1)}, u32[]{:S(2)}, u32[]{:S(2)}) collective-permute-start(bf16[320,640]{1,0:T(8,128)(2,1)} %get-tuple-element.46), channel_id=1, source_target_pairs={{80,64},{113,97},{82,66},{115,99},{84,68},{117,101},{86,70},{119,1... | collective-permute-start | bytes 1228808 | tf_op jit(solution)/shard_map/ppermute | solution.py:452
  106.7 17.5 %collective-permute-start.9 = (bf16[320,640]{1,0:T(8,128)(2,1)}, bf16[320,640]{1,0:T(8,128)(2,1)}, u32[]{:S(2)}, u32[]{:S(2)}) collective-permute-start(bf16[320,640]{1,0:T(8,128)(2,1)} %get-tuple-element.44), channel_id=1, source_target_pairs={{112,64},{81,97},{114,66},{83,99},{116,68},{85,101},{118,70},{87,1... | collective-permute-start | bytes 1228808 | tf_op jit(solution)/shard_map/ppermute | solution.py:452
  131.4 21.0 %collective-permute-start.12 = (bf16[320,640]{1,0:T(8,128)(2,1)}, bf16[320,640]{1,0:T(8,128)(2,1)S(1)}, u32[]{:S(2)}, u32[]{:S(2)}) collective-permute-start(bf16[320,640]{1,0:T(8,128)(2,1)} %shard_map.105.rest_4_), channel_id=1, source_target_pairs={{64,80},{97,113},{66,82},{99,115},{68,84},{101,117},{70,86},{103,1... | collective-permute-start | bytes 1228808 | tf_op jit(solution)/shard_map/ppermute | solution.py:452
  134.0 20.5 %collective-permute-start.13 = (bf16[320,640]{1,0:T(8,128)(2,1)}, bf16[320,640]{1,0:T(8,128)(2,1)S(1)}, u32[]{:S(2)}, u32[]{:S(2)}) collective-permute-start(bf16[320,640]{1,0:T(8,128)(2,1)} %shard_map.105.rest_4_), channel_id=1, source_target_pairs={{64,96},{97,65},{66,98},{99,67},{68,100},{101,69},{70,102},{103,71... | collective-permute-start | bytes 1228808 | tf_op jit(solution)/shard_map/ppermute | solution.py:452
  138.5 16.1 %collective-permute-start.14 = (bf16[320,640]{1,0:T(8,128)(2,1)}, bf16[320,640]{1,0:T(8,128)(2,1)S(1)}, u32[]{:S(2)}, u32[]{:S(2)}) collective-permute-start(bf16[320,640]{1,0:T(8,128)(2,1)} %shard_map.105.rest_4_), channel_id=1, source_target_pairs={{64,112},{97,81},{66,114},{99,83},{68,116},{101,85},{70,118},{103,... | collective-permute-start | bytes 1228808 | tf_op jit(solution)/shard_map/ppermute | solution.py:452
  152.4 2.1 %copy-start.3 = (bf16[320,640]{1,0:T(8,128)(2,1)}, bf16[320,640]{1,0:T(8,128)(2,1)S(1)}, u32[]{:S(2)}) copy-start(bf16[320,640]{1,0:T(8,128)(2,1)S(1)} %collective-permute-done.12.rest_5_) | copy-start | bytes 1228804
  154.5 0.8 copy-start.4
  154.5 0.9 copy-start.5
  166.2 8.4 %copy-start.2 = (f32[5120]{0:T(1024)S(1)}, f32[5120]{0:T(1024)}, u32[]{:S(2)}) copy-start(f32[5120]{0:T(1024)} %param.19) | copy-start | bytes 61444
  166.2 1.3 copy-start
  167.4 35.0 %all-to-all-start = ((bf16[16,96,640]{2,1,0:T(8,128)(2,1)}), bf16[16,96,640]{2,1,0:T(8,128)(2,1)}, u32[]{:S(2)}, u32[]{:S(2)}) async-start(bf16[16,96,640]{2,1,0:T(8,128)(2,1)} %shard_map.107), calls=%async_computation | async-start | bytes 3932160 | tf_op jit(solution)/shard_map/all_to_all | solution.py:504

commit v6 on v5

--- a/solution.py
+++ b/solution.py
@@ -481,12 +481,11 @@
     out, tail = out[:3], out[3]
     pieces = [own] + [ring_send(o, p) for o, p in zip(out, reduce_moves(0))]
     rim_late = send(tail, [(i, i + 1) for i in range(4, 7)])
-    att_main = attend_main(qt, kt, vt, first)
-    pieces, att_main = hold((pieces, att_main))
     fresh = update(place, step_sizes, pieces, start)
-    fresh, gt, rim_late = hold((fresh, gt, rim_late))
+    fresh, gt, rim_late, q_main = hold((fresh, gt, rim_late, qt))
     crossed = ring_send(fresh, [(0, m, 1, m) for m in range(3)])
     gates = pack_gate(gt, heads)
+    att_main = attend_main(q_main, kt, vt, first)
     held = jnp.where(part[0] == 0, fresh, crossed)
     held, gates = hold((held, gates))
     gate_tokens = lax.all_to_all(gates, "head", split_axis=0, concat_axis=0)

time: 208 us -> 216 us (1.038)
  starting transfers between devices: 51.5 us -> 57.8 us
    ppermute x2, waiting for transfers between devices: 1.36 us -> 17 us  [send(): return lax.ppermute(array, 'ctx', pairs)]
    ppermute x13, waiting for transfers between devices: 27.3 us -> 13 us  [ring_send(): return lax.ppermute(array, ('ctx', 'head'), pairs)]
    ppermute x13, starting transfers between devices: 32.1 us -> 39.1 us  [ring_send(): return lax.ppermute(array, ('ctx', 'head'), pairs)]
  transfers between devices with their start and end apart: 17 -> 17, of which waited for: 8 -> 6; matrix products, arithmetic and copies ran while one was open for 2% -> 2% of each run, Pallas kernels for 34% -> 33%
where the time goes in v6:
time: 216 us; the launch traced here: 215 us
  Pallas kernels  91.9 us (43%)
  starting transfers between devices  57.8 us (27%)
  waiting for transfers between devices  57.1 us (26%)
  other arithmetic  4.01 us (2%)
  local copies, waits for them, and re-layouts  3.22 us (1%)
    ppermute x13, starting transfers between devices, ring_send(): return lax.ppermute(array, ('ctx', 'head'), pairs)  39.1 us
    pallas_call x2, Pallas kernels, grads(): pl.pallas_call(functools.partial(grads_kernel, static), grid_spec=pltpu.P...  32.5 us
    all_to_all x1, waiting for transfers between devices, shards(): mixed_tokens = lax.all_to_all(mixed, 'head', split_axis=0, concat_axis=0)  27.1 us
    ppermute x2, waiting for transfers between devices, send(): return lax.ppermute(array, 'ctx', pairs)  17 us
    pallas_call x1, Pallas kernels, attend_main(): pl.pallas_call(functools.partial(attend_kernel, blocks, None), grid_spec=...  15.4 us
    pallas_call x2, Pallas kernels, update(): pl.pallas_call(update_kernel, in_specs=[smem, smem] + [vmem] * (4 + len(o...  14.8 us
    ppermute x13, waiting for transfers between devices, ring_send(): return lax.ppermute(array, ('ctx', 'head'), pairs)  13 us
    pallas_call x1, Pallas kernels, apply_mix(): pl.pallas_call(functools.partial(apply_kernel, dests), grid_spec=pltpu.Pr...  10.7 us
  transfers between devices with their start and end apart: 17, of which 6 were waited for; matrix products, arithmetic and copies ran while one was open for 2% of the time, Pallas kernels for 33%

profile of v6, /device:TPU:32, one launch (start us, length us, event | category | flops | bytes accessed | tf_op | source)
XLA Modules:
  0.0 215.0 jit_solution(237872350408002388)
XLA Ops:
  0.0 16.3 %shard_map.100 = (bf16[320,640]{1,0:T(8,128)(2,1)}, bf16[320,640]{1,0:T(8,128)(2,1)}, bf16[320,640]{1,0:T(8,128)(2,1)}, bf16[320,640]{1,0:T(8,128)(2,1)}, bf16[640,1024]{1,0:T(8,128)(2,1)}) custom-call(s32[1]{0:T(128)} %bitcast.place_ref, bf16[320,3072]{1,0:T(8,128)(2,1)} %bitcast.14, bf16[320,3072]{1,0:T(8,128)(2,1)} %bitcast.18, f32[1,3072]{1,0:T(1,128)} %r_ref.3, ...), custom_call_target="tpu_custom_call" | custom-call | flops 7549747200 | bytes 3932160 | tf_op jit(solution)/shard_map/pallas_call | solution.py:118
  16.3 3.5 %collective-permute-start.3 = (bf16[640,1024]{1,0:T(8,128)(2,1)}, bf16[640,1024]{1,0:T(8,128)(2,1)S(1)}, u32[]{:S(2)}, u32[]{:S(2)}) collective-permute-start(bf16[640,1024]{1,0:T(8,128)(2,1)} %get-tuple-element.32), channel_id=1, source_target_pairs={{64,80},{80,96},{96,112},{65,81},{81,97},{97,113},{66,82},{82,98},... | collective-permute-start | bytes 3932168 | tf_op jit(solution)/shard_map/ppermute | solution.py:456
  19.8 0.7 collective-permute-start
  20.5 0.7 collective-permute-start.1
  21.2 0.7 collective-permute-start.2
  22.5 0.0 collective-permute-done.r1
  22.6 0.0 copy-start.6
  22.6 0.0 collective-permute-done.1.r2
  22.6 0.0 copy-start.7
  22.6 0.0 collective-permute-done.2.r3
  22.6 0.0 copy-start.8
  22.6 0.7 copy-done.6
  23.3 0.1 copy-done.7
  23.5 0.1 copy-done.8
  23.6 7.5 %shard_map.101 = bf16[320,640]{1,0:T(8,128)(2,1)} custom-call(s32[1]{0:T(128)} %bitcast.place_ref, f32[1]{0:T(128)S(6)} %copy.13.step_ref, bf16[320,640]{1,0:T(8,128)(2,1)} %get-tuple-element.24.own, bf16[320,640]{1,0:T(8,128)(2,1)} %copy-done.6, bf16[320,640]{1,0:T(8,128)(2,1)} %copy-done.7, bf16[320,640]{1,0:T(8,128)(2,1)} %copy-done.8, ...), custom_call_target="tpu_custom_call" | custom-call | flops 1638400000 | bytes 3276800 | tf_op jit(solution)/shard_map/pallas_call | solution.py:175
  31.1 17.0 %collective-permute-done.3 = bf16[640,1024]{1,0:T(8,128)(2,1)S(1)} collective-permute-done((bf16[640,1024]{1,0:T(8,128)(2,1)}, bf16[640,1024]{1,0:T(8,128)(2,1)S(1)}, u32[]{:S(2)}, u32[]{:S(2)}) %collective-permute-start.3) | collective-permute-done | bytes 1310752 | tf_op jit(solution)/shard_map/ppermute | solution.py:456
  48.1 1.3 collective-permute-start.4
  49.4 0.0 copy-start.1
  49.4 4.3 %shard_map.102 = bf16[16,96,640]{2,1,0:T(8,128)(2,1)} custom-call(bf16[320,3072]{1,0:T(8,128)(2,1)} %bitcast.13), custom_call_target="tpu_custom_call" | custom-call | bytes 7864320 | tf_op jit(solution)/shard_map/pallas_call | solution.py:381
  53.7 6.8 %collective-permute-done.4 = bf16[320,640]{1,0:T(8,128)(2,1)S(1)} collective-permute-done((bf16[320,640]{1,0:T(8,128)(2,1)}, bf16[320,640]{1,0:T(8,128)(2,1)S(1)}, u32[]{:S(2)}, u32[]{:S(2)}) %collective-permute-start.4) | collective-permute-done | bytes 409632 | tf_op jit(solution)/shard_map/ppermute | solution.py:452
  60.5 0.0 copy-done.1
  60.5 0.8 broadcast_select_fusion.1.rest_0_
  61.3 2.7 %collective-permute-start.5 = (bf16[320,640]{1,0:T(8,128)(2,1)}, bf16[320,640]{1,0:T(8,128)(2,1)}, u32[]{:S(2)}, u32[]{:S(2)}) collective-permute-start(bf16[320,640]{1,0:T(8,128)(2,1)} %broadcast_select_fusion.1.rest_0_), channel_id=1, source_target_pairs={{0,16},{33,49},{2,18},{35,51},{4,20},{37,53},{6,22},{39,55},{8,24}... | collective-permute-start | bytes 1228808 | tf_op jit(solution)/shard_map/ppermute | solution.py:452
  64.0 5.1 %collective-permute-start.7 = (bf16[320,640]{1,0:T(8,128)(2,1)}, bf16[320,640]{1,0:T(8,128)(2,1)}, u32[]{:S(2)}, u32[]{:S(2)}) collective-permute-start(bf16[320,640]{1,0:T(8,128)(2,1)} %broadcast_select_fusion.1.rest_0_), channel_id=1, source_target_pairs={{0,32},{33,1},{2,34},{35,3},{4,36},{37,5},{6,38},{39,7},{8,40},{41... | collective-permute-start | bytes 1228808 | tf_op jit(solution)/shard_map/ppermute | solution.py:452
  69.1 1.9 collective-permute-start.8
  71.0 2.4 %collective-permute-done.5.rest_1_ = bf16[320,640]{1,0:T(8,128)(2,1)} collective-permute-done((bf16[320,640]{1,0:T(8,128)(2,1)}, bf16[320,640]{1,0:T(8,128)(2,1)}, u32[]{:S(2)}, u32[]{:S(2)}) %collective-permute-start.5) | collective-permute-done | bytes 409632 | tf_op jit(solution)/shard_map/ppermute | solution.py:452
  73.4 1.3 collective-permute-start.6
  74.7 7.0 %all-to-all-start.1 = ((bf16[16,96,640]{2,1,0:T(8,128)(2,1)}), bf16[16,96,640]{2,1,0:T(8,128)(2,1)S(1)}, u32[]{:S(2)}, u32[]{:S(2)}) async-start(bf16[16,96,640]{2,1,0:T(8,128)(2,1)} %shard_map.102), calls=%async_computation.1 | async-start | bytes 3932160 | tf_op jit(solution)/shard_map/all_to_all | solution.py:491
  81.7 1.5 collective-permute-done.7.rest_2_
  83.3 0.0 collective-permute-done.8.rest_3_
  83.3 16.2 %shard_map.103 = (bf16[320,640]{1,0:T(8,128)(2,1)}, bf16[320,640]{1,0:T(8,128)(2,1)}, bf16[320,640]{1,0:T(8,128)(2,1)}, bf16[320,640]{1,0:T(8,128)(2,1)}) custom-call(s32[1]{0:T(128)} %bitcast.place_ref, bf16[320,3072]{1,0:T(8,128)(2,1)} %bitcast.15, bf16[320,3072]{1,0:T(8,128)(2,1)} %bitcast.19, f32[1,3072]{1,0:T(1,128)} %r_ref.3, ...), custom_call_target="tpu_custom_call" | custom-call | flops 7549747200 | bytes 3932160 | tf_op jit(solution)/shard_map/pallas_call | solution.py:118
  99.4 11.5 %collective-permute-start.10 = (bf16[320,640]{1,0:T(8,128)(2,1)}, bf16[320,640]{1,0:T(8,128)(2,1)}, u32[]{:S(2)}, u32[]{:S(2)}) collective-permute-start(bf16[320,640]{1,0:T(8,128)(2,1)} %get-tuple-element.37), channel_id=1, source_target_pairs={{96,64},{65,97},{98,66},{67,99},{100,68},{69,101},{102,70},{71,103... | collective-permute-start | bytes 1228808 | tf_op jit(solution)/shard_map/ppermute | solution.py:452
  111.0 1.3 collective-permute-start.11
  112.3 4.6 %collective-permute-start.9 = (bf16[320,640]{1,0:T(8,128)(2,1)}, bf16[320,640]{1,0:T(8,128)(2,1)}, u32[]{:S(2)}, u32[]{:S(2)}) collective-permute-start(bf16[320,640]{1,0:T(8,128)(2,1)} %get-tuple-element.36), channel_id=1, source_target_pairs={{112,64},{81,97},{114,66},{83,99},{116,68},{85,101},{118,70},{87,1... | collective-permute-start | bytes 1228808 | tf_op jit(solution)/shard_map/ppermute | solution.py:452
  116.8 15.4 %shard_map.105.rest_1_ = f32[320,3072]{1,0:T(8,128)} custom-call(s32[1]{0:T(128)} %bitcast.3.first_ref, bf16[320,3072]{1,0:T(8,128)(2,1)} %bitcast.22, bf16[320,3072]{1,0:T(8,128)(2,1)} %bitcast.16, bf16[320,3072]{1,0:T(8,128)(2,1)} %bitcast.20), custom_call_target="tpu_custom_call" | custom-call | flops 3355443200 | bytes 9830400 | tf_op jit(solution)/shard_map/pallas_call | solution.py:264
  132.2 0.0 collective-permute-done.10.r2
  132.2 0.0 collective-permute-done.11.r3
  132.2 0.0 collective-permute-done.9.r1
  132.2 7.3 %shard_map.104.rest_4_ = bf16[320,640]{1,0:T(8,128)(2,1)} custom-call(s32[1]{0:T(128)} %bitcast.place_ref, f32[1]{0:T(128)S(6)} %copy.13.step_ref, bf16[320,640]{1,0:T(8,128)(2,1)} %get-tuple-element.35.own, bf16[320,640]{1,0:T(8,128)(2,1)} %collective-permute-done.9.r1, bf16[320,640]{1,0:T(8,128)(2,1)} %collective-permute-done.10.r2, ...), custom_call_target="tpu_custom_call" | custom-call | flops 1638400000 | bytes 3276800 | tf_op jit(solution)/shard_map/pallas_call | solution.py:175
  139.5 1.9 collective-permute-start.12
  141.4 4.6 %collective-permute-start.13 = (bf16[320,640]{1,0:T(8,128)(2,1)}, bf16[320,640]{1,0:T(8,128)(2,1)S(1)}, u32[]{:S(2)}, u32[]{:S(2)}) collective-permute-start(bf16[320,640]{1,0:T(8,128)(2,1)} %shard_map.104.rest_4_), channel_id=1, source_target_pairs={{64,96},{97,65},{66,98},{99,67},{68,100},{101,69},{70,102},{103,71... | collective-permute-start | bytes 1228808 | tf_op jit(solution)/shard_map/ppermute | solution.py:452
  146.1 2.1 collective-permute-start.14
  148.2 0.0 collective-permute-done.6
  148.2 2.5 %broadcast_select_fusion.rest_0_ = bf16[640,1024]{1,0:T(8,128)(2,1)} fusion(bf16[640,1024]{1,0:T(8,128)(2,1)} %collective-permute-done.6, bf16[640,1024]{1,0:T(8,128)(2,1)S(1)} %collective-permute-done.3, pred[]{:T(512)S(6)} %le.3), kind=kLoop, calls=%fused_computation | loop fusion | flops 655360 | bytes 3932161 | tf_op jit(solution)/shard_map/jit(_where)/select_n | solution.py:501
  150.8 9.2 %shard_map.106.att_ref = f32[320,3072]{1,0:T(8,128)} custom-call(s32[1]{0:T(128)} %bitcast.3.first_ref, bf16[320,3072]{1,0:T(8,128)(2,1)} %bitcast.23, bf16[320,3072]{1,0:T(8,128)(2,1)} %bitcast.17, bf16[320,3072]{1,0:T(8,128)(2,1)} %bitcast.21, bf16[640,1024]{1,0:T(8,128)(2,1)} %broadcast_select_fusion.rest_0_, ...), custom_call_target="tpu_custom_call", output_to_operand_aliasing={{}: (5, {})} | custom-call | flops 1677721600 | bytes 5242880 | tf_op jit(solution)/shard_map/pallas_call | solution.py:288
  160.0 0.0 collective-permute-done.12.rest_5_
  160.0 0.0 copy-start.3
  160.0 2.3 %collective-permute-done.13.rest_6_ = bf16[320,640]{1,0:T(8,128)(2,1)S(1)} collective-permute-done((bf16[320,640]{1,0:T(8,128)(2,1)}, bf16[320,640]{1,0:T(8,128)(2,1)S(1)}, u32[]{:S(2)}, u32[]{:S(2)}) %collective-permute-start.13) | collective-permute-done | bytes 409632 | tf_op jit(solution)/shard_map/ppermute | solution.py:452
  162.3 0.0 copy-start.4
  162.3 0.0 collective-permute-done.14.rest_7_
  162.3 0.0 copy-start.5
  162.3 0.0 copy-done.3
  162.3 0.7 copy-done.4
  163.0 0.1 copy-done.5
  163.2 10.7 %shard_map.107 = bf16[16,96,640]{2,1,0:T(8,128)(2,1)} custom-call(s32[1]{0:T(128)} %bitcast.place_ref, s32[1]{0:T(128)} %bitcast.1.part_ref, bf16[320,3072]{1,0:T(8,128)(2,1)} %bitcast.24, f32[320,3072]{1,0:T(8,128)} %shard_map.106.att_ref, bf16[320,640]{1,0:T(8,128)(2,1)} %broadcast_select_fusion.1.rest_0_, ...), custom_call_target="tpu_custom_call" | custom-call | flops 3774873600 | bytes 7864320 | tf_op jit(solution)/shard_map/pallas_call | solution.py:351
  173.9 0.0 all-to-all-done.1.g_ref
  173.9 0.0 copy-start
  173.9 1.3 copy-done
  175.2 7.0 %all-to-all-start = ((bf16[16,96,640]{2,1,0:T(8,128)(2,1)}), bf16[16,96,640]{2,1,0:T(8,128)(2,1)}, u32[]{:S(2)}, u32[]{:S(2)}) async-start(bf16[16,96,640]{2,1,0:T(8,128)(2,1)} %shard_map.107), calls=%async_computation | async-start | bytes 3932160 | tf_op jit(solution)/shard_map/all_to_all | solution.py:503
  182.1 0.0 copy-done.2
  182.2 0.1 reshape.17
  182.2 0.7 pad_maximum_fusion.gain_ref
  182.9 27.1 %all-to-all-done.m_ref = bf16[16,96,640]{2,1,0:T(8,128)(2,1)} async-done(((bf16[16,96,640]{2,1,0:T(8,128)(2,1)}), bf16[16,96,640]{2,1,0:T(8,128)(2,1)}, u32[]{:S(2)}, u32[]{:S(2)}) %all-to-all-start) | async-done | bytes 1966112 | tf_op jit(solution)/shard_map/all_to_all | solution.py:503
  210.0 5.0 %shard_map.108 = bf16[2,96,5120]{2,1,0:T(8,128)(2,1)} custom-call(bf16[16,96,640]{2,1,0:T(8,128)(2,1)} %all-to-all-done.m_ref, bf16[16,96,640]{2,1,0:T(8,128)(2,1)} %copy-done, f32[16,640]{1,0:T(8,128)} %pad_maximum_fusion.gain_ref), custom_call_target="tpu_custom_call" | custom-call | flops 9830400 | bytes 5898240 | tf_op jit(solution)/shard_map/pallas_call | solution.py:423
  (1 shorter events, 0.0 us)
Async XLA Ops:
  16.3 31.7 %collective-permute-start.3 = (bf16[640,1024]{1,0:T(8,128)(2,1)}, bf16[640,1024]{1,0:T(8,128)(2,1)S(1)}, u32[]{:S(2)}, u32[]{:S(2)}) collective-permute-start(bf16[640,1024]{1,0:T(8,128)(2,1)} %get-tuple-element.32), channel_id=1, source_target_pairs={{64,80},{80,96},{96,112},{65,81},{81,97},{97,113},{66,82},{82,98},... | collective-permute-start | bytes 3932168 | tf_op jit(solution)/shard_map/ppermute | solution.py:456
  19.8 2.7 %collective-permute-start = (bf16[320,640]{1,0:T(8,128)(2,1)}, bf16[320,640]{1,0:T(8,128)(2,1)S(1)}, u32[]{:S(2)}, u32[]{:S(2)}) collective-permute-start(bf16[320,640]{1,0:T(8,128)(2,1)} %get-tuple-element.25), channel_id=1, source_target_pairs={{48,0},{17,33},{50,2},{19,35},{52,4},{21,37},{54,6},{23,39},{56,8}... | collective-permute-start | bytes 1228808 | tf_op jit(solution)/shard_map/ppermute | solution.py:452
  20.5 2.1 collective-permute-start.1
  21.2 1.4 collective-permute-start.2
  22.6 0.8 copy-start.6
  22.6 0.9 copy-start.7
  22.6 1.0 copy-start.8
  48.1 12.4 %collective-permute-start.4 = (bf16[320,640]{1,0:T(8,128)(2,1)}, bf16[320,640]{1,0:T(8,128)(2,1)S(1)}, u32[]{:S(2)}, u32[]{:S(2)}) collective-permute-start(bf16[320,640]{1,0:T(8,128)(2,1)} %shard_map.101), channel_id=1, source_target_pairs={{0,64},{33,97},{2,66},{35,99},{4,68},{37,101},{6,70},{39,103},{8,7... | collective-permute-start | bytes 1228808 | tf_op jit(solution)/shard_map/ppermute | solution.py:452
  49.4 11.1 %copy-start.1 = (bf16[320,640]{1,0:T(8,128)(2,1)S(1)}, bf16[320,640]{1,0:T(8,128)(2,1)}, u32[]{:S(2)}) copy-start(bf16[320,640]{1,0:T(8,128)(2,1)} %shard_map.101) | copy-start | bytes 1228804
  61.3 12.1 %collective-permute-start.5 = (bf16[320,640]{1,0:T(8,128)(2,1)}, bf16[320,640]{1,0:T(8,128)(2,1)}, u32[]{:S(2)}, u32[]{:S(2)}) collective-permute-start(bf16[320,640]{1,0:T(8,128)(2,1)} %broadcast_select_fusion.1.rest_0_), channel_id=1, source_target_pairs={{0,16},{33,49},{2,18},{35,51},{4,20},{37,53},{6,22},{39,55},{8,24}... | collective-permute-start | bytes 1228808 | tf_op jit(solution)/shard_map/ppermute | solution.py:452
  64.0 19.3 %collective-permute-start.7 = (bf16[320,640]{1,0:T(8,128)(2,1)}, bf16[320,640]{1,0:T(8,128)(2,1)}, u32[]{:S(2)}, u32[]{:S(2)}) collective-permute-start(bf16[320,640]{1,0:T(8,128)(2,1)} %broadcast_select_fusion.1.rest_0_), channel_id=1, source_target_pairs={{0,32},{33,1},{2,34},{35,3},{4,36},{37,5},{6,38},{39,7},{8,40},{41... | collective-permute-start | bytes 1228808 | tf_op jit(solution)/shard_map/ppermute | solution.py:452
  69.1 14.2 %collective-permute-start.8 = (bf16[320,640]{1,0:T(8,128)(2,1)}, bf16[320,640]{1,0:T(8,128)(2,1)}, u32[]{:S(2)}, u32[]{:S(2)}) collective-permute-start(bf16[320,640]{1,0:T(8,128)(2,1)} %broadcast_select_fusion.1.rest_0_), channel_id=1, source_target_pairs={{0,48},{33,17},{2,50},{35,19},{4,52},{37,21},{6,54},{39,23},{8,56}... | collective-permute-start | bytes 1228808 | tf_op jit(solution)/shard_map/ppermute | solution.py:452
  73.4 74.8 %collective-permute-start.6 = (bf16[640,1024]{1,0:T(8,128)(2,1)}, bf16[640,1024]{1,0:T(8,128)(2,1)}, u32[]{:S(2)}, u32[]{:S(2)}) collective-permute-start(bf16[640,1024]{1,0:T(8,128)(2,1)} %get-tuple-element.32), channel_id=1, source_target_pairs={{0,16},{16,32},{32,48},{48,64},{1,17},{17,33},{33,49},{49,65},{2,1... | collective-permute-start | bytes 3932168 | tf_op jit(solution)/shard_map/ppermute | solution.py:456
  74.7 99.2 %all-to-all-start.1 = ((bf16[16,96,640]{2,1,0:T(8,128)(2,1)}), bf16[16,96,640]{2,1,0:T(8,128)(2,1)S(1)}, u32[]{:S(2)}, u32[]{:S(2)}) async-start(bf16[16,96,640]{2,1,0:T(8,128)(2,1)} %shard_map.102), calls=%async_computation.1 | async-start | bytes 3932160 | tf_op jit(solution)/shard_map/all_to_all | solution.py:491
  99.4 32.8 %collective-permute-start.10 = (bf16[320,640]{1,0:T(8,128)(2,1)}, bf16[320,640]{1,0:T(8,128)(2,1)}, u32[]{:S(2)}, u32[]{:S(2)}) collective-permute-start(bf16[320,640]{1,0:T(8,128)(2,1)} %get-tuple-element.37), channel_id=1, source_target_pairs={{96,64},{65,97},{98,66},{67,99},{100,68},{69,101},{102,70},{71,103... | collective-permute-start | bytes 1228808 | tf_op jit(solution)/shard_map/ppermute | solution.py:452
  111.0 21.2 %collective-permute-start.11 = (bf16[320,640]{1,0:T(8,128)(2,1)}, bf16[320,640]{1,0:T(8,128)(2,1)}, u32[]{:S(2)}, u32[]{:S(2)}) collective-permute-start(bf16[320,640]{1,0:T(8,128)(2,1)} %get-tuple-element.38), channel_id=1, source_target_pairs={{80,64},{113,97},{82,66},{115,99},{84,68},{117,101},{86,70},{119,1... | collective-permute-start | bytes 1228808 | tf_op jit(solution)/shard_map/ppermute | solution.py:452
  112.3 19.9 %collective-permute-start.9 = (bf16[320,640]{1,0:T(8,128)(2,1)}, bf16[320,640]{1,0:T(8,128)(2,1)}, u32[]{:S(2)}, u32[]{:S(2)}) collective-permute-start(bf16[320,640]{1,0:T(8,128)(2,1)} %get-tuple-element.36), channel_id=1, source_target_pairs={{112,64},{81,97},{114,66},{83,99},{116,68},{85,101},{118,70},{87,1... | collective-permute-start | bytes 1228808 | tf_op jit(solution)/shard_map/ppermute | solution.py:452
  139.5 20.5 %collective-permute-start.12 = (bf16[320,640]{1,0:T(8,128)(2,1)}, bf16[320,640]{1,0:T(8,128)(2,1)S(1)}, u32[]{:S(2)}, u32[]{:S(2)}) collective-permute-start(bf16[320,640]{1,0:T(8,128)(2,1)} %shard_map.104.rest_4_), channel_id=1, source_target_pairs={{64,80},{97,113},{66,82},{99,115},{68,84},{101,117},{70,86},{103,1... | collective-permute-start | bytes 1228808 | tf_op jit(solution)/shard_map/ppermute | solution.py:452
  141.4 20.8 %collective-permute-start.13 = (bf16[320,640]{1,0:T(8,128)(2,1)}, bf16[320,640]{1,0:T(8,128)(2,1)S(1)}, u32[]{:S(2)}, u32[]{:S(2)}) collective-permute-start(bf16[320,640]{1,0:T(8,128)(2,1)} %shard_map.104.rest_4_), channel_id=1, source_target_pairs={{64,96},{97,65},{66,98},{99,67},{68,100},{101,69},{70,102},{103,71... | collective-permute-start | bytes 1228808 | tf_op jit(solution)/shard_map/ppermute | solution.py:452
  146.1 16.2 %collective-permute-start.14 = (bf16[320,640]{1,0:T(8,128)(2,1)}, bf16[320,640]{1,0:T(8,128)(2,1)S(1)}, u32[]{:S(2)}, u32[]{:S(2)}) collective-permute-start(bf16[320,640]{1,0:T(8,128)(2,1)} %shard_map.104.rest_4_), channel_id=1, source_target_pairs={{64,112},{97,81},{66,114},{99,83},{68,116},{101,85},{70,118},{103,... | collective-permute-start | bytes 1228808 | tf_op jit(solution)/shard_map/ppermute | solution.py:452
  160.0 2.3 %copy-start.3 = (bf16[320,640]{1,0:T(8,128)(2,1)}, bf16[320,640]{1,0:T(8,128)(2,1)S(1)}, u32[]{:S(2)}) copy-start(bf16[320,640]{1,0:T(8,128)(2,1)S(1)} %collective-permute-done.12.rest_5_) | copy-start | bytes 1228804
  162.3 0.8 copy-start.4
  162.3 0.9 copy-start.5
  173.9 8.3 %copy-start.2 = (f32[5120]{0:T(1024)S(1)}, f32[5120]{0:T(1024)}, u32[]{:S(2)}) copy-start(f32[5120]{0:T(1024)} %param.19) | copy-start | bytes 61444
  173.9 1.3 copy-start
  175.2 34.9 %all-to-all-start = ((bf16[16,96,640]{2,1,0:T(8,128)(2,1)}), bf16[16,96,640]{2,1,0:T(8,128)(2,1)}, u32[]{:S(2)}, u32[]{:S(2)}) async-start(bf16[16,96,640]{2,1,0:T(8,128)(2,1)} %shard_map.107), calls=%async_computation | async-start | bytes 3932160 | tf_op jit(solution)/shard_map/all_to_all | solution.py:503
